TPU v7x, 32 devices: a whole 2x2x4 slice. The times are simulated.
32 devices in a mesh: group: 2 (over y), ctx: 4 (over z), head: 2 (over x), rep: 2 (over core).
Axes of the slice: x: 2, y: 2, z: 4, core: 2. Of those that a mesh axis runs over, the one named last changes fastest.
Arguments:
- queries: bfloat16 [6144, 5120], P(('group', 'ctx', 'rep'), 'head'), parts along dimension 0, may hold values from -6 to 6
- key_vectors: bfloat16 [6144, 5120], P(('group', 'ctx', 'rep'), 'head'), parts along dimension 0, may hold values from -6 to 6
- value_vectors: bfloat16 [6144, 5120], P(('group', 'ctx', 'rep'), 'head'), parts along dimension 0, may hold values from -6 to 6
- gate_input: bfloat16 [6144, 5120], P(('group', 'ctx', 'rep'), 'head'), parts along dimension 0, may hold values from -6 to 6
- norm_gain: float32 [5120], P('head'), may hold values from 0.25 to 1.75
- decay_rate: float32 [40], P('head'), may hold values from 3.25520833e-05 to 0.03125
- band_reach: int32 [40], P('head'), may hold values from 1 to 24, as said below
Outputs:
- mixed_heads: bfloat16 [6144, 5120], P(('group', 'ctx', 'rep'), 'head'), parts along dimension 0
There are 2 independent parts, one for each index of `group`. A program takes and returns all parts, laid end to end along the dimension named above; an argument that names none is the same for every part. Nothing has to cross between parts.
Inputs may be any that keep to these rules, and one draw needn't show every extreme that they name: `band_reach`: each head's reach is either at most 2 or exactly 24; in every draw some head has reach 2 and some head has 24.
All inputs are finite; a program needn't handle non-finite values.
Results may differ from a plain program's by a relative error of at most 0.0059.
Values may be sent and summed in bfloat16 or wider, within the bound.
No kernel may reach another device: no remote copies, remote signals or barrier semaphores. Data moves between devices by JAX's collectives and lax.ppermute only.
A program may use at most 128 MiB of HBM per device.

v0:
```python
import jax
import jax.numpy as jnp
from jax import lax
from jax.sharding import PartitionSpec as P

BLOCK = 128
REACH = 2


EPSILON = 1e-06


def passed_along(value, axis, steps):
    count = lax.axis_size(axis)
    first, last = (max(0, -steps), min(count, count - steps))
    return lax.ppermute(value, axis, [(source, source + steps) for source in range(first, last)])


def carried_in(part, axis, combine, identity):
    place = lax.axis_index(axis)
    gathered = jax.tree.map(lambda a: lax.all_gather(a, axis), part)
    state = jax.tree.map(lambda a, e: jnp.zeros_like(a) + jnp.asarray(e, a.dtype), part, identity)

    def one(step, state):
        return combine(
            state, jax.tree.map(lambda a: lax.dynamic_index_in_dim(a, step, 0, False), gathered)
        )

    return lax.fori_loop(0, place, one, state)


def combine_states(earlier, later):
    return (later[1][:, None, None] * earlier[0] + later[0], earlier[1] * later[1])


def near_masked(query_rows, key_window, value_window, decay_rate, band_reach, query_pos, key_pos):
    is_full = band_reach > REACH
    distance = query_pos[:, None] - key_pos[None, :]
    block_gap = query_pos[:, None] // BLOCK - key_pos[None, :] // BLOCK
    in_band = jnp.where(
        is_full[:, None, None], block_gap[None] == 0, block_gap[None] <= band_reach[:, None, None]
    )
    allowed = in_band & (distance >= 0)[None] & (key_pos >= 0)[None, None, :]
    scores = jnp.einsum("ihd,jhd->hij", query_rows, key_window, preferred_element_type=jnp.float32)
    fading = jnp.exp(
        -decay_rate[:, None, None] * jnp.maximum(distance, 0).astype(jnp.float32)[None]
    )
    weights = jnp.where(allowed, scores * fading, 0.0).astype(jnp.bfloat16)
    return jnp.einsum("hij,jhd->ihd", weights, value_window, preferred_element_type=jnp.float32)


def retain(
    queries,
    key_vectors,
    value_vectors,
    gate_input,
    decay_rate,
    band_reach,
    norm_gain,
    offset,
    fetch_tail,
    carry_state,
):
    length = queries.shape[0]
    heads_here = decay_rate.shape[0]
    head_size = queries.shape[1] // heads_here
    tail_span = REACH * BLOCK
    packed = jnp.stack([key_vectors[length - tail_span :], value_vectors[length - tail_span :]])
    arrived = fetch_tail(packed)

    def split_heads(rows_in):
        return rows_in.reshape(rows_in.shape[0], heads_here, head_size)

    query_rows = split_heads(queries)
    key_rows = split_heads(key_vectors)
    value_rows = split_heads(value_vectors)
    blocks_here = length // BLOCK
    offsets = jnp.arange(BLOCK, dtype=jnp.float32)
    key_fade = jnp.exp(-decay_rate[None, :] * (BLOCK - offsets)[:, None])
    faded_keys = (
        key_rows.reshape(blocks_here, BLOCK, heads_here, head_size).astype(jnp.float32)
        * key_fade[None, :, :, None]
    ).astype(jnp.bfloat16)
    states = jnp.einsum(
        "cthx,cthy->hcxy",
        faded_keys,
        value_rows.reshape(blocks_here, BLOCK, heads_here, head_size),
        preferred_element_type=jnp.float32,
    )
    block_index = jnp.arange(blocks_here, dtype=jnp.float32)
    to_final = jnp.exp(-decay_rate[:, None] * ((blocks_here - 1 - block_index) * BLOCK)[None, :])
    summary = jnp.einsum("hc,hcxy->hxy", to_final, states, precision=lax.Precision.HIGHEST)
    chain_power = jnp.exp(-decay_rate * float(length))
    carried = carry_state((summary, chain_power))[0]
    key_window = split_heads(jnp.concatenate([arrived[0], key_vectors], 0))
    value_window = split_heads(jnp.concatenate([arrived[1], value_vectors], 0))
    query_pos = offset + jnp.arange(length, dtype=jnp.int32)
    key_pos = offset - tail_span + jnp.arange(tail_span + length, dtype=jnp.int32)
    near_part = near_masked(
        query_rows, key_window, value_window, decay_rate, band_reach, query_pos, key_pos
    )
    block_gap = block_index[:, None] - 1.0 - block_index[None, :]
    coefficient = jnp.where(
        block_gap[None] >= 0,
        jnp.exp(-decay_rate[:, None, None] * (jnp.maximum(block_gap, 0.0) * BLOCK)[None]),
        0.0,
    )
    entry_fade = jnp.exp(-decay_rate[:, None] * (block_index * BLOCK)[None, :])
    prior_state = (
        jnp.einsum("hcd,hdxy->hcxy", coefficient, states, precision=lax.Precision.HIGHEST)
        + entry_fade[:, :, None, None] * carried[:, None]
    )
    prior_rounded = prior_state.astype(jnp.bfloat16)
    query_fade = jnp.exp(-decay_rate[None, :] * offsets[:, None])
    faded_queries = (
        query_rows.reshape(blocks_here, BLOCK, heads_here, head_size).astype(jnp.float32)
        * query_fade[None, :, :, None]
    ).astype(jnp.bfloat16)
    far_part = jnp.einsum(
        "cthx,hcxy->cthy", faded_queries, prior_rounded, preferred_element_type=jnp.float32
    ).reshape(length, heads_here, head_size)
    is_full = band_reach > REACH
    retained = near_part + jnp.where(is_full[None, :, None], far_part, 0.0)
    row_mean = jnp.mean(retained, axis=-1, keepdims=True)
    centred = retained - row_mean
    variance = jnp.mean(centred * centred, axis=-1, keepdims=True)
    normed = centred * lax.rsqrt(variance + EPSILON)
    gate_rows = split_heads(gate_input).astype(jnp.float32)
    mixed_rows = jax.nn.silu(gate_rows) * normed * norm_gain.reshape(heads_here, head_size)[None]
    return mixed_rows.astype(jnp.bfloat16).reshape(length, heads_here * head_size)


def per_device(queries, key_vectors, value_vectors, gate_input, norm_gain, decay_rate, band_reach):
    offset = lax.axis_index(("ctx", "rep")) * queries.shape[0]

    def fetch_tail(packed):
        return passed_along(packed, ("ctx", "rep"), 1)

    def carry_state(packed_state):
        identity = (jnp.zeros_like(packed_state[0]), jnp.ones_like(packed_state[1]))
        return carried_in(packed_state, ("ctx", "rep"), combine_states, identity)

    return retain(
        queries,
        key_vectors,
        value_vectors,
        gate_input,
        decay_rate,
        band_reach,
        norm_gain,
        offset,
        fetch_tail,
        carry_state,
    )


def solution(mesh):
    return jax.shard_map(
        per_device,
        mesh=mesh,
        in_specs=(
            P(("group", "ctx", "rep"), "head"),
            P(("group", "ctx", "rep"), "head"),
            P(("group", "ctx", "rep"), "head"),
            P(("group", "ctx", "rep"), "head"),
            P("head"),
            P("head"),
            P("head"),
        ),
        out_specs=P(("group", "ctx", "rep"), "head"),
        check_vma=False,
    )
```

profile of v0, /device:TPU:25, one launch (start us, length us, event | category | flops | bytes accessed | tf_op | source)
XLA Modules:
  0.0 246.6 jit_solution(14393510640672791388)
XLA Ops:
  6.6 4.7 %reshape.383 = f32[3,128,20,128]{3,2,1,0:T(8,128)} reshape(bf16[384,2560]{1,0:T(8,128)(2,1)} %param.10) | data formatting | bytes 5898240 | tf_op jit(solution)/shard_map/convert_element_type | solution.py:81
  11.2 3.1 %reshape_reshape.2 = bf16[3,128,20,128]{3,2,1,0:T(8,128)(2,1)S(1)} reshape(bf16[384,2560]{1,0:T(8,128)(2,1)} %param.11) | data formatting | bytes 3932160 | tf_op jit(solution)/shard_map/reshape;reshape | solution.py:87
  15.9 2.9 %multiply_convert_fusion.1 = bf16[3,128,20,128]{3,2,1,0:T(8,128)(2,1)S(1)} fusion(f32[3,128,20,128]{3,2,1,0:T(8,128)} %reshape.383, f32[128,20]{1,0:T(8,128)S(1)} %get-tuple-element.64), kind=kLoop, calls=%fused_computation.13 | loop fusion | flops 1966080 | bytes 5908480 | tf_op jit(solution)/shard_map/convert_element_type | solution.py:83
  19.6 12.1 %fusion.6 = f32[20,1,128,128]{3,1,2,0:T(1,128)} fusion(f32[20,3,128,128]{3,2,1,0:T(8,128)S(1)} %fusion.23, f32[20,3,1,1]{1,0,2,3:T(8,128)S(1)} %get-tuple-element.63), kind=kOutput, calls=%fused_computation.7 | convolution fusion | flops 11796480 | bytes 5243120 | tf_op jit(solution)/shard_map/hc,hcxy->hxy/dot_general | solution.py:92
  31.7 2.8 %copy.29 = bf16[384,2560]{0,1:T(8,128)(2,1)S(1)} copy(bf16[384,2560]{1,0:T(8,128)(2,1)} %param.10) | data formatting | bytes 3932160 | tf_op args[1]
  34.5 4.0 %copy.30 = bf16[384,2560]{0,1:T(8,128)(2,1)} copy(bf16[384,2560]{1,0:T(8,128)(2,1)} %param.11) | data formatting | bytes 3932160 | tf_op args[2]
  38.5 1.5 slice_bitcast_fusion
  40.0 1.8 pad_maximum_fusion
  41.8 1.3 collective-permute-start
  43.1 4.8 %reshape.384 = f32[3,128,20,128]{3,2,1,0:T(8,128)} reshape(bf16[384,2560]{1,0:T(8,128)(2,1)} %param.9) | data formatting | bytes 5898240 | tf_op jit(solution)/shard_map/convert_element_type | solution.py:116
  47.9 4.0 %copy.35 = bf16[384,2560]{0,1:T(8,128)(2,1)} copy(bf16[384,2560]{1,0:T(8,128)(2,1)} %param.9) | data formatting | bytes 3932160 | tf_op args[0]
  51.8 109.6 %all-reduce = f32[160]{0:T(256)S(1)} all-reduce(f32[160]{0:T(256)S(1)} %get-tuple-element.66), channel_id=2, replica_groups=mesh['group'=2,'ctx'=4,'head'=2,'rep'=2] {'ctx','rep'}, use_global_device_ids=true, to_apply=%add | all-reduce | flops 160 | bytes 1280
  161.5 2.4 copy.34
  164.0 4.3 %copy.28 = f32[384,2560]{0,1:T(8,128)} copy(bf16[384,2560]{1,0:T(8,128)(2,1)} %param.12) | data formatting | bytes 5898240 | tf_op jit(solution)/shard_map/convert_element_type | solution.py:128
  171.9 4.3 %multiply_convert_fusion = bf16[3,128,20,128]{3,2,1,0:T(8,128)(2,1)} fusion(f32[3,128,20,128]{3,2,1,0:T(8,128)} %reshape.384, f32[128,20]{1,0:T(8,128)S(1)} %get-tuple-element.65), kind=kLoop, calls=%fused_computation.12 | loop fusion | flops 1966080 | bytes 5908480 | tf_op jit(solution)/shard_map/convert_element_type | solution.py:118
  176.3 1.9 fusion.54
  178.1 1.4 copy.33
  179.7 11.4 %while.12 = (s32[]{:T(128)}, f32[20,128,128]{2,1,0:T(8,128)S(1)}, s32[]{:T(128)}, f32[8,20]{1,0:T(8,128)S(1)}, f32[8,20,128,128]{3,2,1,0:T(8,128)}, /*index=5*/s32[]{:T(128)}, s32[]{:T(128)}, s32[]{:T(128)}) while((s32[]{:T(128)}, f32[20,128,128]{2,1,0:T(8,128)S(1)}, s32[]{:T(128)}, f32[8,20]{1,0:T(8,128)S(1)}, f32[8,20,128,128]{3,2,1,0:T(8,128)}, ...), condition=%wide.region_1.2_spmd, body=%wide.region_0.1_spmd.sunk | while | flops 655365 | bytes 3932527 | solution.py:29
  179.7 1.6 bitcast_add_fusion.3
  181.4 1.6 bitcast_add_fusion.3
  183.0 1.6 bitcast_add_fusion.3
  184.6 1.6 bitcast_add_fusion.3
  186.2 1.6 bitcast_add_fusion.3
  187.9 1.6 bitcast_add_fusion.3
  189.5 1.6 bitcast_add_fusion.3
  191.1 15.9 %add_convert_fusion = bf16[20,3,128,128]{3,1,2,0:T(4,128)(2,1)S(1)} fusion(f32[20,128,128]{2,1,0:T(8,128)S(1)} %get-tuple-element.49, f32[20,3]{1,0:T(8,128)S(1)} %get-tuple-element.62, f32[20,3,128,128]{3,2,1,0:T(8,128)} %copy-done, f32[3,3]{1,0:T(4,128)S(1)} %maximum_multiply_fusion, f32[20]{0:T(128)S(1)} %get-tuple-element.67, pred[3,3]{1,0:T(4,128)(4,1)S(1)} %fusion.47), kind=kOutput, calls=%fused_computation.11 | convolution fusion | flops 38338920 | bytes 7209325 | tf_op jit(solution)/shard_map/hcd,hdxy->hcxy/dot_general | solution.py:110
  207.7 2.3 copy.43
  210.0 5.6 %copy.44 = f32[384,20,128]{0,2,1:T(8,128)} copy(f32[384,20,128]{2,0,1:T(8,128)} %bitcast.49) | data formatting | bytes 7864320 | tf_op jit(solution)/shard_map/reshape | solution.py:121
  215.7 14.7 %fusion.55 = (f32[384,20]{0,1:T(8,128)}, f32[384,20,128]{0,2,1:T(8,128)}) fusion(f32[384,20,128]{0,2,1:T(8,128)} %copy.44, pred[20]{0:T(512)(128)(4,1)S(1)} %broadcast_compare_fusion.1, f32[384,640]{0,1:T(8,128)} %fusion.32, f32[20]{0:T(128)S(1)} %get-tuple-element.67, s32[384,640]{0,1:T(8,128)} %broadcast_subtract_fusion, s32[20]{0:T(128)S(1)} %copy-done.6, ...), kind=kOutput, calls=%fused_computation.84 | convolution fusion | flops 2571952640 | bytes 18873140 | tf_op jit(solution)/shard_map/hij,jhd->ihd/dot_general | solution.py:49
  231.3 2.9 %multiply_reduce_fusion = f32[384,20]{0,1:T(8,128)S(1)} fusion(f32[384,20,128]{0,2,1:T(8,128)} %get-tuple-element.69, f32[384,20]{0,1:T(8,128)S(1)} %broadcast_multiply_fusion), kind=kLoop, calls=%fused_computation.16 | loop fusion | flops 2941440 | bytes 3993600 | tf_op jit(solution)/shard_map/reduce_sum | solution.py:126
  234.2 3.1 %multiply_convert_fusion.2 = bf16[384,20,128]{0,2,1:T(8,128)(2,1)S(1)} fusion(f32[384,20,128]{0,2,1:T(8,128)S(1)} %bitcast.48, f32[384,20,128]{0,2,1:T(8,128)} %get-tuple-element.69, f32[20,128]{1,0:T(8,128)S(1)} %bitcast.58, f32[384,20]{0,1:T(8,128)S(1)} %add_rsqrt_fusion, f32[384,20]{0,1:T(8,128)S(1)} %broadcast_multiply_fusion), kind=kLoop, calls=%fused_computation.15 | loop fusion | flops 8847360 | bytes 9902080 | tf_op jit(solution)/shard_map/convert_element_type | solution.py:130
  237.3 2.4 copy.45
  (51 shorter events, 7.2 us)
Async XLA Ops:
  6.5 173.0 %all-gather.4.cloned.1.call-start = ((), (), s32[]{:S(2)}) async-start(), calls=%async_computation | async-start | bytes 11796480 | tf_op jit(solution)/shard_map/all_gather | solution.py:21
  11.2 3.1 %copy-start.7 = (u32[32]{0:T(128)S(1)}, u32[32]{0:T(128)}, u32[]{:S(2)}) copy-start(u32[32]{0:T(128)} %constant.89) | copy-start | bytes 388
  11.2 4.3 %copy-start.5 = (f32[20]{0:T(128)S(1)}, f32[20]{0:T(128)}, u32[]{:S(2)}) copy-start(f32[20]{0:T(128)} %param.14) | copy-start | bytes 244
  19.6 12.1 %copy-start = (f32[20,3,128,128]{3,2,1,0:T(8,128)}, f32[20,3,128,128]{3,2,1,0:T(8,128)S(1)}, u32[]{:S(2)}) copy-start(f32[20,3,128,128]{3,2,1,0:T(8,128)S(1)} %fusion.23) | copy-start | bytes 11796484
  41.8 134.5 %collective-permute-start = (bf16[2,256,2560]{1,2,0:T(8,128)(2,1)}, bf16[2,256,2560]{1,2,0:T(8,128)(2,1)}, u32[]{:S(2)}, u32[]{:S(2)}) collective-permute-start(bf16[2,256,2560]{1,2,0:T(8,128)(2,1)} %pad_maximum_fusion), channel_id=1, source_target_pairs={{0,1},{1,4},{4,5},{5,8},{8,9},{9,12},{12,13},{2,3},{3,6},{6,7},{7,... | collective-permute-start | bytes 7864328 | tf_op jit(solution)/shard_map/ppermute | solution.py:16
  164.0 4.4 %copy-start.6 = (s32[20]{0:T(128)S(1)}, s32[20]{0:T(128)}, u32[]{:S(2)}) copy-start(s32[20]{0:T(128)} %param.15) | copy-start | bytes 244
  191.1 15.9 %copy-start.2 = (bf16[3,128,20,128]{3,2,1,0:T(8,128)(2,1)S(1)}, bf16[3,128,20,128]{3,2,1,0:T(8,128)(2,1)}, u32[]{:S(2)}) copy-start(bf16[3,128,20,128]{3,2,1,0:T(8,128)(2,1)} %multiply_convert_fusion) | copy-start | bytes 5898244
  210.0 5.6 %copy-start.3 = (bf16[384,2560]{0,1:T(8,128)(2,1)S(1)}, bf16[384,2560]{0,1:T(8,128)(2,1)}, u32[]{:S(2)}) copy-start(bf16[384,2560]{0,1:T(8,128)(2,1)} %copy.30) | copy-start | bytes 5898244
  230.3 3.9 %copy-start.1 = (f32[384,2560]{0,1:T(8,128)S(1)}, f32[384,2560]{0,1:T(8,128)}, u32[]{:S(2)}) copy-start(f32[384,2560]{0,1:T(8,128)} %copy.28) | copy-start | bytes 11796484
  230.3 3.9 %copy-start.4 = (f32[2560]{0:T(1024)S(1)}, f32[2560]{0:T(1024)}, u32[]{:S(2)}) copy-start(f32[2560]{0:T(1024)} %param.13) | copy-start | bytes 30724
Sparse Core Ops, SparseCore 0:
  31.8 117.5 all-gather.3
where the time goes:
time: 248 us; the launch traced here: 247 us
  blocking collectives  110 us (44%)
  local copies, waits for them, and re-layouts  46.1 us (19%)
  matrix products  44.1 us (18%)
  other arithmetic  30.9 us (12%)
  between operations  14.3 us (6%)
    unnamed x1, blocking collectives  110 us
    dot_general x1, matrix products, retain(): jnp.einsum('hcd,hdxy->hcxy', coefficient, states, precision=lax.Precision...  15.9 us
    dot_general x1, matrix products, near_masked(): jnp.einsum('hij,jhd->ihd', weights, value_window, preferred_element_type=...  14.7 us
    dot_general x1, matrix products, retain(): jnp.einsum('hc,hcxy->hxy', to_final, states, precision=lax.Precision.HIGH...  12.1 us
    unnamed x21, local copies, waits for them, and re-layouts  11.4 us
    add x7, other arithmetic, combine_states(): later[1][:, None, None] * earlier[0] + later[0]  11.1 us
    reshape x1, local copies, waits for them, and re-layouts, retain(): far_part = jnp.einsum('cthx,hcxy->cthy', faded_queries, prior_rounded, pr...  5.64 us
  transfers between devices with their start and end apart: 2, of which 0 were waited for; matrix products, arithmetic and copies ran while one was open for 15% of the time, Pallas kernels for 0%

commit v1 on v0

v1 whole, which is shorter than its diff:
```python
import jax
import jax.numpy as jnp
from jax import lax
from jax.experimental import pallas as pl
from jax.experimental.pallas import tpu as pltpu
from jax.sharding import PartitionSpec as P

BLOCK = 128
REACH = 2
EPSILON = 1e-06
F32 = jnp.float32
BF16 = jnp.bfloat16
VMEM_LIMIT = 32 * 1024 * 1024


def group_of(heads):
    return max(g for g in range(1, 6) if heads % g == 0)


def row_offsets():
    return lax.broadcasted_iota(jnp.int32, (BLOCK, BLOCK), 0).astype(F32)


def power(rate, tokens):
    return jnp.exp(jnp.full((1, BLOCK), -tokens, F32) * rate)


def states_kernel(place, rates, reaches, k_ref, v_ref, carry_ref, second_ref):
    blocks = k_ref.shape[0] // BLOCK
    group = carry_ref.shape[0]
    offsets = row_offsets()
    for g in range(group):
        head = (place[0] + pl.program_id(0)) * group + g
        rate = rates[head]
        is_full = (reaches[head] > REACH).astype(F32)
        base = jnp.exp((offsets - float(BLOCK)) * rate)
        columns = slice(g * BLOCK, (g + 1) * BLOCK)
        parts = []
        for t in range(blocks):
            faded = k_ref[t * BLOCK : (t + 1) * BLOCK, columns].astype(F32) * base
            if t == blocks - 2:
                second = faded.astype(BF16)
            if t < blocks - 1:
                faded = faded * (power(rate, (blocks - 1 - t) * BLOCK) * is_full)
            parts.append(faded.astype(BF16))
        values = v_ref[:, columns]
        dims = (((0,), (0,)), ((), ()))
        carry = lax.dot_general(jnp.concatenate(parts, 0), values, dims, preferred_element_type=F32)
        carry_ref[g] = carry.astype(BF16)
        rows = values[(blocks - 2) * BLOCK : (blocks - 1) * BLOCK]
        second_ref[g] = lax.dot_general(second, rows, dims, preferred_element_type=F32).astype(BF16)


def block_states(keys, values, rates, reaches, place, count):
    length, features = keys.shape
    size = features // rates.shape[0]
    group = group_of(count)
    rows = pl.BlockSpec((length, group * size), lambda i, place, rates, reaches: (0, place[0] + i))
    state = pl.BlockSpec((group, size, size), lambda i, place, rates, reaches: (i, 0, 0))
    shape = jax.ShapeDtypeStruct((count, size, size), BF16)
    return pl.pallas_call(
        states_kernel,
        grid_spec=pltpu.PrefetchScalarGridSpec(
            num_scalar_prefetch=3,
            grid=(count // group,),
            in_specs=[rows, rows],
            out_specs=[state, state],
        ),
        out_shape=[shape, shape],
        compiler_params=pltpu.CompilerParams(vmem_limit_bytes=VMEM_LIMIT),
        name="block_states",
    )(jnp.reshape(place * (count // group), (1,)), rates, reaches, keys, values)


def local_kernel(rates, reaches, q_ref, k_ref, v_ref, out_ref):
    length = q_ref.shape[0]
    blocks = length // BLOCK
    group = q_ref.shape[1] // BLOCK
    gap = row_offsets() - lax.broadcasted_iota(jnp.int32, (BLOCK, BLOCK), 1).astype(F32)
    causal = gap >= 0
    for g in range(group):
        head = pl.program_id(0) * group + g
        rate = rates[head]
        reach = reaches[head]
        columns = slice(g * BLOCK, (g + 1) * BLOCK)
        fading = jnp.exp(gap * (-rate))
        tables = [jnp.where(causal, fading, 0.0)]
        for back in range(1, blocks):
            tables.append(fading * (power(rate, back * BLOCK) * (reach >= back).astype(F32)))
        for t in range(blocks):
            rows = slice(t * BLOCK, (t + 1) * BLOCK)
            scores = lax.dot_general(
                q_ref[rows, columns],
                k_ref[: (t + 1) * BLOCK, columns],
                (((1,), (1,)), ((), ())),
                preferred_element_type=F32,
            )
            weights = jnp.concatenate(
                [scores[:, u * BLOCK : (u + 1) * BLOCK] * tables[t - u] for u in range(t + 1)], 1
            ).astype(BF16)
            out_ref[rows, columns] = jnp.dot(
                weights, v_ref[: (t + 1) * BLOCK, columns], preferred_element_type=F32
            )


def local_part(queries, keys, values, rates, reaches):
    length, features = queries.shape
    heads = rates.shape[0]
    size = features // heads
    group = group_of(heads)
    rows = pl.BlockSpec((length, group * size), lambda i, rates, reaches: (0, i))
    return pl.pallas_call(
        local_kernel,
        grid_spec=pltpu.PrefetchScalarGridSpec(
            num_scalar_prefetch=2, grid=(heads // group,), in_specs=[rows] * 3, out_specs=rows
        ),
        out_shape=jax.ShapeDtypeStruct((length, features), F32),
        compiler_params=pltpu.CompilerParams(vmem_limit_bytes=VMEM_LIMIT),
        cost_estimate=pl.CostEstimate(
            flops=12 * heads * BLOCK**3 * 2, bytes_accessed=10 * length * features, transcendentals=0
        ),
        name="local_part",
    )(rates, reaches, queries, keys, values)


def finish_kernel(place, rates, reaches, q_ref, g_ref, near_ref, gain_ref, carry_ref, second_ref, _, out_ref):
    blocks = q_ref.shape[0] // BLOCK
    group = carry_ref.shape[0]
    offsets = row_offsets()
    for g in range(group):
        head = (place[0] + pl.program_id(0)) * group + g
        rate = rates[head]
        reach = reaches[head]
        columns = slice(g * BLOCK, (g + 1) * BLOCK)
        fade = jnp.exp(offsets * (-rate))
        faded = [q_ref[t * BLOCK : (t + 1) * BLOCK, columns].astype(F32) * fade for t in range(blocks)]
        parts = [
            (faded[t] * (power(rate, t * BLOCK) * (reach > t).astype(F32))).astype(BF16)
            for t in range(blocks)
        ]
        far = jnp.dot(jnp.concatenate(parts, 0), carry_ref[g], preferred_element_type=F32)
        is_second = jnp.logical_and(reach >= 2, reach <= REACH).astype(F32)
        second = (faded[0] * (power(rate, BLOCK) * is_second)).astype(BF16)
        extra = jnp.dot(second, second_ref[g], preferred_element_type=F32)
        gain = gain_ref[:, columns]
        for t in range(blocks):
            rows = slice(t * BLOCK, (t + 1) * BLOCK)
            retained = near_ref[rows, columns] + far[rows]
            if t == 0:
                retained = retained + extra
            centred = retained - jnp.mean(retained, axis=-1, keepdims=True)
            variance = jnp.mean(centred * centred, axis=-1, keepdims=True)
            gate = g_ref[rows, columns].astype(F32)
            silu = gate / (1.0 + jnp.exp(-gate))
            out_ref[rows, columns] = (silu * (centred * lax.rsqrt(variance + EPSILON)) * gain).astype(BF16)


def finish(queries, gates, near, gain, rates, reaches, carry, second, place, into):
    length, features = queries.shape
    size = features // rates.shape[0]
    count = carry.shape[0]
    group = group_of(count)
    rows = pl.BlockSpec((length, group * size), lambda i, place, rates, reaches: (0, place[0] + i))
    state = pl.BlockSpec((group, size, size), lambda i, place, rates, reaches: (i, 0, 0))
    line = pl.BlockSpec((1, group * size), lambda i, place, rates, reaches: (0, place[0] + i))
    operands = [queries, gates, near, gain[None], carry, second]
    specs = [rows, rows, rows, line, state, state]
    aliases = {}
    if into is None:
        into = jnp.zeros((8, BLOCK), BF16)
    else:
        aliases = {9: 0}
    return pl.pallas_call(
        finish_kernel,
        grid_spec=pltpu.PrefetchScalarGridSpec(
            num_scalar_prefetch=3,
            grid=(count // group,),
            in_specs=specs + [pl.BlockSpec(memory_space=pl.ANY)],
            out_specs=rows,
        ),
        out_shape=jax.ShapeDtypeStruct((length, features), BF16),
        input_output_aliases=aliases,
        compiler_params=pltpu.CompilerParams(vmem_limit_bytes=VMEM_LIMIT),
        name="finish",
    )(jnp.reshape(place * (count // group), (1,)), rates, reaches, *operands, into)


def mixed(a, x, b, y):
    total = a[:, None, None] * x.astype(F32) + b[:, None, None] * y.astype(F32)
    return total.astype(BF16)


def chained(total, step_fade):
    count = lax.axis_size("ctx")
    one = jnp.ones_like(step_fade)
    current, arrived = total, None
    for hop in range(count - 1):
        got = lax.ppermute(current, "ctx", [(hop, hop + 1)])
        arrived = got if arrived is None else arrived + got
        if hop < count - 2:
            current = mixed(step_fade, got, one, total)
    return arrived


def in_two_steps(total, step_fade):
    one = jnp.ones_like(step_fade)
    first = lax.ppermute(total, "ctx", [(0, 1), (2, 3)])
    current = mixed(step_fade, first, one, total)
    near = lax.ppermute(current, "ctx", [(1, 2)])
    far = lax.ppermute(current, "ctx", [(1, 3)])
    return mixed(one, first, jnp.where(lax.axis_index("ctx") == 3, step_fade, one), near + far)


def per_device(queries, key_vectors, value_vectors, gate_input, norm_gain, decay_rate, band_reach):
    length = queries.shape[0]
    heads = decay_rate.shape[0]
    half = heads // 2
    rep = lax.axis_index("rep")
    other = 1 - rep
    away_carry, away_second = block_states(key_vectors, value_vectors, decay_rate, band_reach, other, half)
    own_carry, own_second = block_states(key_vectors, value_vectors, decay_rate, band_reach, rep, half)
    swap = [(0, 1), (1, 0)]
    from_pair = lax.ppermute(away_carry, "rep", swap)

    full = (band_reach > REACH).astype(F32)
    device_fade = lax.dynamic_slice_in_dim(full * jnp.exp(-decay_rate * float(length)), rep * half, half)
    chip_fade = lax.dynamic_slice_in_dim(full * jnp.exp(-decay_rate * float(2 * length)), rep * half, half)
    one = jnp.ones_like(device_fade)
    first = rep == 0
    total = mixed(jnp.where(first, device_fade, one), own_carry, jnp.where(first, one, device_fade), from_pair)

    cut = half * 3 // 5
    plans = [(slice(0, cut), chained), (slice(cut, half), in_two_steps if lax.axis_size("ctx") == 4 else chained)]
    own, away = [], []
    for part, plan in plans:
        arrived = plan(total[part], chip_fade[part])
        zero = jnp.zeros_like(one[part])
        is_first = first.astype(F32)
        fade = device_fade[part]
        own.append(mixed(jnp.where(first, one[part], fade), arrived, zero + (1.0 - is_first), from_pair[part]))
        sent = mixed(jnp.where(first, fade, one[part]), arrived, zero + is_first, own_carry[part])
        away.append(lax.ppermute(sent, "rep", swap))
    count = lax.axis_size("ctx") * 2
    steps = [(i, i + 1) for i in range(count - 1)]
    second_own = lax.ppermute(away_second, ("ctx", "rep"), steps)
    second_away = lax.ppermute(own_second, ("ctx", "rep"), steps)

    near = local_part(queries, key_vectors, value_vectors, decay_rate, band_reach)
    out = finish(queries, gate_input, near, norm_gain, decay_rate, band_reach, jnp.concatenate(own), second_own, rep, None)
    return finish(queries, gate_input, near, norm_gain, decay_rate, band_reach, jnp.concatenate(away), second_away, other, out)


def solution(mesh):
    rows = P(("group", "ctx", "rep"), "head")
    return jax.shard_map(
        per_device,
        mesh=mesh,
        in_specs=(rows, rows, rows, rows, P("head"), P("head"), P("head")),
        out_specs=rows,
        check_vma=False,
    )
```

time: 248 us -> 65.7 us (0.26)
  blocking collectives: 110 us -> 0 us
  matrix products: 44.1 us -> 0 us
  local copies, waits for them, and re-layouts: 46.1 us -> 6.08 us
  other arithmetic: 30.9 us -> 4.14 us
  Pallas kernels: 0 us -> 22.6 us
  waiting for transfers between devices: 0.02 us -> 16.7 us
  starting transfers between devices: 1.28 us -> 15.5 us
  between operations: 14.3 us -> 0.27 us
    unnamed x1 -> x0, blocking collectives: 110 us -> none
    dot_general x5 -> x0, matrix products: 44.1 us -> none  [the longest x1 15.9 us: retain(): jnp.einsum('hcd,hdxy->hcxy', coefficient, states, precision=lax.Precision...]
    pallas_call x0 -> x5, Pallas kernels: none -> 22.6 us  [the longest x1 11.2 us: local_part(): pl.pallas_call(local_kernel, grid_spec=pltpu.PrefetchScalarGridSpec(num_s...]
    ppermute x1 -> x11, waiting for transfers between devices: 0.01 us -> 16.7 us  [the longest x1 6.6 us: in_two_steps(): first = lax.ppermute(total, 'ctx', [(0, 1), (2, 3)])]
    ppermute x1 -> x11, starting transfers between devices: 1.28 us -> 15.5 us  [the longest x2 6.09 us: per_device(): away.append(lax.ppermute(sent, 'rep', swap))]
    convert_element_type x3 -> x0, local copies, waits for them, and re-layouts: 13.8 us -> none  [the longest x1 4.82 us: retain(): query_rows.reshape(blocks_here, BLOCK, heads_here, head_size)]
    add x7 -> x0, other arithmetic: 11.1 us -> none  [combine_states(): later[1][:, None, None] * earlier[0] + later[0]]
    reshape x2 -> x0, local copies, waits for them, and re-layouts: 8.05 us -> none  [the longest x1 5.64 us: retain(): far_part = jnp.einsum('cthx,hcxy->cthy', faded_queries, prior_rounded, pr...]
  transfers between devices with their start and end apart: 2 -> 11, of which waited for: 0 -> 3; matrix products, arithmetic and copies ran while one was open for 15% -> 7% of each run, Pallas kernels for 0% -> 25%
where the time goes in v1:
time: 65.7 us; the launch traced here: 65.3 us
  Pallas kernels  22.6 us (34%)
  waiting for transfers between devices  16.7 us (25%)
  starting transfers between devices  15.5 us (24%)
  local copies, waits for them, and re-layouts  6.08 us (9%)
  other arithmetic  4.14 us (6%)
    pallas_call x1, Pallas kernels, local_part(): pl.pallas_call(local_kernel, grid_spec=pltpu.PrefetchScalarGridSpec(num_s...  11.2 us
    pallas_call x2, Pallas kernels, finish(): pl.pallas_call(finish_kernel, grid_spec=pltpu.PrefetchScalarGridSpec(num_...  7.58 us
    ppermute x1, waiting for transfers between devices, in_two_steps(): first = lax.ppermute(total, 'ctx', [(0, 1), (2, 3)])  6.6 us
    ppermute x3, waiting for transfers between devices, chained(): got = lax.ppermute(current, 'ctx', [(hop, hop + 1)])  6.24 us
    ppermute x2, starting transfers between devices, per_device(): away.append(lax.ppermute(sent, 'rep', swap))  6.09 us
    unnamed x24, local copies, waits for them, and re-layouts  5.97 us
    pallas_call x2, Pallas kernels, block_states(): pl.pallas_call(states_kernel, grid_spec=pltpu.PrefetchScalarGridSpec(num_...  3.85 us
    convert_element_type x7, other arithmetic, mixed(): return total.astype(BF16)  3.84 us
  transfers between devices with their start and end apart: 11, of which 3 were waited for; matrix products, arithmetic and copies ran while one was open for 7% of the time, Pallas kernels for 25%

profile of v1, /device:TPU:25, one launch (start us, length us, event | category | flops | bytes accessed | tf_op | source)
XLA Modules:
  0.0 65.3 jit_solution(11369890934963675277)
XLA Ops:
  0.0 1.5 %copy-done.1 = bf16[384,2560]{1,0:T(8,128)(2,1)S(1)} copy-done((bf16[384,2560]{1,0:T(8,128)(2,1)S(1)}, bf16[384,2560]{1,0:T(8,128)(2,1)}, u32[]{:S(2)}) %copy-start.1) | copy-done | bytes 1966104
  1.5 1.5 %copy-done.3 = bf16[384,2560]{1,0:T(8,128)(2,1)S(1)} copy-done((bf16[384,2560]{1,0:T(8,128)(2,1)S(1)}, bf16[384,2560]{1,0:T(8,128)(2,1)}, u32[]{:S(2)}) %copy-start.3) | copy-done | bytes 1966104
  3.1 0.7 %copy-done.7 = f32[20]{0:T(128)S(1)} copy-done((f32[20]{0:T(128)S(1)}, f32[20]{0:T(128)}, u32[]{:S(2)}) %copy-start.7) | copy-done | bytes 104
  3.8 0.7 %copy-done.9 = s32[20]{0:T(128)S(1)} copy-done((s32[20]{0:T(128)S(1)}, s32[20]{0:T(128)}, u32[]{:S(2)}) %copy-start.9) | copy-done | bytes 104
  4.4 2.3 %block_states.3 = (bf16[10,128,128]{2,1,0:T(8,128)(2,1)}, bf16[10,128,128]{2,1,0:T(8,128)(2,1)}) custom-call(s32[1]{0:T(128)} %bitcast.place, f32[20]{0:T(128)S(1)} %copy-done.7, s32[20]{0:T(128)S(1)} %copy-done.9, bf16[384,2560]{1,0:T(8,128)(2,1)S(1)} %copy-done.1, bf16[384,2560]{1,0:T(8,128)(2,1)S(1)} %copy-done.3), custom_call_target="tpu_custom_call" | custom-call | tf_op jit(solution)/shard_map/block_states/pallas_call | solution.py:61
  6.7 0.7 %collective-permute-start = (bf16[10,128,128]{2,1,0:T(8,128)(2,1)}, bf16[10,128,128]{2,1,0:T(8,128)(2,1)}, u32[]{:S(2)}, u32[]{:S(2)}) collective-permute-start(bf16[10,128,128]{2,1,0:T(8,128)(2,1)} %get-tuple-element.10), channel_id=1, source_target_pairs={{0,1},{1,0},{2,3},{3,2},{4,5},{5,4},{6,7},{7,6},{8,9},{9,8},{10,11... | collective-permute-start | bytes 983048 | tf_op jit(solution)/shard_map/ppermute | solution.py:223
  7.4 1.3 %collective-permute-start.10 = (bf16[10,128,128]{2,1,0:T(8,128)(2,1)}, bf16[10,128,128]{2,1,0:T(8,128)(2,1)S(1)}, u32[]{:S(2)}, u32[]{:S(2)}) collective-permute-start(bf16[10,128,128]{2,1,0:T(8,128)(2,1)} %get-tuple-element.12), channel_id=1, source_target_pairs={{0,1},{1,4},{4,5},{5,8},{8,9},{9,12},{12,13},{2,3},{3,6},{6,7},{7,... | collective-permute-start | bytes 983048 | tf_op jit(solution)/shard_map/ppermute | solution.py:245
  8.7 1.5 %copy-done.4 = bf16[384,2560]{1,0:T(8,128)(2,1)S(1)} copy-done((bf16[384,2560]{1,0:T(8,128)(2,1)S(1)}, bf16[384,2560]{1,0:T(8,128)(2,1)}, u32[]{:S(2)}) %copy-start.4) | copy-done | bytes 1966104
  10.2 1.6 %block_states.2 = (bf16[10,128,128]{2,1,0:T(8,128)(2,1)S(1)}, bf16[10,128,128]{2,1,0:T(8,128)(2,1)S(1)}) custom-call(s32[1]{0:T(128)} %bitcast.1.place, f32[20]{0:T(128)S(1)} %copy-done.8, s32[20]{0:T(128)S(1)} %copy-done.10, bf16[384,2560]{1,0:T(8,128)(2,1)S(1)} %copy-done.2, bf16[384,2560]{1,0:T(8,128)(2,1)S(1)} %copy-done.4), custom_call_target="tpu_custom_call" | custom-call | tf_op jit(solution)/shard_map/block_states/pallas_call | solution.py:61
  11.8 1.3 %collective-permute-start.9 = (bf16[10,128,128]{2,1,0:T(8,128)(2,1)S(1)}, bf16[10,128,128]{2,1,0:T(8,128)(2,1)S(1)}, u32[]{:S(2)}, u32[]{:S(2)}) collective-permute-start(bf16[10,128,128]{2,1,0:T(8,128)(2,1)S(1)} %get-tuple-element.11), channel_id=1, source_target_pairs={{0,1},{1,4},{4,5},{5,8},{8,9},{9,12},{12,13},{2,3},{3,6},{6,7},{7,... | collective-permute-start | bytes 983048 | tf_op jit(solution)/shard_map/ppermute | solution.py:246
  13.1 0.1 broadcast_select_fusion.4
  13.4 1.2 %add_convert_fusion = bf16[10,128,128]{2,1,0:T(8,128)(2,1)S(1)} fusion(bf16[10,128,128]{2,1,0:T(8,128)(2,1)} %collective-permute-done, bf16[10,128,128]{2,1,0:T(8,128)(2,1)S(1)} %get-tuple-element.9, f32[10]{0:T(128)S(1)} %broadcast_select_fusion.3, f32[10]{0:T(128)S(1)} %get-tuple-element.15), kind=kLoop, calls=%fused_computation | loop fusion | flops 983040 | bytes 983120 | tf_op jit(solution)/shard_map/convert_element_type | solution.py:190
  14.6 1.3 %collective-permute-start.5 = (bf16[4,128,128]{2,1,0:T(8,128)(2,1)S(1)}, bf16[4,128,128]{2,1,0:T(8,128)(2,1)S(1)}, u32[]{:S(2)}, u32[]{:S(2)}) collective-permute-start(bf16[4,128,128]{2,1,0:T(8,128)(2,1)S(1)} %slice.41), channel_id=1, source_target_pairs={{0,4},{8,12},{1,5},{9,13},{2,6},{10,14},{3,7},{11,15},{16,20},{24,... | collective-permute-start | bytes 393224 | tf_op jit(solution)/shard_map/ppermute | solution.py:207
  15.9 0.7 %collective-permute-start.1 = (bf16[6,128,128]{2,1,0:T(8,128)(2,1)S(1)}, bf16[6,128,128]{2,1,0:T(8,128)(2,1)S(1)}, u32[]{:S(2)}, u32[]{:S(2)}) collective-permute-start(bf16[6,128,128]{2,1,0:T(8,128)(2,1)S(1)} %slice.40), channel_id=1, source_target_pairs={{0,4},{1,5},{2,6},{3,7},{16,20},{17,21},{18,22},{19,23}} | collective-permute-start | bytes 589832 | tf_op jit(solution)/shard_map/ppermute | solution.py:198
  16.6 6.6 %collective-permute-done.5 = bf16[4,128,128]{2,1,0:T(8,128)(2,1)S(1)} collective-permute-done((bf16[4,128,128]{2,1,0:T(8,128)(2,1)S(1)}, bf16[4,128,128]{2,1,0:T(8,128)(2,1)S(1)}, u32[]{:S(2)}, u32[]{:S(2)}) %collective-permute-start.5) | collective-permute-done | bytes 131104 | tf_op jit(solution)/shard_map/ppermute | solution.py:207
  23.2 0.1 fusion.7
  23.4 1.6 %collective-permute-start.7 = (bf16[4,128,128]{2,1,0:T(8,128)(2,1)S(1)}, bf16[4,128,128]{2,1,0:T(8,128)(2,1)S(1)}, u32[]{:S(2)}, u32[]{:S(2)}) collective-permute-start(bf16[4,128,128]{2,1,0:T(8,128)(2,1)S(1)} %fusion.7), channel_id=1, source_target_pairs={{4,12},{5,13},{6,14},{7,15},{20,28},{21,29},{22,30},{23,31}} | collective-permute-start | bytes 393224 | tf_op jit(solution)/shard_map/ppermute | solution.py:210
  24.9 0.7 %collective-permute-start.6 = (bf16[4,128,128]{2,1,0:T(8,128)(2,1)S(1)}, bf16[4,128,128]{2,1,0:T(8,128)(2,1)S(1)}, u32[]{:S(2)}, u32[]{:S(2)}) collective-permute-start(bf16[4,128,128]{2,1,0:T(8,128)(2,1)S(1)} %fusion.7), channel_id=1, source_target_pairs={{4,8},{5,9},{6,10},{7,11},{20,24},{21,25},{22,26},{23,27}} | collective-permute-start | bytes 393224 | tf_op jit(solution)/shard_map/ppermute | solution.py:209
  25.6 0.1 fusion
  25.8 0.7 %collective-permute-start.2 = (bf16[6,128,128]{2,1,0:T(8,128)(2,1)S(1)}, bf16[6,128,128]{2,1,0:T(8,128)(2,1)S(1)}, u32[]{:S(2)}, u32[]{:S(2)}) collective-permute-start(bf16[6,128,128]{2,1,0:T(8,128)(2,1)S(1)} %fusion), channel_id=1, source_target_pairs={{4,8},{5,9},{6,10},{7,11},{20,24},{21,25},{22,26},{23,27}} | collective-permute-start | bytes 589832 | tf_op jit(solution)/shard_map/ppermute | solution.py:198
  26.4 3.8 %collective-permute-done.7 = bf16[4,128,128]{2,1,0:T(8,128)(2,1)S(1)} collective-permute-done((bf16[4,128,128]{2,1,0:T(8,128)(2,1)S(1)}, bf16[4,128,128]{2,1,0:T(8,128)(2,1)S(1)}, u32[]{:S(2)}, u32[]{:S(2)}) %collective-permute-start.7) | collective-permute-done | bytes 131104 | tf_op jit(solution)/shard_map/ppermute | solution.py:210
  30.2 1.0 %fusion.12 = (bf16[4,128,128]{2,1,0:T(8,128)(2,1)S(1)}, bf16[4,128,128]{2,1,0:T(8,128)(2,1)S(1)}) fusion(bf16[10,128,128]{2,1,0:T(8,128)(2,1)} %collective-permute-done, f32[]{:T(128)S(6)} %sub.8, f32[4]{0:T(128)S(1)} %get-tuple-element.24, bf16[4,128,128]{2,1,0:T(8,128)(2,1)S(1)} %collective-permute-done.6, ...), kind=kLoop, calls=%fused_computation.23 | loop fusion | flops 786432 | bytes 786468 | tf_op jit(solution)/shard_map/convert_element_type | solution.py:190
  31.3 0.1 fusion.1
  31.4 1.3 %collective-permute-start.3 = (bf16[6,128,128]{2,1,0:T(8,128)(2,1)S(1)}, bf16[6,128,128]{2,1,0:T(8,128)(2,1)S(1)}, u32[]{:S(2)}, u32[]{:S(2)}) collective-permute-start(bf16[6,128,128]{2,1,0:T(8,128)(2,1)S(1)} %fusion.1), channel_id=1, source_target_pairs={{8,12},{9,13},{10,14},{11,15},{24,28},{25,29},{26,30},{27,31}} | collective-permute-start | bytes 589832 | tf_op jit(solution)/shard_map/ppermute | solution.py:198
  32.7 0.1 fusion.10
  32.8 3.6 %collective-permute-start.8 = (bf16[4,128,128]{2,1,0:T(8,128)(2,1)S(1)}, bf16[4,128,128]{2,1,0:T(8,128)(2,1)S(1)}, u32[]{:S(2)}, u32[]{:S(2)}) collective-permute-start(bf16[4,128,128]{2,1,0:T(8,128)(2,1)S(1)} %fusion.10), channel_id=1, source_target_pairs={{0,1},{1,0},{2,3},{3,2},{4,5},{5,4},{6,7},{7,6},{8,9},{9,8},{10,11... | collective-permute-start | bytes 393224 | tf_op jit(solution)/shard_map/ppermute | solution.py:242
  36.4 6.2 %collective-permute-done.3 = bf16[6,128,128]{2,1,0:T(8,128)(2,1)S(1)} collective-permute-done((bf16[6,128,128]{2,1,0:T(8,128)(2,1)S(1)}, bf16[6,128,128]{2,1,0:T(8,128)(2,1)S(1)}, u32[]{:S(2)}, u32[]{:S(2)}) %collective-permute-start.3) | collective-permute-done | bytes 196640 | tf_op jit(solution)/shard_map/ppermute | solution.py:198
  42.6 1.1 %fusion.5 = (bf16[6,128,128]{2,1,0:T(8,128)(2,1)S(1)}, bf16[6,128,128]{2,1,0:T(8,128)(2,1)S(1)}) fusion(bf16[10,128,128]{2,1,0:T(8,128)(2,1)} %collective-permute-done, f32[]{:T(128)S(6)} %sub.8, f32[6]{0:T(128)S(1)} %get-tuple-element.21, bf16[6,128,128]{2,1,0:T(8,128)(2,1)S(1)} %collective-permute-done.3, ...), kind=kLoop, calls=%fused_computation.10 | loop fusion | flops 1277952 | bytes 1376312 | tf_op jit(solution)/shard_map/convert_element_type | solution.py:190
  43.8 2.5 %collective-permute-start.4 = (bf16[6,128,128]{2,1,0:T(8,128)(2,1)S(1)}, bf16[6,128,128]{2,1,0:T(8,128)(2,1)S(1)}, u32[]{:S(2)}, u32[]{:S(2)}) collective-permute-start(bf16[6,128,128]{2,1,0:T(8,128)(2,1)S(1)} %get-tuple-element.18), channel_id=1, source_target_pairs={{0,1},{1,0},{2,3},{3,2},{4,5},{5,4},{6,7},{7,6},{8,9},{9,8},{10,11... | collective-permute-start | bytes 589832 | tf_op jit(solution)/shard_map/ppermute | solution.py:242
  46.3 11.2 %local_part.1.near_ref = f32[384,2560]{1,0:T(8,128)S(1)} custom-call(f32[20]{0:T(128)S(1)} %copy-done.8, s32[20]{0:T(128)S(1)} %copy-done.10, bf16[384,2560]{1,0:T(8,128)(2,1)S(1)} %copy-done, bf16[384,2560]{1,0:T(8,128)(2,1)S(1)} %copy-done.2, bf16[384,2560]{1,0:T(8,128)(2,1)S(1)} %copy-done.5), custom_call_target="tpu_custom_call" | custom-call | flops 1006632960 | bytes 9830400 | tf_op jit(solution)/shard_map/local_part/pallas_call | solution.py:112
  57.6 3.8 %finish.2._ = bf16[384,2560]{1,0:T(8,128)(2,1)} custom-call(s32[1]{0:T(128)} %bitcast.1.place, f32[20]{0:T(128)S(1)} %copy-done.8, s32[20]{0:T(128)S(1)} %copy-done.10, bf16[384,2560]{1,0:T(8,128)(2,1)S(1)} %copy-done, bf16[384,2560]{1,0:T(8,128)(2,1)S(1)} %copy-done.6, f32[384,2560]{1,0:T(8,128)S(1)} %local_part.1.near_ref, ...), custom_call_target="tpu_custom_call" | custom-call | tf_op jit(solution)/shard_map/finish/pallas_call | solution.py:173
  61.5 3.8 %finish.3 = bf16[384,2560]{1,0:T(8,128)(2,1)} custom-call(s32[1]{0:T(128)} %bitcast.place, f32[20]{0:T(128)S(1)} %copy-done.8, s32[20]{0:T(128)S(1)} %copy-done.10, bf16[384,2560]{1,0:T(8,128)(2,1)S(1)} %copy-done, bf16[384,2560]{1,0:T(8,128)(2,1)S(1)} %copy-done.6, f32[384,2560]{1,0:T(8,128)S(1)} %local_part.1.near_ref, ...), custom_call_target="tpu_custom_call", output_to_operand_aliasing={{}: (9, {})} | custom-call | tf_op jit(solution)/shard_map/finish/pallas_call | solution.py:173
  (39 shorter events, 0.4 us)
Async XLA Ops:
  0.0 1.5 %copy-start.1 = (bf16[384,2560]{1,0:T(8,128)(2,1)S(1)}, bf16[384,2560]{1,0:T(8,128)(2,1)}, u32[]{:S(2)}) copy-start(bf16[384,2560]{1,0:T(8,128)(2,1)} %k_ref.5) | copy-start | bytes 5898244
  1.5 1.5 %copy-start.3 = (bf16[384,2560]{1,0:T(8,128)(2,1)S(1)}, bf16[384,2560]{1,0:T(8,128)(2,1)}, u32[]{:S(2)}) copy-start(bf16[384,2560]{1,0:T(8,128)(2,1)} %v_ref.5) | copy-start | bytes 5898244
  3.1 0.7 %copy-start.7 = (f32[20]{0:T(128)S(1)}, f32[20]{0:T(128)}, u32[]{:S(2)}) copy-start(f32[20]{0:T(128)} %rates.9) | copy-start | bytes 244
  3.7 0.7 %copy-start.9 = (s32[20]{0:T(128)S(1)}, s32[20]{0:T(128)}, u32[]{:S(2)}) copy-start(s32[20]{0:T(128)} %reaches.9) | copy-start | bytes 244
  4.4 4.2 %copy-start.2 = (bf16[384,2560]{1,0:T(8,128)(2,1)S(1)}, bf16[384,2560]{1,0:T(8,128)(2,1)}, u32[]{:S(2)}) copy-start(bf16[384,2560]{1,0:T(8,128)(2,1)} %k_ref.5) | copy-start | bytes 5898244
  4.4 4.3 %copy-start.8 = (f32[20]{0:T(128)S(1)}, f32[20]{0:T(128)}, u32[]{:S(2)}) copy-start(f32[20]{0:T(128)} %rates.9) | copy-start | bytes 244
  4.4 4.3 %copy-start.10 = (s32[20]{0:T(128)S(1)}, s32[20]{0:T(128)}, u32[]{:S(2)}) copy-start(s32[20]{0:T(128)} %reaches.9) | copy-start | bytes 244
  6.7 6.7 %collective-permute-start = (bf16[10,128,128]{2,1,0:T(8,128)(2,1)}, bf16[10,128,128]{2,1,0:T(8,128)(2,1)}, u32[]{:S(2)}, u32[]{:S(2)}) collective-permute-start(bf16[10,128,128]{2,1,0:T(8,128)(2,1)} %get-tuple-element.10), channel_id=1, source_target_pairs={{0,1},{1,0},{2,3},{3,2},{4,5},{5,4},{6,7},{7,6},{8,9},{9,8},{10,11... | collective-permute-start | bytes 983048 | tf_op jit(solution)/shard_map/ppermute | solution.py:223
  7.4 50.2 %collective-permute-start.10 = (bf16[10,128,128]{2,1,0:T(8,128)(2,1)}, bf16[10,128,128]{2,1,0:T(8,128)(2,1)S(1)}, u32[]{:S(2)}, u32[]{:S(2)}) collective-permute-start(bf16[10,128,128]{2,1,0:T(8,128)(2,1)} %get-tuple-element.12), channel_id=1, source_target_pairs={{0,1},{1,4},{4,5},{5,8},{8,9},{9,12},{12,13},{2,3},{3,6},{6,7},{7,... | collective-permute-start | bytes 983048 | tf_op jit(solution)/shard_map/ppermute | solution.py:245
  8.7 1.5 %copy-start.4 = (bf16[384,2560]{1,0:T(8,128)(2,1)S(1)}, bf16[384,2560]{1,0:T(8,128)(2,1)}, u32[]{:S(2)}) copy-start(bf16[384,2560]{1,0:T(8,128)(2,1)} %v_ref.5) | copy-start | bytes 5898244
  11.8 49.6 %collective-permute-start.9 = (bf16[10,128,128]{2,1,0:T(8,128)(2,1)S(1)}, bf16[10,128,128]{2,1,0:T(8,128)(2,1)S(1)}, u32[]{:S(2)}, u32[]{:S(2)}) collective-permute-start(bf16[10,128,128]{2,1,0:T(8,128)(2,1)S(1)} %get-tuple-element.11), channel_id=1, source_target_pairs={{0,1},{1,4},{4,5},{5,8},{8,9},{9,12},{12,13},{2,3},{3,6},{6,7},{7,... | collective-permute-start | bytes 983048 | tf_op jit(solution)/shard_map/ppermute | solution.py:246
  14.6 8.7 %collective-permute-start.5 = (bf16[4,128,128]{2,1,0:T(8,128)(2,1)S(1)}, bf16[4,128,128]{2,1,0:T(8,128)(2,1)S(1)}, u32[]{:S(2)}, u32[]{:S(2)}) collective-permute-start(bf16[4,128,128]{2,1,0:T(8,128)(2,1)S(1)} %slice.41), channel_id=1, source_target_pairs={{0,4},{8,12},{1,5},{9,13},{2,6},{10,14},{3,7},{11,15},{16,20},{24,... | collective-permute-start | bytes 393224 | tf_op jit(solution)/shard_map/ppermute | solution.py:207
  15.9 9.7 %collective-permute-start.1 = (bf16[6,128,128]{2,1,0:T(8,128)(2,1)S(1)}, bf16[6,128,128]{2,1,0:T(8,128)(2,1)S(1)}, u32[]{:S(2)}, u32[]{:S(2)}) collective-permute-start(bf16[6,128,128]{2,1,0:T(8,128)(2,1)S(1)} %slice.40), channel_id=1, source_target_pairs={{0,4},{1,5},{2,6},{3,7},{16,20},{17,21},{18,22},{19,23}} | collective-permute-start | bytes 589832 | tf_op jit(solution)/shard_map/ppermute | solution.py:198
  23.2 23.1 %copy-start.5 = (bf16[384,2560]{1,0:T(8,128)(2,1)S(1)}, bf16[384,2560]{1,0:T(8,128)(2,1)}, u32[]{:S(2)}) copy-start(bf16[384,2560]{1,0:T(8,128)(2,1)} %v_ref.5) | copy-start | bytes 5898244
  23.4 23.0 %copy-start = (bf16[384,2560]{1,0:T(8,128)(2,1)S(1)}, bf16[384,2560]{1,0:T(8,128)(2,1)}, u32[]{:S(2)}) copy-start(bf16[384,2560]{1,0:T(8,128)(2,1)} %q_ref.5) | copy-start | bytes 5898244
  23.4 6.9 %collective-permute-start.7 = (bf16[4,128,128]{2,1,0:T(8,128)(2,1)S(1)}, bf16[4,128,128]{2,1,0:T(8,128)(2,1)S(1)}, u32[]{:S(2)}, u32[]{:S(2)}) collective-permute-start(bf16[4,128,128]{2,1,0:T(8,128)(2,1)S(1)} %fusion.7), channel_id=1, source_target_pairs={{4,12},{5,13},{6,14},{7,15},{20,28},{21,29},{22,30},{23,31}} | collective-permute-start | bytes 393224 | tf_op jit(solution)/shard_map/ppermute | solution.py:210
  24.9 5.3 %collective-permute-start.6 = (bf16[4,128,128]{2,1,0:T(8,128)(2,1)S(1)}, bf16[4,128,128]{2,1,0:T(8,128)(2,1)S(1)}, u32[]{:S(2)}, u32[]{:S(2)}) collective-permute-start(bf16[4,128,128]{2,1,0:T(8,128)(2,1)S(1)} %fusion.7), channel_id=1, source_target_pairs={{4,8},{5,9},{6,10},{7,11},{20,24},{21,25},{22,26},{23,27}} | collective-permute-start | bytes 393224 | tf_op jit(solution)/shard_map/ppermute | solution.py:209
  25.8 5.5 %collective-permute-start.2 = (bf16[6,128,128]{2,1,0:T(8,128)(2,1)S(1)}, bf16[6,128,128]{2,1,0:T(8,128)(2,1)S(1)}, u32[]{:S(2)}, u32[]{:S(2)}) collective-permute-start(bf16[6,128,128]{2,1,0:T(8,128)(2,1)S(1)} %fusion), channel_id=1, source_target_pairs={{4,8},{5,9},{6,10},{7,11},{20,24},{21,25},{22,26},{23,27}} | collective-permute-start | bytes 589832 | tf_op jit(solution)/shard_map/ppermute | solution.py:198
  31.4 11.2 %collective-permute-start.3 = (bf16[6,128,128]{2,1,0:T(8,128)(2,1)S(1)}, bf16[6,128,128]{2,1,0:T(8,128)(2,1)S(1)}, u32[]{:S(2)}, u32[]{:S(2)}) collective-permute-start(bf16[6,128,128]{2,1,0:T(8,128)(2,1)S(1)} %fusion.1), channel_id=1, source_target_pairs={{8,12},{9,13},{10,14},{11,15},{24,28},{25,29},{26,30},{27,31}} | collective-permute-start | bytes 589832 | tf_op jit(solution)/shard_map/ppermute | solution.py:198
  32.8 28.6 %collective-permute-start.8 = (bf16[4,128,128]{2,1,0:T(8,128)(2,1)S(1)}, bf16[4,128,128]{2,1,0:T(8,128)(2,1)S(1)}, u32[]{:S(2)}, u32[]{:S(2)}) collective-permute-start(bf16[4,128,128]{2,1,0:T(8,128)(2,1)S(1)} %fusion.10), channel_id=1, source_target_pairs={{0,1},{1,0},{2,3},{3,2},{4,5},{5,4},{6,7},{7,6},{8,9},{9,8},{10,11... | collective-permute-start | bytes 393224 | tf_op jit(solution)/shard_map/ppermute | solution.py:242
  43.8 13.7 %copy-start.11 = (f32[2560]{0:T(1024)S(1)}, f32[2560]{0:T(1024)}, u32[]{:S(2)}) copy-start(f32[2560]{0:T(1024)} %param.11) | copy-start | bytes 30724
  43.8 17.6 %collective-permute-start.4 = (bf16[6,128,128]{2,1,0:T(8,128)(2,1)S(1)}, bf16[6,128,128]{2,1,0:T(8,128)(2,1)S(1)}, u32[]{:S(2)}, u32[]{:S(2)}) collective-permute-start(bf16[6,128,128]{2,1,0:T(8,128)(2,1)S(1)} %get-tuple-element.18), channel_id=1, source_target_pairs={{0,1},{1,0},{2,3},{3,2},{4,5},{5,4},{6,7},{7,6},{8,9},{9,8},{10,11... | collective-permute-start | bytes 589832 | tf_op jit(solution)/shard_map/ppermute | solution.py:242
  46.3 11.3 %copy-start.6 = (bf16[384,2560]{1,0:T(8,128)(2,1)S(1)}, bf16[384,2560]{1,0:T(8,128)(2,1)}, u32[]{:S(2)}) copy-start(bf16[384,2560]{1,0:T(8,128)(2,1)} %g_ref.3) | copy-start | bytes 5898244

commit v2 on v1

v2 whole, which is shorter than its diff:
```python
import functools

import jax
import jax.numpy as jnp
from jax import lax
from jax.experimental import pallas as pl
from jax.experimental.pallas import tpu as pltpu
from jax.sharding import PartitionSpec as P

BLOCK = 128
REACH = 2
EPSILON = 1e-06
F32 = jnp.float32
BF16 = jnp.bfloat16
MIB = 1024 * 1024
CHUNK = 5
CUT = 6
TRANS = (((0,), (0,)), ((), ()))
ROWS = (((1,), (1,)), ((), ()))
ANY = pl.BlockSpec(memory_space=pl.ANY)
HERE = pl.BlockSpec(memory_space=pltpu.VMEM)
SMEM = pltpu.SMEM


def chunk_of(heads):
    return max(g for g in range(1, CHUNK + 1) if heads % g == 0)


def row_offsets():
    return lax.broadcasted_iota(jnp.int32, (BLOCK, BLOCK), 0).astype(F32)


def power(rate, tokens):
    return jnp.exp(jnp.full((1, BLOCK), -tokens, F32) * rate)


def span(head, heads):
    return pl.ds(pl.multiple_of(head * BLOCK, BLOCK), heads * BLOCK)


def columns(g, heads=1):
    return slice(g * BLOCK, (g + heads) * BLOCK)


def centred(rows):
    return rows - jnp.mean(rows, axis=-1, keepdims=True)


def fetch(source, target, sem):
    copy = pltpu.make_async_copy(source, target, sem)
    copy.start()
    return copy


def real_head(relative, count):
    rep = lax.axis_index("rep")
    return rep * count + relative if relative < count else (1 - rep) * count + (relative - count)


def states_kernel(
    rate_in, reach_in, k_in, v_in, own_ref, away_ref, second_ref, k_ref, v_ref, coef_ref,
    rates, reaches, sems,
):
    heads = second_ref.shape[0]
    count = heads // 2
    blocks = k_in.shape[0] // BLOCK
    chunk = chunk_of(count)
    small = [fetch(rate_in, rates, sems.at[0]), fetch(reach_in, reaches, sems.at[1])]
    loads = []
    for j in range(heads // chunk):
        where = span(real_head(j * chunk, count), chunk)
        here = columns(j * chunk, chunk)
        loads.append(fetch(k_in.at[:, where], k_ref.at[:, here], sems.at[2 + 2 * j]))
        loads.append(fetch(v_in.at[:, where], v_ref.at[:, here], sems.at[3 + 2 * j]))
    for copy in small:
        copy.wait()
    first = (lax.axis_index("rep") == 0).astype(F32)
    last = (lax.axis_index("ctx") == 3).astype(F32)
    for g in range(count):
        head = real_head(g, count)
        is_full = (reaches[head] > REACH).astype(F32)
        device = power(rates[head], blocks * BLOCK) * is_full
        chip = power(rates[head], 2 * blocks * BLOCK) * is_full
        one = jnp.ones_like(device)
        rows = [first * device + (1.0 - first), first + (1.0 - first) * device, chip, last * chip + (1.0 - last)]
        for i, row in enumerate(rows + [one * first, one * (1.0 - first)]):
            coef_ref[i, g] = row
    offsets = row_offsets() - float(BLOCK)
    for g in range(heads):
        if g % chunk == 0:
            loads[2 * (g // chunk)].wait()
            loads[2 * (g // chunk) + 1].wait()
        head = real_head(g, count)
        rate = rates[head]
        is_full = (reaches[head] > REACH).astype(F32)
        base = jnp.exp(offsets * rate)
        parts = []
        for t in range(blocks):
            faded = k_ref[t * BLOCK : (t + 1) * BLOCK, columns(g)].astype(F32) * base
            if t == blocks - 2:
                second = faded.astype(BF16)
            if t < blocks - 1:
                faded = faded * (power(rate, (blocks - 1 - t) * BLOCK) * is_full)
            parts.append(faded.astype(BF16))
        values = v_ref[:, columns(g)]
        carry = lax.dot_general(jnp.concatenate(parts, 0), values, TRANS, preferred_element_type=F32)
        carry = centred(carry).astype(BF16)
        if g < count:
            own_ref[g] = carry
        else:
            away_ref[g - count] = carry
        rows = values[(blocks - 2) * BLOCK : (blocks - 1) * BLOCK]
        state = lax.dot_general(second, rows, TRANS, preferred_element_type=F32)
        second_ref[g] = centred(state).astype(BF16)


def block_states(keys, values, rates, reaches):
    length, features = keys.shape
    heads = rates.shape[0]
    half = jax.ShapeDtypeStruct((heads // 2, BLOCK, BLOCK), BF16)
    rows = jax.ShapeDtypeStruct((length, features), BF16)
    coefs = jax.ShapeDtypeStruct((6, heads // 2, 1, BLOCK), F32)
    return pl.pallas_call(
        states_kernel,
        in_specs=[ANY] * 4,
        out_specs=[HERE] * 6,
        out_shape=[half, half, jax.ShapeDtypeStruct((heads, BLOCK, BLOCK), BF16), rows, rows, coefs],
        scratch_shapes=[
            SMEM(rates.shape, F32),
            SMEM(reaches.shape, jnp.int32),
            pltpu.SemaphoreType.DMA((2 + 2 * (heads // chunk_of(heads // 2)),)),
        ],
        compiler_params=pltpu.CompilerParams(vmem_limit_bytes=10 * MIB),
        name="block_states",
    )(rates, reaches, keys, values)


def local_kernel(
    start, rate_in, reach_in, gain_in, q_in, g_in, k_ref, v_ref, near_ref, faded_ref, second_ref, silu_ref,
    rates, reaches, gain, q_ref, g_ref, weights, sems,
):
    length = k_ref.shape[0]
    blocks = length // BLOCK
    count = near_ref.shape[1] // BLOCK
    half = k_ref.shape[1] // BLOCK // 2
    head0 = real_head(start, half)
    where = span(head0, count)
    small = [fetch(rate_in, rates, sems.at[0]), fetch(reach_in, reaches, sems.at[1])]
    load = fetch(q_in.at[:, where], q_ref, sems.at[3])
    gates = [fetch(g_in.at[:, where], g_ref, sems.at[4]), fetch(gain_in, gain, sems.at[2])]
    for copy in small:
        copy.wait()
    offsets = row_offsets()
    gap = offsets - lax.broadcasted_iota(jnp.int32, (BLOCK, BLOCK), 1).astype(F32)
    causal = gap >= 0
    load.wait()
    for g in range(count):
        rate = rates[head0 + g]
        reach = reaches[head0 + g]
        fading = jnp.exp(gap * (-rate))
        tables = [jnp.where(causal, fading, 0.0)]
        for back in range(1, blocks):
            tables.append(fading * (power(rate, back * BLOCK) * (reach >= back).astype(F32)))
        fade = jnp.exp(offsets * (-rate))
        is_second = jnp.logical_and(reach >= 2, reach <= REACH).astype(F32)
        for t in range(blocks):
            rows = slice(t * BLOCK, (t + 1) * BLOCK)
            queries = q_ref[rows, columns(g)]
            scores = lax.dot_general(
                queries, k_ref[: (t + 1) * BLOCK, columns(start + g)], ROWS, preferred_element_type=F32
            )
            for u in range(t + 1):
                tile = slice(u * BLOCK, (u + 1) * BLOCK)
                weights[g, rows, tile] = (scores[:, tile] * tables[t - u]).astype(BF16)
            faded = queries.astype(F32) * fade
            faded_ref[rows, columns(g)] = (faded * (power(rate, t * BLOCK) * (reach > t).astype(F32))).astype(BF16)
            if t == 0:
                second_ref[:, columns(g)] = (faded * (power(rate, BLOCK) * is_second)).astype(BF16)
    for g in range(count):
        for t in range(blocks):
            rows = slice(t * BLOCK, (t + 1) * BLOCK)
            near = jnp.dot(
                weights[g, rows, : (t + 1) * BLOCK],
                v_ref[: (t + 1) * BLOCK, columns(start + g)],
                preferred_element_type=F32,
            )
            near_ref[rows, columns(g)] = centred(near)
    for copy in gates:
        copy.wait()
    for g in range(count):
        gate = g_ref[:, columns(g)].astype(F32)
        silu_ref[:, columns(g)] = gate / (1.0 + jnp.exp(-gate)) * gain[pl.ds(head0 + g, 1), :]


def local_part(start, count, queries, gates, keys, values, gain, rates, reaches):
    length = keys.shape[0]
    width = count * BLOCK
    rows = jax.ShapeDtypeStruct((length, width), BF16)
    wide = jax.ShapeDtypeStruct((length, width), F32)
    return pl.pallas_call(
        functools.partial(local_kernel, start),
        in_specs=[ANY] * 5 + [HERE] * 2,
        out_specs=[HERE] * 4,
        out_shape=[wide, rows, jax.ShapeDtypeStruct((BLOCK, width), BF16), wide],
        scratch_shapes=[
            SMEM(rates.shape, F32),
            SMEM(reaches.shape, jnp.int32),
            pltpu.VMEM(gain.shape, F32),
            pltpu.VMEM((length, width), BF16),
            pltpu.VMEM((length, width), BF16),
            pltpu.VMEM((count, length, length), BF16),
            pltpu.SemaphoreType.DMA((5,)),
        ],
        compiler_params=pltpu.CompilerParams(vmem_limit_bytes=14 * MIB),
        cost_estimate=pl.CostEstimate(flops=1, bytes_accessed=1, transcendentals=0),
        name=f"local_{start}",
    )(rates, reaches, gain, queries, gates, keys, values)


def finish_kernel(mine, parts, *refs):
    locals_in, refs = refs[: 4 * parts], refs[4 * parts :]
    carry_ref, second_ref = refs[:2]
    out_ref, retained, rows_ref, sems = refs[-4:]
    count = carry_ref.shape[0]
    blocks = out_ref.shape[0] // BLOCK
    head0 = real_head(0 if mine else count, count)
    second0 = count if mine else 0
    stores = []
    start = 0
    for j in range(parts):
        near_ref, faded_ref, fsecond_ref, silu_ref = locals_in[4 * j : 4 * j + 4]
        heads = near_ref.shape[1] // BLOCK
        for g in range(heads):
            cols = columns(g)
            here = columns(start + g)
            far = jnp.dot(faded_ref[:, cols], carry_ref[start + g], preferred_element_type=F32)
            extra = jnp.dot(fsecond_ref[:, cols], second_ref[second0 + start + g], preferred_element_type=F32)
            retained[:BLOCK, here] = near_ref[:BLOCK, cols] + far[:BLOCK] + extra
            retained[BLOCK:, here] = near_ref[BLOCK:, cols] + far[BLOCK:]
        for g in range(heads):
            for t in range(blocks):
                rows = slice(t * BLOCK, (t + 1) * BLOCK)
                parted = retained[rows, columns(start + g)]
                variance = jnp.mean(parted * parted, axis=-1, keepdims=True)
                mixed_rows = silu_ref[rows, columns(g)] * (parted * lax.rsqrt(variance + EPSILON))
                rows_ref[rows, columns(start + g)] = mixed_rows.astype(BF16)
        here = columns(start, heads)
        stores.append(fetch(rows_ref.at[:, here], out_ref.at[:, span(head0 + start, heads)], sems.at[j]))
        start += heads
    for copy in stores:
        copy.wait()


def finish(parts, carry, second, into=None):
    mine = into is None
    length = parts[0][0].shape[0]
    count = carry.shape[0]
    width = count * BLOCK
    operands = [x for part in parts for x in part] + [carry, second] + ([] if mine else [into])
    return pl.pallas_call(
        functools.partial(finish_kernel, mine, len(parts)),
        in_specs=[HERE] * (4 * len(parts) + 2) + ([] if mine else [ANY]),
        out_specs=ANY,
        out_shape=jax.ShapeDtypeStruct((length, 2 * width), BF16),
        scratch_shapes=[
            pltpu.VMEM((length, width), F32),
            pltpu.VMEM((length, width), BF16),
            pltpu.SemaphoreType.DMA((len(parts),)),
        ],
        input_output_aliases={} if mine else {4 * len(parts) + 2: 0},
        compiler_params=pltpu.CompilerParams(vmem_limit_bytes=10 * MIB),
        name="finish_own" if mine else "finish_away",
    )(*operands)


def mixed(a, x, b, y):
    total = a * x.astype(F32) + b * y.astype(F32)
    return total.astype(BF16)


def after(value, *others):
    return lax.optimization_barrier((value, *others))[0]


def per_device(queries, key_vectors, value_vectors, gate_input, norm_gain, decay_rate, band_reach):
    length = queries.shape[0]
    half = decay_rate.shape[0] // 2
    chips = lax.axis_size("ctx")
    swap = [(0, 1), (1, 0)]
    steps = [(i, i + 1) for i in range(2 * chips - 1)]
    stay = functools.partial(pltpu.with_memory_space_constraint, memory_space=pltpu.HBM)
    keys, values, queries, gates = [stay(x) for x in (key_vectors, value_vectors, queries, gate_input)]
    rates, reaches, gain = stay(decay_rate), stay(band_reach), stay(norm_gain.reshape(-1, BLOCK))

    own, away, seconds, keys, values, coefs = block_states(keys, values, rates, reaches)
    from_pair = lax.ppermute(away, "rep", swap)
    few = half // 2
    local = lambda start, count, *others: local_part(
        start, count, after(queries, *others), gates, keys, values, gain, rates, reaches
    )
    own_parts = [local(0, few, own)]
    from_pair, _ = lax.optimization_barrier((from_pair, own_parts[0][0]))

    to_mine, to_pair, chip_fade, late_fade, is_first, is_last = [coefs[i] for i in range(6)]
    one = jnp.ones((1, 1, 1), F32)
    total = mixed(to_mine, own, to_pair, from_pair)

    cut = half * CUT // 10
    chain, pair = slice(0, cut), slice(cut, half)
    hop = lambda x, *pairs: lax.ppermute(x, "ctx", list(pairs))
    step = lambda part, got: mixed(chip_fade[part], got, one, total[part])
    b1 = hop(total[chain], (0, 1))
    if chips == 4:
        a1 = hop(total[pair], (0, 1), (2, 3))
        neighbour = lambda x, *pairs: lax.ppermute(x, ("ctx", "rep"), list(pairs))
        second_late = neighbour(after(seconds, total), (3, 4), (5, 6))
        b2 = hop(step(chain, b1), (1, 2))
        a1, second_late = lax.optimization_barrier((a1, second_late))
        t1 = step(pair, a1)
        second = neighbour(after(seconds, t1), (0, 1), (2, 3), (4, 5), (6, 7), (1, 2))
        away_parts = [local(half, few, t1)]
        near, far = hop(t1, (1, 2)), hop(t1, (1, 3))
        b2, _ = lax.optimization_barrier((b2, away_parts[0][0]))
        t2 = step(chain, b2)
        b3 = hop(t2, (2, 3))
        own_parts.append(local(few, half - few, t2))
        away_parts.append(local(half + few, half - few, t2, second))
        b3, near, far, _, _ = lax.optimization_barrier((b3, near, far, own_parts[1][0], away_parts[1][0]))
        second = second + second_late
        arrived_b = b1 + b2 + b3
        arrived_a = mixed(one, a1, late_fade[pair], near + far)
    else:
        a1 = hop(total[pair], (0, 1))
        second = lax.ppermute(seconds, ("ctx", "rep"), steps)
        own_parts.append(local(few, half - few, total))
        away_parts = [local(half, few, total)]
        arrived_a, arrived_b, got_a, got_b = a1, b1, a1, b1
        for i in range(1, chips - 1):
            got_a, got_b = hop(step(pair, got_a), (i, i + 1)), hop(step(chain, got_b), (i, i + 1))
            arrived_a, arrived_b = arrived_a + got_a, arrived_b + got_b
        away_parts.append(local(half + few, half - few))
    arrived = jnp.concatenate([arrived_b, arrived_a])
    sent = mixed(to_mine, arrived, is_first, own)
    kept = mixed(to_pair, arrived, is_last, from_pair)
    got = lax.ppermute(sent, "rep", swap)
    out = finish(own_parts, kept, second)
    return finish(away_parts, got, second, out)


def solution(mesh):
    rows = P(("group", "ctx", "rep"), "head")
    return jax.shard_map(
        per_device,
        mesh=mesh,
        in_specs=(rows, rows, rows, rows, P("head"), P("head"), P("head")),
        out_specs=rows,
        check_vma=False,
    )
```

time: 65.7 us -> 40.6 us (0.62)
  Pallas kernels: 22.6 us -> 15.7 us
  local copies, waits for them, and re-layouts: 6.08 us -> 0.04 us
  starting transfers between devices: 15.5 us -> 10 us
  waiting for transfers between devices: 16.7 us -> 13.3 us
  other arithmetic: 4.14 us -> 0.89 us
    pallas_call x5 -> x7, Pallas kernels: 22.6 us -> 15.7 us  [the longest x4 9.03 us: local_part(): pl.pallas_call(functools.partial(local_kernel, start), in_specs=[ANY] * 5...]
    unnamed x24 -> x3, local copies, waits for them, and re-layouts: 5.97 us -> 0.01 us
    ppermute x11 -> x10, starting transfers between devices: 15.5 us -> 10 us  [the longest x6 5.89 us: per_device(): hop = lambda x, *pairs: lax.ppermute(x, 'ctx', list(pairs))]
    ppermute x11 -> x10, waiting for transfers between devices: 16.7 us -> 13.3 us  [the longest x6 13.3 us: per_device(): hop = lambda x, *pairs: lax.ppermute(x, 'ctx', list(pairs))]
    convert_element_type x7 -> x6, other arithmetic: 3.84 us -> 0.66 us  [mixed(): return total.astype(BF16)]
  transfers between devices with their start and end apart: 11 -> 10, of which waited for: 3 -> 2; matrix products, arithmetic and copies ran while one was open for 7% -> 1% of each run, Pallas kernels for 25% -> 26%
where the time goes in v2:
time: 40.6 us; the launch traced here: 40.3 us
  Pallas kernels  15.7 us (39%)
  waiting for transfers between devices  13.3 us (33%)
  starting transfers between devices  10 us (25%)
  other arithmetic  0.89 us (2%)
    ppermute x6, waiting for transfers between devices, per_device(): hop = lambda x, *pairs: lax.ppermute(x, 'ctx', list(pairs))  13.3 us
    pallas_call x4, Pallas kernels, local_part(): pl.pallas_call(functools.partial(local_kernel, start), in_specs=[ANY] * 5...  9.03 us
    ppermute x6, starting transfers between devices, per_device(): hop = lambda x, *pairs: lax.ppermute(x, 'ctx', list(pairs))  5.89 us
    pallas_call x1, Pallas kernels, block_states(): pl.pallas_call(states_kernel, in_specs=[ANY] * 4, out_specs=[HERE] * 6, o...  3.41 us
    pallas_call x2, Pallas kernels, finish(): pl.pallas_call(functools.partial(finish_kernel, mine, len(parts)), in_spe...  3.29 us
    ppermute x2, starting transfers between devices, per_device(): neighbour = lambda x, *pairs: lax.ppermute(x, ('ctx', 'rep'), list(pairs))  1.99 us
    ppermute x1, starting transfers between devices, per_device(): got = lax.ppermute(sent, 'rep', swap)  1.38 us
  transfers between devices with their start and end apart: 10, of which 2 were waited for; matrix products, arithmetic and copies ran while one was open for 1% of the time, Pallas kernels for 26%

profile of v2, /device:TPU:25, one launch (start us, length us, event | category | flops | bytes accessed | tf_op | source)
XLA Modules:
  0.0 40.3 jit_solution(17200258201911422865)
XLA Ops:
  0.0 3.4 %block_states.1 = (bf16[10,128,128]{2,1,0:T(8,128)(2,1)S(1)}, bf16[10,128,128]{2,1,0:T(8,128)(2,1)S(1)}, bf16[20,128,128]{2,1,0:T(8,128)(2,1)S(1)}, bf16[384,256...) custom-call(f32[20]{0:T(128)} %rate_in.9, s32[20]{0:T(128)} %reach_in.9, ...), custom_call_target="tpu_custom_call" | custom-call | tf_op jit(solution)/shard_map/block_states/pallas_call | solution.py:123
  3.4 0.7 %collective-permute-start = (bf16[10,128,128]{2,1,0:T(8,128)(2,1)S(1)}, bf16[10,128,128]{2,1,0:T(8,128)(2,1)S(1)}, u32[]{:S(2)}, u32[]{:S(2)}) collective-permute-start(bf16[10,128,128]{2,1,0:T(8,128)(2,1)S(1)} %get-tuple-element.42), channel_id=1, source_target_pairs={{0,1},{1,0},{2,3},{3,2},{4,5},{5,4},{6,7},{7,6},{8,9},{9,8},{10,11... | collective-permute-start | bytes 983048 | tf_op jit(solution)/shard_map/ppermute | solution.py:296
  4.2 2.2 %local_0.1 = (f32[384,640]{1,0:T(8,128)S(1)}, bf16[384,640]{1,0:T(8,128)(2,1)S(1)}, bf16[128,640]{1,0:T(8,128)(2,1)S(1)}, f32[384,640]{1,0:T(8,128)S(1)}) custom-call(f32[20]{0:T(128)} %rate_in.9, s32[20]{0:T(128)} %reach_in.9, f32[20,128]{1,0:T(8,128)} %bitcast.14, bf16[384,2560]{1,0:T(8,128)(2,1)} %q_in.3, bf16[384,2560]{1,0:T(8,128)(2,1)} %g_in.7, ...), custom_call_target="tpu_custom_call" | custom-call | flops 1 | bytes 1 | tf_op jit(solution)/shard_map/local_0/pallas_call | solution.py:200
  6.4 0.0 collective-permute-done
  6.4 0.1 fusion.1
  6.6 0.7 %collective-permute-start.2 = (bf16[20,128,128]{2,1,0:T(8,128)(2,1)S(1)}, bf16[20,128,128]{2,1,0:T(8,128)(2,1)S(1)}, u32[]{:S(2)}, u32[]{:S(2)}) collective-permute-start(bf16[20,128,128]{2,1,0:T(8,128)(2,1)S(1)} %get-tuple-element.57), channel_id=1, source_target_pairs={{5,8},{9,12},{7,10},{11,14},{21,24},{25,28},{23,26},{27,30}} | collective-permute-start | bytes 1966088 | tf_op jit(solution)/shard_map/ppermute | solution.py:315
  7.3 0.7 %collective-permute-start.3 = (bf16[6,128,128]{2,1,0:T(8,128)(2,1)S(1)}, bf16[6,128,128]{2,1,0:T(8,128)(2,1)S(1)}, u32[]{:S(2)}, u32[]{:S(2)}) collective-permute-start(bf16[6,128,128]{2,1,0:T(8,128)(2,1)S(1)} %slice.49), channel_id=1, source_target_pairs={{0,4},{1,5},{2,6},{3,7},{16,20},{17,21},{18,22},{19,23}} | collective-permute-start | bytes 589832 | tf_op jit(solution)/shard_map/ppermute | solution.py:310
  8.0 1.3 %collective-permute-start.1 = (bf16[4,128,128]{2,1,0:T(8,128)(2,1)S(1)}, bf16[4,128,128]{2,1,0:T(8,128)(2,1)S(1)}, u32[]{:S(2)}, u32[]{:S(2)}) collective-permute-start(bf16[4,128,128]{2,1,0:T(8,128)(2,1)S(1)} %slice.48), channel_id=1, source_target_pairs={{0,4},{8,12},{1,5},{9,13},{2,6},{10,14},{3,7},{11,15},{16,20},{24,... | collective-permute-start | bytes 393224 | tf_op jit(solution)/shard_map/ppermute | solution.py:310
  9.3 0.0 collective-permute-done.3
  9.4 0.1 fusion.6
  9.4 0.7 %collective-permute-start.4 = (bf16[6,128,128]{2,1,0:T(8,128)(2,1)S(1)}, bf16[6,128,128]{2,1,0:T(8,128)(2,1)S(1)}, u32[]{:S(2)}, u32[]{:S(2)}) collective-permute-start(bf16[6,128,128]{2,1,0:T(8,128)(2,1)S(1)} %fusion.6), channel_id=1, source_target_pairs={{4,8},{5,9},{6,10},{7,11},{20,24},{21,25},{22,26},{23,27}} | collective-permute-start | bytes 589832 | tf_op jit(solution)/shard_map/ppermute | solution.py:310
  10.1 10.5 %collective-permute-done.1 = bf16[4,128,128]{2,1,0:T(8,128)(2,1)S(1)} collective-permute-done((bf16[4,128,128]{2,1,0:T(8,128)(2,1)S(1)}, bf16[4,128,128]{2,1,0:T(8,128)(2,1)S(1)}, u32[]{:S(2)}, u32[]{:S(2)}) %collective-permute-start.1) | collective-permute-done | bytes 131104 | tf_op jit(solution)/shard_map/ppermute | solution.py:310
  20.6 0.0 collective-permute-done.2
  20.7 1.3 %collective-permute-start.5 = (bf16[20,128,128]{2,1,0:T(8,128)(2,1)S(1)}, bf16[20,128,128]{2,1,0:T(8,128)(2,1)S(1)}, u32[]{:S(2)}, u32[]{:S(2)}) collective-permute-start(bf16[20,128,128]{2,1,0:T(8,128)(2,1)S(1)} %get-tuple-element.57), channel_id=1, source_target_pairs={{0,1},{4,5},{8,9},{12,13},{1,4},{2,3},{6,7},{10,11},{14,15},{3,6},... | collective-permute-start | bytes 1966088 | tf_op jit(solution)/shard_map/ppermute | solution.py:315
  22.0 0.7 %collective-permute-start.7 = (bf16[4,128,128]{2,1,0:T(8,128)(2,1)S(1)}, bf16[4,128,128]{2,1,0:T(8,128)(2,1)S(1)}, u32[]{:S(2)}, u32[]{:S(2)}) collective-permute-start(bf16[4,128,128]{2,1,0:T(8,128)(2,1)S(1)} %fusion.9), channel_id=1, source_target_pairs={{4,8},{5,9},{6,10},{7,11},{20,24},{21,25},{22,26},{23,27}} | collective-permute-start | bytes 393224 | tf_op jit(solution)/shard_map/ppermute | solution.py:310
  22.7 1.3 %collective-permute-start.8 = (bf16[4,128,128]{2,1,0:T(8,128)(2,1)S(1)}, bf16[4,128,128]{2,1,0:T(8,128)(2,1)S(1)}, u32[]{:S(2)}, u32[]{:S(2)}) collective-permute-start(bf16[4,128,128]{2,1,0:T(8,128)(2,1)S(1)} %fusion.9), channel_id=1, source_target_pairs={{4,12},{5,13},{6,14},{7,15},{20,28},{21,29},{22,30},{23,31}} | collective-permute-start | bytes 393224 | tf_op jit(solution)/shard_map/ppermute | solution.py:310
  24.0 2.3 %local_10.1 = (f32[384,640]{1,0:T(8,128)S(1)}, bf16[384,640]{1,0:T(8,128)(2,1)S(1)}, bf16[128,640]{1,0:T(8,128)(2,1)S(1)}, f32[384,640]{1,0:T(8,128)S(1)}) custom-call(f32[20]{0:T(128)} %rate_in.9, s32[20]{0:T(128)} %reach_in.9, f32[20,128]{1,0:T(8,128)} %bitcast.15, bf16[384,2560]{1,0:T(8,128)(2,1)} %q_in.3, bf16[384,2560]{1,0:T(8,128)(2,1)} %g_in.7, ...), custom_call_target="tpu_custom_call" | custom-call | flops 1 | bytes 1 | tf_op jit(solution)/shard_map/local_10/pallas_call | solution.py:200
  26.3 0.0 collective-permute-done.4
  26.3 0.1 fusion.7
  26.3 1.3 %collective-permute-start.6 = (bf16[6,128,128]{2,1,0:T(8,128)(2,1)S(1)}, bf16[6,128,128]{2,1,0:T(8,128)(2,1)S(1)}, u32[]{:S(2)}, u32[]{:S(2)}) collective-permute-start(bf16[6,128,128]{2,1,0:T(8,128)(2,1)S(1)} %fusion.7), channel_id=1, source_target_pairs={{8,12},{9,13},{10,14},{11,15},{24,28},{25,29},{26,30},{27,31}} | collective-permute-start | bytes 589832 | tf_op jit(solution)/shard_map/ppermute | solution.py:310
  27.7 2.3 %local_5.1 = (f32[384,640]{1,0:T(8,128)S(1)}, bf16[384,640]{1,0:T(8,128)(2,1)S(1)}, bf16[128,640]{1,0:T(8,128)(2,1)S(1)}, f32[384,640]{1,0:T(8,128)S(1)}) custom-call(f32[20]{0:T(128)} %rate_in.9, s32[20]{0:T(128)} %reach_in.9, f32[20,128]{1,0:T(8,128)} %bitcast.16, bf16[384,2560]{1,0:T(8,128)(2,1)} %q_in.3, bf16[384,2560]{1,0:T(8,128)(2,1)} %g_in.7, ...), custom_call_target="tpu_custom_call" | custom-call | flops 1 | bytes 1 | tf_op jit(solution)/shard_map/local_5/pallas_call | solution.py:200
  29.9 0.0 collective-permute-done.5
  29.9 2.3 %local_15.1 = (f32[384,640]{1,0:T(8,128)S(1)}, bf16[384,640]{1,0:T(8,128)(2,1)S(1)}, bf16[128,640]{1,0:T(8,128)(2,1)S(1)}, f32[384,640]{1,0:T(8,128)S(1)}) custom-call(f32[20]{0:T(128)} %rate_in.9, s32[20]{0:T(128)} %reach_in.9, f32[20,128]{1,0:T(8,128)} %bitcast.17, bf16[384,2560]{1,0:T(8,128)(2,1)} %q_in.3, bf16[384,2560]{1,0:T(8,128)(2,1)} %g_in.7, ...), custom_call_target="tpu_custom_call" | custom-call | flops 1 | bytes 1 | tf_op jit(solution)/shard_map/local_15/pallas_call | solution.py:200
  32.2 0.0 collective-permute-done.7
  32.2 0.0 collective-permute-done.8
  32.2 2.8 %collective-permute-done.6 = bf16[6,128,128]{2,1,0:T(8,128)(2,1)S(1)} collective-permute-done((bf16[6,128,128]{2,1,0:T(8,128)(2,1)S(1)}, bf16[6,128,128]{2,1,0:T(8,128)(2,1)S(1)}, u32[]{:S(2)}, u32[]{:S(2)}) %collective-permute-start.6) | collective-permute-done | bytes 196640 | tf_op jit(solution)/shard_map/ppermute | solution.py:310
  35.0 0.1 fusion.10
  35.1 0.3 fusion.5
  35.4 1.4 %collective-permute-start.9 = (bf16[10,128,128]{2,1,0:T(8,128)(2,1)S(1)}, bf16[10,128,128]{2,1,0:T(8,128)(2,1)S(1)}, u32[]{:S(2)}, u32[]{:S(2)}) collective-permute-start(bf16[10,128,128]{2,1,0:T(8,128)(2,1)S(1)} %get-tuple-element.76), channel_id=1, source_target_pairs={{0,1},{1,0},{2,3},{3,2},{4,5},{5,4},{6,7},{7,6},{8,9},{9,8},{10,11... | collective-permute-start | bytes 983048 | tf_op jit(solution)/shard_map/ppermute | solution.py:345
  36.8 0.2 add.42.refs_9_
  37.0 1.6 %finish_own.1.refs_10_ = bf16[384,2560]{1,0:T(8,128)(2,1)} custom-call(f32[384,640]{1,0:T(8,128)S(1)} %get-tuple-element.46.refs_0_, bf16[384,640]{1,0:T(8,128)(2,1)S(1)} %get-tuple-element.69.refs_1_, bf16[128,640]{1,0:T(8,128)(2,1)S(1)} %get-tuple-element.70.refs_2_, f32[384,640]{1,0:T(8,128)S(1)} %get-tuple-element.71.refs_3_, ...), custom_call_target="tpu_custom_call" | custom-call | tf_op jit(solution)/shard_map/finish_own/pallas_call | solution.py:260
  38.7 1.6 %finish_away.1 = bf16[384,2560]{1,0:T(8,128)(2,1)} custom-call(f32[384,640]{1,0:T(8,128)S(1)} %get-tuple-element.52.refs_0_, bf16[384,640]{1,0:T(8,128)(2,1)S(1)} %get-tuple-element.53.refs_1_, bf16[128,640]{1,0:T(8,128)(2,1)S(1)} %get-tuple-element.54.refs_2_, f32[384,640]{1,0:T(8,128)S(1)} %get-tuple-element.55.refs_3_, ...), custom_call_target="tpu_custom_call", output_to_operand_aliasing={{}: (10, {})} | custom-call | tf_op jit(solution)/shard_map/finish_away/pallas_call | solution.py:260
  (11 shorter events, 0.1 us)
Async XLA Ops:
  3.4 3.0 %collective-permute-start = (bf16[10,128,128]{2,1,0:T(8,128)(2,1)S(1)}, bf16[10,128,128]{2,1,0:T(8,128)(2,1)S(1)}, u32[]{:S(2)}, u32[]{:S(2)}) collective-permute-start(bf16[10,128,128]{2,1,0:T(8,128)(2,1)S(1)} %get-tuple-element.42), channel_id=1, source_target_pairs={{0,1},{1,0},{2,3},{3,2},{4,5},{5,4},{6,7},{7,6},{8,9},{9,8},{10,11... | collective-permute-start | bytes 983048 | tf_op jit(solution)/shard_map/ppermute | solution.py:296
  6.6 14.1 %collective-permute-start.2 = (bf16[20,128,128]{2,1,0:T(8,128)(2,1)S(1)}, bf16[20,128,128]{2,1,0:T(8,128)(2,1)S(1)}, u32[]{:S(2)}, u32[]{:S(2)}) collective-permute-start(bf16[20,128,128]{2,1,0:T(8,128)(2,1)S(1)} %get-tuple-element.57), channel_id=1, source_target_pairs={{5,8},{9,12},{7,10},{11,14},{21,24},{25,28},{23,26},{27,30}} | collective-permute-start | bytes 1966088 | tf_op jit(solution)/shard_map/ppermute | solution.py:315
  7.3 2.0 %collective-permute-start.3 = (bf16[6,128,128]{2,1,0:T(8,128)(2,1)S(1)}, bf16[6,128,128]{2,1,0:T(8,128)(2,1)S(1)}, u32[]{:S(2)}, u32[]{:S(2)}) collective-permute-start(bf16[6,128,128]{2,1,0:T(8,128)(2,1)S(1)} %slice.49), channel_id=1, source_target_pairs={{0,4},{1,5},{2,6},{3,7},{16,20},{17,21},{18,22},{19,23}} | collective-permute-start | bytes 589832 | tf_op jit(solution)/shard_map/ppermute | solution.py:310
  8.0 12.6 %collective-permute-start.1 = (bf16[4,128,128]{2,1,0:T(8,128)(2,1)S(1)}, bf16[4,128,128]{2,1,0:T(8,128)(2,1)S(1)}, u32[]{:S(2)}, u32[]{:S(2)}) collective-permute-start(bf16[4,128,128]{2,1,0:T(8,128)(2,1)S(1)} %slice.48), channel_id=1, source_target_pairs={{0,4},{8,12},{1,5},{9,13},{2,6},{10,14},{3,7},{11,15},{16,20},{24,... | collective-permute-start | bytes 393224 | tf_op jit(solution)/shard_map/ppermute | solution.py:310
  9.4 16.8 %collective-permute-start.4 = (bf16[6,128,128]{2,1,0:T(8,128)(2,1)S(1)}, bf16[6,128,128]{2,1,0:T(8,128)(2,1)S(1)}, u32[]{:S(2)}, u32[]{:S(2)}) collective-permute-start(bf16[6,128,128]{2,1,0:T(8,128)(2,1)S(1)} %fusion.6), channel_id=1, source_target_pairs={{4,8},{5,9},{6,10},{7,11},{20,24},{21,25},{22,26},{23,27}} | collective-permute-start | bytes 589832 | tf_op jit(solution)/shard_map/ppermute | solution.py:310
  20.7 9.2 %collective-permute-start.5 = (bf16[20,128,128]{2,1,0:T(8,128)(2,1)S(1)}, bf16[20,128,128]{2,1,0:T(8,128)(2,1)S(1)}, u32[]{:S(2)}, u32[]{:S(2)}) collective-permute-start(bf16[20,128,128]{2,1,0:T(8,128)(2,1)S(1)} %get-tuple-element.57), channel_id=1, source_target_pairs={{0,1},{4,5},{8,9},{12,13},{1,4},{2,3},{6,7},{10,11},{14,15},{3,6},... | collective-permute-start | bytes 1966088 | tf_op jit(solution)/shard_map/ppermute | solution.py:315
  22.0 10.2 %collective-permute-start.7 = (bf16[4,128,128]{2,1,0:T(8,128)(2,1)S(1)}, bf16[4,128,128]{2,1,0:T(8,128)(2,1)S(1)}, u32[]{:S(2)}, u32[]{:S(2)}) collective-permute-start(bf16[4,128,128]{2,1,0:T(8,128)(2,1)S(1)} %fusion.9), channel_id=1, source_target_pairs={{4,8},{5,9},{6,10},{7,11},{20,24},{21,25},{22,26},{23,27}} | collective-permute-start | bytes 393224 | tf_op jit(solution)/shard_map/ppermute | solution.py:310
  22.7 9.5 %collective-permute-start.8 = (bf16[4,128,128]{2,1,0:T(8,128)(2,1)S(1)}, bf16[4,128,128]{2,1,0:T(8,128)(2,1)S(1)}, u32[]{:S(2)}, u32[]{:S(2)}) collective-permute-start(bf16[4,128,128]{2,1,0:T(8,128)(2,1)S(1)} %fusion.9), channel_id=1, source_target_pairs={{4,12},{5,13},{6,14},{7,15},{20,28},{21,29},{22,30},{23,31}} | collective-permute-start | bytes 393224 | tf_op jit(solution)/shard_map/ppermute | solution.py:310
  26.3 8.7 %collective-permute-start.6 = (bf16[6,128,128]{2,1,0:T(8,128)(2,1)S(1)}, bf16[6,128,128]{2,1,0:T(8,128)(2,1)S(1)}, u32[]{:S(2)}, u32[]{:S(2)}) collective-permute-start(bf16[6,128,128]{2,1,0:T(8,128)(2,1)S(1)} %fusion.7), channel_id=1, source_target_pairs={{8,12},{9,13},{10,14},{11,15},{24,28},{25,29},{26,30},{27,31}} | collective-permute-start | bytes 589832 | tf_op jit(solution)/shard_map/ppermute | solution.py:310
  35.4 3.2 %collective-permute-start.9 = (bf16[10,128,128]{2,1,0:T(8,128)(2,1)S(1)}, bf16[10,128,128]{2,1,0:T(8,128)(2,1)S(1)}, u32[]{:S(2)}, u32[]{:S(2)}) collective-permute-start(bf16[10,128,128]{2,1,0:T(8,128)(2,1)S(1)} %get-tuple-element.76), channel_id=1, source_target_pairs={{0,1},{1,0},{2,3},{3,2},{4,5},{5,4},{6,7},{7,6},{8,9},{9,8},{10,11... | collective-permute-start | bytes 983048 | tf_op jit(solution)/shard_map/ppermute | solution.py:345

commit v3 on v2

--- a/solution.py
+++ b/solution.py
@@ -14,7 +14,7 @@
 BF16 = jnp.bfloat16
 MIB = 1024 * 1024
 CHUNK = 5
-CUT = 6
+CUT = 5
 TRANS = (((0,), (0,)), ((), ()))
 ROWS = (((1,), (1,)), ((), ()))
 ANY = pl.BlockSpec(memory_space=pl.ANY)
@@ -75,14 +75,13 @@
     for copy in small:
         copy.wait()
     first = (lax.axis_index("rep") == 0).astype(F32)
-    last = (lax.axis_index("ctx") == 3).astype(F32)
     for g in range(count):
         head = real_head(g, count)
         is_full = (reaches[head] > REACH).astype(F32)
         device = power(rates[head], blocks * BLOCK) * is_full
         chip = power(rates[head], 2 * blocks * BLOCK) * is_full
         one = jnp.ones_like(device)
-        rows = [first * device + (1.0 - first), first + (1.0 - first) * device, chip, last * chip + (1.0 - last)]
+        rows = [first * device + (1.0 - first), first + (1.0 - first) * device, chip]
         for i, row in enumerate(rows + [one * first, one * (1.0 - first)]):
             coef_ref[i, g] = row
     offsets = row_offsets() - float(BLOCK)
@@ -119,7 +118,7 @@
     heads = rates.shape[0]
     half = jax.ShapeDtypeStruct((heads // 2, BLOCK, BLOCK), BF16)
     rows = jax.ShapeDtypeStruct((length, features), BF16)
-    coefs = jax.ShapeDtypeStruct((6, heads // 2, 1, BLOCK), F32)
+    coefs = jax.ShapeDtypeStruct((5, heads // 2, 1, BLOCK), F32)
     return pl.pallas_call(
         states_kernel,
         in_specs=[ANY] * 4,
@@ -295,48 +294,49 @@
     own, away, seconds, keys, values, coefs = block_states(keys, values, rates, reaches)
     from_pair = lax.ppermute(away, "rep", swap)
     few = half // 2
+    neighbour = lambda x, *pairs: lax.ppermute(x, ("ctx", "rep"), list(pairs))
     local = lambda start, count, *others: local_part(
         start, count, after(queries, *others), gates, keys, values, gain, rates, reaches
     )
-    own_parts = [local(0, few, own)]
-    from_pair, _ = lax.optimization_barrier((from_pair, own_parts[0][0]))
-
-    to_mine, to_pair, chip_fade, late_fade, is_first, is_last = [coefs[i] for i in range(6)]
+    to_mine, to_pair, chip_fade, is_first, is_last = [coefs[i] for i in range(5)]
     one = jnp.ones((1, 1, 1), F32)
     total = mixed(to_mine, own, to_pair, from_pair)
 
     cut = half * CUT // 10
-    chain, pair = slice(0, cut), slice(cut, half)
-    hop = lambda x, *pairs: lax.ppermute(x, "ctx", list(pairs))
+    chain, tail = slice(0, cut), slice(cut, half)
+    hop = lambda x, i: lax.ppermute(x, "ctx", [(i, i + 1)])
     step = lambda part, got: mixed(chip_fade[part], got, one, total[part])
-    b1 = hop(total[chain], (0, 1))
+    b1 = hop(total[chain], 0)
     if chips == 4:
-        a1 = hop(total[pair], (0, 1), (2, 3))
-        neighbour = lambda x, *pairs: lax.ppermute(x, ("ctx", "rep"), list(pairs))
-        second_late = neighbour(after(seconds, total), (3, 4), (5, 6))
-        b2 = hop(step(chain, b1), (1, 2))
-        a1, second_late = lax.optimization_barrier((a1, second_late))
-        t1 = step(pair, a1)
-        second = neighbour(after(seconds, t1), (0, 1), (2, 3), (4, 5), (6, 7), (1, 2))
-        away_parts = [local(half, few, t1)]
-        near, far = hop(t1, (1, 2)), hop(t1, (1, 3))
+        a1 = hop(total[tail], 0)
+        second = neighbour(after(seconds, total), (0, 1), (2, 3), (4, 5), (6, 7), (1, 2), (5, 6))
+        t1 = step(chain, b1)
+        b2 = hop(t1, 1)
+        own_parts = [local(0, few, t1)]
+        a1, _ = lax.optimization_barrier((a1, own_parts[0][0]))
+        u1 = step(tail, a1)
+        a2 = hop(u1, 1)
+        second_late = neighbour(after(seconds, u1), (3, 4))
+        away_parts = [local(half, few, u1)]
         b2, _ = lax.optimization_barrier((b2, away_parts[0][0]))
         t2 = step(chain, b2)
-        b3 = hop(t2, (2, 3))
+        b3 = hop(t2, 2)
         own_parts.append(local(few, half - few, t2))
-        away_parts.append(local(half + few, half - few, t2, second))
-        b3, near, far, _, _ = lax.optimization_barrier((b3, near, far, own_parts[1][0], away_parts[1][0]))
+        a2, _ = lax.optimization_barrier((a2, own_parts[1][0]))
+        u2 = step(tail, a2)
+        a3 = hop(u2, 2)
+        away_parts.append(local(half + few, half - few, u2, second))
+        a3, b3, second_late, _ = lax.optimization_barrier((a3, b3, second_late, away_parts[1][0]))
         second = second + second_late
-        arrived_b = b1 + b2 + b3
-        arrived_a = mixed(one, a1, late_fade[pair], near + far)
+        arrived_a, arrived_b = a1 + a2 + a3, b1 + b2 + b3
     else:
-        a1 = hop(total[pair], (0, 1))
+        a1 = hop(total[tail], 0)
         second = lax.ppermute(seconds, ("ctx", "rep"), steps)
-        own_parts.append(local(few, half - few, total))
+        own_parts = [local(0, few), local(few, half - few, total)]
         away_parts = [local(half, few, total)]
         arrived_a, arrived_b, got_a, got_b = a1, b1, a1, b1
         for i in range(1, chips - 1):
-            got_a, got_b = hop(step(pair, got_a), (i, i + 1)), hop(step(chain, got_b), (i, i + 1))
+            got_a, got_b = hop(step(tail, got_a), i), hop(step(chain, got_b), i)
             arrived_a, arrived_b = arrived_a + got_a, arrived_b + got_b
         away_parts.append(local(half + few, half - few))
     arrived = jnp.concatenate([arrived_b, arrived_a])

time: 40.6 us -> 34.8 us (0.86)
  waiting for transfers between devices: 13.3 us -> 5.27 us
  starting transfers between devices: 10 us -> 12.3 us
    ppermute x6, waiting for transfers between devices: 13.3 us -> 4.01 us  [per_device(): hop = lambda x, i: lax.ppermute(x, 'ctx', [(i, i + 1)])]
    ppermute x1, starting transfers between devices: 1.38 us -> 4.25 us  [per_device(): got = lax.ppermute(sent, 'rep', swap)]
    ppermute x1, waiting for transfers between devices: 0.01 us -> 1.25 us  [per_device(): from_pair = lax.ppermute(away, 'rep', swap)]
    ppermute x6, starting transfers between devices: 5.89 us -> 5.27 us  [per_device(): hop = lambda x, i: lax.ppermute(x, 'ctx', [(i, i + 1)])]
  transfers between devices with their start and end apart: 10 -> 10, of which waited for: 2 -> 3; matrix products, arithmetic and copies ran while one was open for 1% -> 1% of each run, Pallas kernels for 26% -> 31%
where the time goes in v3:
time: 34.8 us; the launch traced here: 34.5 us
  Pallas kernels  15.7 us (45%)
  starting transfers between devices  12.3 us (35%)
  waiting for transfers between devices  5.27 us (15%)
  other arithmetic  0.9 us (3%)
    pallas_call x4, Pallas kernels, local_part(): pl.pallas_call(functools.partial(local_kernel, start), in_specs=[ANY] * 5...  9.04 us
    ppermute x6, starting transfers between devices, per_device(): hop = lambda x, i: lax.ppermute(x, 'ctx', [(i, i + 1)])  5.27 us
    ppermute x1, starting transfers between devices, per_device(): got = lax.ppermute(sent, 'rep', swap)  4.25 us
    ppermute x6, waiting for transfers between devices, per_device(): hop = lambda x, i: lax.ppermute(x, 'ctx', [(i, i + 1)])  4.01 us
    pallas_call x1, Pallas kernels, block_states(): pl.pallas_call(states_kernel, in_specs=[ANY] * 4, out_specs=[HERE] * 6, o...  3.41 us
    pallas_call x2, Pallas kernels, finish(): pl.pallas_call(functools.partial(finish_kernel, mine, len(parts)), in_spe...  3.3 us
    ppermute x2, starting transfers between devices, per_device(): neighbour = lambda x, *pairs: lax.ppermute(x, ('ctx', 'rep'), list(pairs))  1.99 us
    ppermute x1, waiting for transfers between devices, per_device(): from_pair = lax.ppermute(away, 'rep', swap)  1.25 us
  transfers between devices with their start and end apart: 10, of which 3 were waited for; matrix products, arithmetic and copies ran while one was open for 1% of the time, Pallas kernels for 31%

profile of v3, /device:TPU:25, one launch (start us, length us, event | category | flops | bytes accessed | tf_op | source)
XLA Modules:
  0.0 34.5 jit_solution(1379886631125756809)
XLA Ops:
  0.0 3.4 %block_states.1 = (bf16[10,128,128]{2,1,0:T(8,128)(2,1)S(1)}, bf16[10,128,128]{2,1,0:T(8,128)(2,1)S(1)}, bf16[20,128,128]{2,1,0:T(8,128)(2,1)S(1)}, bf16[384,256...) custom-call(f32[20]{0:T(128)} %rate_in.9, s32[20]{0:T(128)} %reach_in.9, ...), custom_call_target="tpu_custom_call" | custom-call | tf_op jit(solution)/shard_map/block_states/pallas_call | solution.py:122
  3.4 0.7 %collective-permute-start = (bf16[10,128,128]{2,1,0:T(8,128)(2,1)S(1)}, bf16[10,128,128]{2,1,0:T(8,128)(2,1)S(1)}, u32[]{:S(2)}, u32[]{:S(2)}) collective-permute-start(bf16[10,128,128]{2,1,0:T(8,128)(2,1)S(1)} %get-tuple-element.41), channel_id=1, source_target_pairs={{0,1},{1,0},{2,3},{3,2},{4,5},{5,4},{6,7},{7,6},{8,9},{9,8},{10,11... | collective-permute-start | bytes 983048 | tf_op jit(solution)/shard_map/ppermute | solution.py:295
  4.2 1.2 %collective-permute-done = bf16[10,128,128]{2,1,0:T(8,128)(2,1)S(1)} collective-permute-done((bf16[10,128,128]{2,1,0:T(8,128)(2,1)S(1)}, bf16[10,128,128]{2,1,0:T(8,128)(2,1)S(1)}, u32[]{:S(2)}, u32[]{:S(2)}) %collective-permute-start) | collective-permute-done | bytes 327712 | tf_op jit(solution)/shard_map/ppermute | solution.py:295
  5.4 0.1 fusion.1
  5.6 0.7 %collective-permute-start.2 = (bf16[5,128,128]{2,1,0:T(8,128)(2,1)S(1)}, bf16[5,128,128]{2,1,0:T(8,128)(2,1)S(1)}, u32[]{:S(2)}, u32[]{:S(2)}) collective-permute-start(bf16[5,128,128]{2,1,0:T(8,128)(2,1)S(1)} %get-tuple-element.75), channel_id=1, source_target_pairs={{0,4},{1,5},{2,6},{3,7},{16,20},{17,21},{18,22},{19,23}} | collective-permute-start | bytes 491528 | tf_op jit(solution)/shard_map/ppermute | solution.py:307
  6.3 0.7 %collective-permute-start.1 = (bf16[5,128,128]{2,1,0:T(8,128)(2,1)S(1)}, bf16[5,128,128]{2,1,0:T(8,128)(2,1)S(1)}, u32[]{:S(2)}, u32[]{:S(2)}) collective-permute-start(bf16[5,128,128]{2,1,0:T(8,128)(2,1)S(1)} %get-tuple-element.76), channel_id=1, source_target_pairs={{0,4},{1,5},{2,6},{3,7},{16,20},{17,21},{18,22},{19,23}} | collective-permute-start | bytes 491528 | tf_op jit(solution)/shard_map/ppermute | solution.py:307
  7.0 1.3 %collective-permute-start.5 = (bf16[20,128,128]{2,1,0:T(8,128)(2,1)S(1)}, bf16[20,128,128]{2,1,0:T(8,128)(2,1)S(1)}, u32[]{:S(2)}, u32[]{:S(2)}) collective-permute-start(bf16[20,128,128]{2,1,0:T(8,128)(2,1)S(1)} %get-tuple-element.63), channel_id=1, source_target_pairs={{0,1},{4,5},{8,9},{12,13},{1,4},{9,12},{2,3},{6,7},{10,11},{14,15}... | collective-permute-start | bytes 1966088 | tf_op jit(solution)/shard_map/ppermute | solution.py:297
  8.3 0.0 collective-permute-done.2
  8.3 0.1 fusion.6
  8.4 0.7 %collective-permute-start.4 = (bf16[5,128,128]{2,1,0:T(8,128)(2,1)S(1)}, bf16[5,128,128]{2,1,0:T(8,128)(2,1)S(1)}, u32[]{:S(2)}, u32[]{:S(2)}) collective-permute-start(bf16[5,128,128]{2,1,0:T(8,128)(2,1)S(1)} %fusion.6), channel_id=1, source_target_pairs={{4,8},{5,9},{6,10},{7,11},{20,24},{21,25},{22,26},{23,27}} | collective-permute-start | bytes 491528 | tf_op jit(solution)/shard_map/ppermute | solution.py:307
  9.0 2.3 %local_0.1 = (f32[384,640]{1,0:T(8,128)S(1)}, bf16[384,640]{1,0:T(8,128)(2,1)S(1)}, bf16[128,640]{1,0:T(8,128)(2,1)S(1)}, f32[384,640]{1,0:T(8,128)S(1)}) custom-call(f32[20]{0:T(128)} %rate_in.9, s32[20]{0:T(128)} %reach_in.9, f32[20,128]{1,0:T(8,128)} %bitcast.15, bf16[384,2560]{1,0:T(8,128)(2,1)} %q_in.3, bf16[384,2560]{1,0:T(8,128)(2,1)} %g_in.7, ...), custom_call_target="tpu_custom_call" | custom-call | flops 1 | bytes 1 | tf_op jit(solution)/shard_map/local_0/pallas_call | solution.py:199
  11.3 0.0 collective-permute-done.1
  11.3 0.1 fusion.8
  11.4 0.7 %collective-permute-start.3 = (bf16[5,128,128]{2,1,0:T(8,128)(2,1)S(1)}, bf16[5,128,128]{2,1,0:T(8,128)(2,1)S(1)}, u32[]{:S(2)}, u32[]{:S(2)}) collective-permute-start(bf16[5,128,128]{2,1,0:T(8,128)(2,1)S(1)} %fusion.8), channel_id=1, source_target_pairs={{4,8},{5,9},{6,10},{7,11},{20,24},{21,25},{22,26},{23,27}} | collective-permute-start | bytes 491528 | tf_op jit(solution)/shard_map/ppermute | solution.py:307
  12.1 0.7 %collective-permute-start.8 = (bf16[20,128,128]{2,1,0:T(8,128)(2,1)S(1)}, bf16[20,128,128]{2,1,0:T(8,128)(2,1)S(1)}, u32[]{:S(2)}, u32[]{:S(2)}) collective-permute-start(bf16[20,128,128]{2,1,0:T(8,128)(2,1)S(1)} %get-tuple-element.63), channel_id=1, source_target_pairs={{5,8},{7,10},{21,24},{23,26}} | collective-permute-start | bytes 1966088 | tf_op jit(solution)/shard_map/ppermute | solution.py:297
  12.8 2.3 %local_10.1 = (f32[384,640]{1,0:T(8,128)S(1)}, bf16[384,640]{1,0:T(8,128)(2,1)S(1)}, bf16[128,640]{1,0:T(8,128)(2,1)S(1)}, f32[384,640]{1,0:T(8,128)S(1)}) custom-call(f32[20]{0:T(128)} %rate_in.9, s32[20]{0:T(128)} %reach_in.9, f32[20,128]{1,0:T(8,128)} %bitcast.16, bf16[384,2560]{1,0:T(8,128)(2,1)} %q_in.3, bf16[384,2560]{1,0:T(8,128)(2,1)} %g_in.7, ...), custom_call_target="tpu_custom_call" | custom-call | flops 1 | bytes 1 | tf_op jit(solution)/shard_map/local_10/pallas_call | solution.py:199
  15.0 0.0 collective-permute-done.4
  15.0 0.1 fusion.7
  15.1 1.3 %collective-permute-start.7 = (bf16[5,128,128]{2,1,0:T(8,128)(2,1)S(1)}, bf16[5,128,128]{2,1,0:T(8,128)(2,1)S(1)}, u32[]{:S(2)}, u32[]{:S(2)}) collective-permute-start(bf16[5,128,128]{2,1,0:T(8,128)(2,1)S(1)} %fusion.7), channel_id=1, source_target_pairs={{8,12},{9,13},{10,14},{11,15},{24,28},{25,29},{26,30},{27,31}} | collective-permute-start | bytes 491528 | tf_op jit(solution)/shard_map/ppermute | solution.py:307
  16.4 2.3 %local_5.1 = (f32[384,640]{1,0:T(8,128)S(1)}, bf16[384,640]{1,0:T(8,128)(2,1)S(1)}, bf16[128,640]{1,0:T(8,128)(2,1)S(1)}, f32[384,640]{1,0:T(8,128)S(1)}) custom-call(f32[20]{0:T(128)} %rate_in.9, s32[20]{0:T(128)} %reach_in.9, f32[20,128]{1,0:T(8,128)} %bitcast.17, bf16[384,2560]{1,0:T(8,128)(2,1)} %q_in.3, bf16[384,2560]{1,0:T(8,128)(2,1)} %g_in.7, ...), custom_call_target="tpu_custom_call" | custom-call | flops 1 | bytes 1 | tf_op jit(solution)/shard_map/local_5/pallas_call | solution.py:199
  18.7 0.1 fusion.9
  18.8 1.3 %collective-permute-start.6 = (bf16[5,128,128]{2,1,0:T(8,128)(2,1)S(1)}, bf16[5,128,128]{2,1,0:T(8,128)(2,1)S(1)}, u32[]{:S(2)}, u32[]{:S(2)}) collective-permute-start(bf16[5,128,128]{2,1,0:T(8,128)(2,1)S(1)} %fusion.9), channel_id=1, source_target_pairs={{8,12},{9,13},{10,14},{11,15},{24,28},{25,29},{26,30},{27,31}} | collective-permute-start | bytes 491528 | tf_op jit(solution)/shard_map/ppermute | solution.py:307
  20.1 0.0 collective-permute-done.5
  20.1 2.3 %local_15.1 = (f32[384,640]{1,0:T(8,128)S(1)}, bf16[384,640]{1,0:T(8,128)(2,1)S(1)}, bf16[128,640]{1,0:T(8,128)(2,1)S(1)}, f32[384,640]{1,0:T(8,128)S(1)}) custom-call(f32[20]{0:T(128)} %rate_in.9, s32[20]{0:T(128)} %reach_in.9, f32[20,128]{1,0:T(8,128)} %bitcast.18, bf16[384,2560]{1,0:T(8,128)(2,1)} %q_in.3, bf16[384,2560]{1,0:T(8,128)(2,1)} %g_in.7, ...), custom_call_target="tpu_custom_call" | custom-call | flops 1 | bytes 1 | tf_op jit(solution)/shard_map/local_15/pallas_call | solution.py:199
  22.3 0.3 collective-permute-done.7
  22.7 3.7 %collective-permute-done.6 = bf16[5,128,128]{2,1,0:T(8,128)(2,1)S(1)} collective-permute-done((bf16[5,128,128]{2,1,0:T(8,128)(2,1)S(1)}, bf16[5,128,128]{2,1,0:T(8,128)(2,1)S(1)}, u32[]{:S(2)}, u32[]{:S(2)}) %collective-permute-start.6) | collective-permute-done | bytes 163872 | tf_op jit(solution)/shard_map/ppermute | solution.py:307
  26.4 0.3 fusion.5
  26.7 4.2 %collective-permute-start.9 = (bf16[10,128,128]{2,1,0:T(8,128)(2,1)S(1)}, bf16[10,128,128]{2,1,0:T(8,128)(2,1)S(1)}, u32[]{:S(2)}, u32[]{:S(2)}) collective-permute-start(bf16[10,128,128]{2,1,0:T(8,128)(2,1)S(1)} %get-tuple-element.74), channel_id=1, source_target_pairs={{0,1},{1,0},{2,3},{3,2},{4,5},{5,4},{6,7},{7,6},{8,9},{9,8},{10,11... | collective-permute-start | bytes 983048 | tf_op jit(solution)/shard_map/ppermute | solution.py:345
  30.9 0.2 add.46.refs_9_
  31.2 1.7 %finish_own.1.refs_10_ = bf16[384,2560]{1,0:T(8,128)(2,1)} custom-call(f32[384,640]{1,0:T(8,128)S(1)} %get-tuple-element.45.refs_0_, bf16[384,640]{1,0:T(8,128)(2,1)S(1)} %get-tuple-element.67.refs_1_, bf16[128,640]{1,0:T(8,128)(2,1)S(1)} %get-tuple-element.68.refs_2_, f32[384,640]{1,0:T(8,128)S(1)} %get-tuple-element.69.refs_3_, ...), custom_call_target="tpu_custom_call" | custom-call | tf_op jit(solution)/shard_map/finish_own/pallas_call | solution.py:259
  32.8 0.0 collective-permute-done.9.refs_8_
  32.8 1.6 %finish_away.1 = bf16[384,2560]{1,0:T(8,128)(2,1)} custom-call(f32[384,640]{1,0:T(8,128)S(1)} %get-tuple-element.48.refs_0_, bf16[384,640]{1,0:T(8,128)(2,1)S(1)} %get-tuple-element.49.refs_1_, bf16[128,640]{1,0:T(8,128)(2,1)S(1)} %get-tuple-element.50.refs_2_, f32[384,640]{1,0:T(8,128)S(1)} %get-tuple-element.51.refs_3_, ...), custom_call_target="tpu_custom_call", output_to_operand_aliasing={{}: (10, {})} | custom-call | tf_op jit(solution)/shard_map/finish_away/pallas_call | solution.py:259
  (11 shorter events, 0.1 us)
Async XLA Ops:
  3.4 2.0 %collective-permute-start = (bf16[10,128,128]{2,1,0:T(8,128)(2,1)S(1)}, bf16[10,128,128]{2,1,0:T(8,128)(2,1)S(1)}, u32[]{:S(2)}, u32[]{:S(2)}) collective-permute-start(bf16[10,128,128]{2,1,0:T(8,128)(2,1)S(1)} %get-tuple-element.41), channel_id=1, source_target_pairs={{0,1},{1,0},{2,3},{3,2},{4,5},{5,4},{6,7},{7,6},{8,9},{9,8},{10,11... | collective-permute-start | bytes 983048 | tf_op jit(solution)/shard_map/ppermute | solution.py:295
  5.6 2.7 %collective-permute-start.2 = (bf16[5,128,128]{2,1,0:T(8,128)(2,1)S(1)}, bf16[5,128,128]{2,1,0:T(8,128)(2,1)S(1)}, u32[]{:S(2)}, u32[]{:S(2)}) collective-permute-start(bf16[5,128,128]{2,1,0:T(8,128)(2,1)S(1)} %get-tuple-element.75), channel_id=1, source_target_pairs={{0,4},{1,5},{2,6},{3,7},{16,20},{17,21},{18,22},{19,23}} | collective-permute-start | bytes 491528 | tf_op jit(solution)/shard_map/ppermute | solution.py:307
  6.3 5.0 %collective-permute-start.1 = (bf16[5,128,128]{2,1,0:T(8,128)(2,1)S(1)}, bf16[5,128,128]{2,1,0:T(8,128)(2,1)S(1)}, u32[]{:S(2)}, u32[]{:S(2)}) collective-permute-start(bf16[5,128,128]{2,1,0:T(8,128)(2,1)S(1)} %get-tuple-element.76), channel_id=1, source_target_pairs={{0,4},{1,5},{2,6},{3,7},{16,20},{17,21},{18,22},{19,23}} | collective-permute-start | bytes 491528 | tf_op jit(solution)/shard_map/ppermute | solution.py:307
  7.0 13.1 %collective-permute-start.5 = (bf16[20,128,128]{2,1,0:T(8,128)(2,1)S(1)}, bf16[20,128,128]{2,1,0:T(8,128)(2,1)S(1)}, u32[]{:S(2)}, u32[]{:S(2)}) collective-permute-start(bf16[20,128,128]{2,1,0:T(8,128)(2,1)S(1)} %get-tuple-element.63), channel_id=1, source_target_pairs={{0,1},{4,5},{8,9},{12,13},{1,4},{9,12},{2,3},{6,7},{10,11},{14,15}... | collective-permute-start | bytes 1966088 | tf_op jit(solution)/shard_map/ppermute | solution.py:297
  8.4 6.7 %collective-permute-start.4 = (bf16[5,128,128]{2,1,0:T(8,128)(2,1)S(1)}, bf16[5,128,128]{2,1,0:T(8,128)(2,1)S(1)}, u32[]{:S(2)}, u32[]{:S(2)}) collective-permute-start(bf16[5,128,128]{2,1,0:T(8,128)(2,1)S(1)} %fusion.6), channel_id=1, source_target_pairs={{4,8},{5,9},{6,10},{7,11},{20,24},{21,25},{22,26},{23,27}} | collective-permute-start | bytes 491528 | tf_op jit(solution)/shard_map/ppermute | solution.py:307
  11.4 7.3 %collective-permute-start.3 = (bf16[5,128,128]{2,1,0:T(8,128)(2,1)S(1)}, bf16[5,128,128]{2,1,0:T(8,128)(2,1)S(1)}, u32[]{:S(2)}, u32[]{:S(2)}) collective-permute-start(bf16[5,128,128]{2,1,0:T(8,128)(2,1)S(1)} %fusion.8), channel_id=1, source_target_pairs={{4,8},{5,9},{6,10},{7,11},{20,24},{21,25},{22,26},{23,27}} | collective-permute-start | bytes 491528 | tf_op jit(solution)/shard_map/ppermute | solution.py:307
  12.1 14.3 %collective-permute-start.8 = (bf16[20,128,128]{2,1,0:T(8,128)(2,1)S(1)}, bf16[20,128,128]{2,1,0:T(8,128)(2,1)S(1)}, u32[]{:S(2)}, u32[]{:S(2)}) collective-permute-start(bf16[20,128,128]{2,1,0:T(8,128)(2,1)S(1)} %get-tuple-element.63), channel_id=1, source_target_pairs={{5,8},{7,10},{21,24},{23,26}} | collective-permute-start | bytes 1966088 | tf_op jit(solution)/shard_map/ppermute | solution.py:297
  15.1 7.6 %collective-permute-start.7 = (bf16[5,128,128]{2,1,0:T(8,128)(2,1)S(1)}, bf16[5,128,128]{2,1,0:T(8,128)(2,1)S(1)}, u32[]{:S(2)}, u32[]{:S(2)}) collective-permute-start(bf16[5,128,128]{2,1,0:T(8,128)(2,1)S(1)} %fusion.7), channel_id=1, source_target_pairs={{8,12},{9,13},{10,14},{11,15},{24,28},{25,29},{26,30},{27,31}} | collective-permute-start | bytes 491528 | tf_op jit(solution)/shard_map/ppermute | solution.py:307
  18.8 7.6 %collective-permute-start.6 = (bf16[5,128,128]{2,1,0:T(8,128)(2,1)S(1)}, bf16[5,128,128]{2,1,0:T(8,128)(2,1)S(1)}, u32[]{:S(2)}, u32[]{:S(2)}) collective-permute-start(bf16[5,128,128]{2,1,0:T(8,128)(2,1)S(1)} %fusion.9), channel_id=1, source_target_pairs={{8,12},{9,13},{10,14},{11,15},{24,28},{25,29},{26,30},{27,31}} | collective-permute-start | bytes 491528 | tf_op jit(solution)/shard_map/ppermute | solution.py:307
  26.7 6.1 %collective-permute-start.9 = (bf16[10,128,128]{2,1,0:T(8,128)(2,1)S(1)}, bf16[10,128,128]{2,1,0:T(8,128)(2,1)S(1)}, u32[]{:S(2)}, u32[]{:S(2)}) collective-permute-start(bf16[10,128,128]{2,1,0:T(8,128)(2,1)S(1)} %get-tuple-element.74), channel_id=1, source_target_pairs={{0,1},{1,0},{2,3},{3,2},{4,5},{5,4},{6,7},{7,6},{8,9},{9,8},{10,11... | collective-permute-start | bytes 983048 | tf_op jit(solution)/shard_map/ppermute | solution.py:345

commit v4 on v3

v4 whole, which is shorter than its diff:
```python
import functools

import jax
import jax.numpy as jnp
from jax import lax
from jax.experimental import pallas as pl
from jax.experimental.pallas import tpu as pltpu
from jax.sharding import PartitionSpec as P

BLOCK = 128
REACH = 2
EPSILON = 1e-06
F32 = jnp.float32
BF16 = jnp.bfloat16
MIB = 1024 * 1024
CHUNK = 5
TRANS = (((0,), (0,)), ((), ()))
ROWS = (((1,), (1,)), ((), ()))
ANY = pl.BlockSpec(memory_space=pl.ANY)
HERE = pl.BlockSpec(memory_space=pltpu.VMEM)
SMEM = pltpu.SMEM


def chunk_of(heads):
    return max(g for g in range(1, CHUNK + 1) if heads % g == 0)


def row_offsets():
    return lax.broadcasted_iota(jnp.int32, (BLOCK, BLOCK), 0).astype(F32)


def power(rate, tokens):
    return jnp.exp(jnp.full((1, BLOCK), -tokens, F32) * rate)


def span(head, heads):
    return pl.ds(pl.multiple_of(head * BLOCK, BLOCK), heads * BLOCK)


def columns(g, heads=1):
    return slice(g * BLOCK, (g + heads) * BLOCK)


def centred(rows):
    return rows - jnp.mean(rows, axis=-1, keepdims=True)


def fetch(source, target, sem):
    copy = pltpu.make_async_copy(source, target, sem)
    copy.start()
    return copy


def real_head(relative, count):
    rep = lax.axis_index("rep")
    return rep * count + relative if relative < count else (1 - rep) * count + (relative - count)


def states_kernel(
    rate_in, reach_in, k_in, v_in, own_ref, away_ref, second_ref, k_ref, v_ref, coef_ref, row_ref,
    rates, reaches, sems,
):
    heads = k_ref.shape[1] // BLOCK
    count = heads // 2
    blocks = k_in.shape[0] // BLOCK
    chunk = chunk_of(count)
    small = [fetch(rate_in, rates, sems.at[0]), fetch(reach_in, reaches, sems.at[1])]
    loads = []
    for j in range(heads // chunk):
        where = span(real_head(j * chunk, count), chunk)
        here = columns(j * chunk, chunk)
        loads.append(fetch(k_in.at[:, where], k_ref.at[:, here], sems.at[2 + 2 * j]))
        loads.append(fetch(v_in.at[:, where], v_ref.at[:, here], sems.at[3 + 2 * j]))
    for copy in small:
        copy.wait()
    first = (lax.axis_index("rep") == 0).astype(F32)
    one = jnp.ones((1, BLOCK), F32)
    for g in range(heads):
        head = real_head(g, count)
        row_ref[0, g] = one * rates[head]
        row_ref[1, g] = one * reaches[head].astype(F32)
    for g in range(count):
        head = real_head(g, count)
        is_full = (reaches[head] > REACH).astype(F32)
        device = power(rates[head], blocks * BLOCK) * is_full
        chip = power(rates[head], 2 * blocks * BLOCK) * is_full
        rows = [first * device + (1.0 - first), first + (1.0 - first) * device, chip]
        for i, row in enumerate(rows + [one * first, one * (1.0 - first)]):
            coef_ref[i, g] = row
    offsets = row_offsets() - float(BLOCK)
    for g in range(heads):
        if g % chunk == 0:
            loads[2 * (g // chunk)].wait()
            loads[2 * (g // chunk) + 1].wait()
        head = real_head(g, count)
        rate = rates[head]
        reach = reaches[head]
        is_full = (reach > REACH).astype(F32)
        base = jnp.exp(offsets * rate)
        parts = []
        for t in range(blocks):
            faded = k_ref[t * BLOCK : (t + 1) * BLOCK, columns(g)].astype(F32) * base
            if t == blocks - 2:
                second = faded.astype(BF16)
            if t < blocks - 1:
                faded = faded * (power(rate, (blocks - 1 - t) * BLOCK) * is_full)
            parts.append(faded.astype(BF16))
        values = v_ref[:, columns(g)]
        carry = lax.dot_general(jnp.concatenate(parts, 0), values, TRANS, preferred_element_type=F32)
        carry = centred(carry).astype(BF16)
        if g < count:
            own_ref[g] = carry
        else:
            away_ref[g - count] = carry
        rows = values[(blocks - 2) * BLOCK : (blocks - 1) * BLOCK]
        state = lax.dot_general(second, rows, TRANS, preferred_element_type=F32)
        second_ref[g] = centred(state).astype(BF16)


def block_states(keys, values, rates, reaches):
    length, features = keys.shape
    heads = rates.shape[0]
    half = jax.ShapeDtypeStruct((heads // 2, BLOCK, BLOCK), BF16)
    rows = jax.ShapeDtypeStruct((length, features), BF16)
    coefs = jax.ShapeDtypeStruct((5, heads // 2, 1, BLOCK), F32)
    lines = jax.ShapeDtypeStruct((2, heads, 1, BLOCK), F32)
    return pl.pallas_call(
        states_kernel,
        in_specs=[ANY] * 4,
        out_specs=[HERE] * 7,
        out_shape=[half, half, jax.ShapeDtypeStruct((heads, BLOCK, BLOCK), BF16), rows, rows, coefs, lines],
        scratch_shapes=[
            SMEM(rates.shape, F32),
            SMEM(reaches.shape, jnp.int32),
            pltpu.SemaphoreType.DMA((2 + 2 * (heads // chunk_of(heads // 2)),)),
        ],
        compiler_params=pltpu.CompilerParams(vmem_limit_bytes=10 * MIB),
        name="block_states",
    )(rates, reaches, keys, values)


def local_kernel(
    start, gain_ref, q_ref, g_ref, row_ref, k_ref, v_ref, near_ref, faded_ref, second_ref, silu_ref, weights
):
    length = k_ref.shape[0]
    blocks = length // BLOCK
    count = near_ref.shape[1] // BLOCK
    first = real_head(start, k_ref.shape[1] // BLOCK // 2)
    offsets = row_offsets()
    gap = offsets - lax.broadcasted_iota(jnp.int32, (BLOCK, BLOCK), 1).astype(F32)
    causal = gap >= 0
    for g in range(count):
        rate = row_ref[0, start + g]
        reach = row_ref[1, start + g]
        fading = jnp.exp(gap * (-rate))
        tables = [jnp.where(causal, fading, 0.0)]
        for back in range(1, blocks):
            tables.append(fading * (power(rate, back * BLOCK) * (reach >= back).astype(F32)))
        fade = jnp.exp(offsets * (-rate))
        seconds = jnp.logical_and(reach >= 2, reach <= REACH).astype(F32)
        for t in range(blocks):
            rows = slice(t * BLOCK, (t + 1) * BLOCK)
            queries = q_ref[rows, span(first + g, 1)]
            scores = lax.dot_general(
                queries, k_ref[: (t + 1) * BLOCK, columns(start + g)], ROWS, preferred_element_type=F32
            )
            for u in range(t + 1):
                tile = slice(u * BLOCK, (u + 1) * BLOCK)
                weights[g, rows, tile] = (scores[:, tile] * tables[t - u]).astype(BF16)
            faded = queries.astype(F32) * fade
            faded_ref[rows, columns(g)] = (faded * (power(rate, t * BLOCK) * (reach > t).astype(F32))).astype(BF16)
            if t == 0:
                second_ref[:, columns(g)] = (faded * (power(rate, BLOCK) * seconds)).astype(BF16)
    for g in range(count):
        for t in range(blocks):
            rows = slice(t * BLOCK, (t + 1) * BLOCK)
            near = jnp.dot(
                weights[g, rows, : (t + 1) * BLOCK],
                v_ref[: (t + 1) * BLOCK, columns(start + g)],
                preferred_element_type=F32,
            )
            near_ref[rows, columns(g)] = centred(near)
    for g in range(count):
        gate = g_ref[:, span(first + g, 1)].astype(F32)
        silu_ref[:, columns(g)] = gate / (1.0 + jnp.exp(-gate)) * gain_ref[pl.ds(first + g, 1), :]


def local_part(start, count, gain, queries, gates, lines, keys, values):
    length = keys.shape[0]
    width = count * BLOCK
    rows = jax.ShapeDtypeStruct((length, width), BF16)
    wide = jax.ShapeDtypeStruct((length, width), F32)
    shapes = [wide, rows, jax.ShapeDtypeStruct((BLOCK, width), BF16), wide]
    return pl.pallas_call(
        functools.partial(local_kernel, start),
        in_specs=[HERE] * 6,
        out_specs=[HERE] * len(shapes),
        out_shape=shapes,
        scratch_shapes=[
            pltpu.VMEM((count, length, length), BF16),
        ],
        compiler_params=pltpu.CompilerParams(vmem_limit_bytes=14 * MIB),
        cost_estimate=pl.CostEstimate(flops=1, bytes_accessed=1, transcendentals=0),
        name=f"local_{start}",
    )(gain, queries, gates, lines, keys, values)


def finish_kernel(starts, *refs):
    second_ref = refs[10]
    out_ref, retained, rows_ref, sems = refs[-4:]
    blocks = out_ref.shape[0] // BLOCK
    half = out_ref.shape[1] // BLOCK // 2
    done = 0
    for j, start in enumerate(starts):
        near_ref, faded_ref, factor_ref, _, carry_ref = refs[5 * j : 5 * j + 5]
        for g in range(carry_ref.shape[0]):
            cols = columns(g)
            here = columns(done + g)
            far = jnp.dot(faded_ref[:, cols], carry_ref[g], preferred_element_type=F32)
            extra = jnp.dot(factor_ref[:, cols], second_ref[(start + half) % (2 * half) + g], preferred_element_type=F32)
            retained[:BLOCK, here] = near_ref[:BLOCK, cols] + far[:BLOCK] + extra
            retained[BLOCK:, here] = near_ref[BLOCK:, cols] + far[BLOCK:]
        done += carry_ref.shape[0]
    done = 0
    stores = []
    for j, start in enumerate(starts):
        silu_ref, count = refs[5 * j + 3], refs[5 * j + 4].shape[0]
        for g in range(count):
            here = columns(done + g)
            for t in range(blocks):
                rows = slice(t * BLOCK, (t + 1) * BLOCK)
                parted = retained[rows, here]
                variance = jnp.mean(parted * parted, axis=-1, keepdims=True)
                mixed_rows = silu_ref[rows, columns(g)] * (parted * lax.rsqrt(variance + EPSILON))
                rows_ref[rows, here] = mixed_rows.astype(BF16)
        target = out_ref.at[:, span(real_head(start, half), count)]
        stores.append(fetch(rows_ref.at[:, columns(done, count)], target, sems.at[j]))
        done += count
    for copy in stores:
        copy.wait()


def finish(starts, parts, carries, second, into=None):
    length = parts[0][0].shape[0]
    width = 2 * carries[0].shape[0] * BLOCK
    features = second.shape[0] * BLOCK
    operands = [x for part, carry in zip(parts, carries) for x in (*part, carry)] + [second]
    operands += [] if into is None else [into]
    return pl.pallas_call(
        functools.partial(finish_kernel, starts),
        in_specs=[HERE] * 11 + ([] if into is None else [ANY]),
        out_specs=ANY,
        out_shape=jax.ShapeDtypeStruct((length, features), BF16),
        scratch_shapes=[
            pltpu.VMEM((length, width), F32),
            pltpu.VMEM((length, width), BF16),
            pltpu.SemaphoreType.DMA((2,)),
        ],
        input_output_aliases={} if into is None else {11: 0},
        compiler_params=pltpu.CompilerParams(vmem_limit_bytes=10 * MIB),
        name=f"finish_{starts[0]}",
    )(*operands)


def mixed(a, x, b, y):
    total = a * x.astype(F32) + b * y.astype(F32)
    return total.astype(BF16)


def after(value, *others):
    return lax.optimization_barrier((value, *others))[0]


def per_device(queries, key_vectors, value_vectors, gate_input, norm_gain, decay_rate, band_reach):
    heads = decay_rate.shape[0]
    half = heads // 2
    few = half // 2
    chips = lax.axis_size("ctx")
    stay = functools.partial(pltpu.with_memory_space_constraint, memory_space=pltpu.HBM)
    keys, values = stay(key_vectors), stay(value_vectors)
    rates, reaches, gain = stay(decay_rate), stay(band_reach), norm_gain.reshape(-1, BLOCK)
    gates = gate_input

    own, away, seconds, keys, values, coefs, lines = block_states(keys, values, rates, reaches)
    to_mine, to_pair, chip_fade, is_first, is_last = [coefs[i] for i in range(5)]
    one = jnp.ones((1, 1, 1), F32)
    early, late = slice(0, few), slice(few, half)
    swap = lambda x: lax.ppermute(x, "rep", [(0, 1), (1, 0)])
    steps = [(i, i + 1) for i in range(2 * chips - 1)]
    onward = lambda x, pairs: lax.ppermute(x, ("ctx", "rep"), pairs)
    hop = lambda x, i: lax.ppermute(x, "ctx", [(i, i + 1)])
    step = lambda part, got: mixed(chip_fade[part], got, one, total[part])

    def shared(part, got):
        sent = mixed(to_mine[part], got, is_first[part], own[part])
        kept = mixed(to_pair[part], got, is_last[part], from_pair[part])
        return kept, swap(sent)

    from_pair = swap(away)
    across = [(3, 4)] if chips == 4 else steps
    second_first = onward(seconds, across)
    total = mixed(to_mine, own, to_pair, from_pair)
    b1 = hop(total[early], 0)
    a1 = hop(total[late], 0)
    if chips == 4:
        second_rest = onward(after(seconds, total), [pair for pair in steps if pair not in across])
        part0 = local_part(0, few, gain, after(queries, total), gates, lines, keys, values)
        b1, _ = lax.optimization_barrier((b1, part0[0]))
        t1 = step(early, b1)
        b2 = hop(t1, 1)
        local = lambda start, count, *others: local_part(
            start, count, gain, after(queries, *others), gates, lines, keys, values
        )
        part2 = local(half, few, t1)
        a1, _ = lax.optimization_barrier((a1, part2[0]))
        u1 = step(late, a1)
        a2 = hop(u1, 1)
        part1 = local(few, half - few, u1)
        b2, second_first, _ = lax.optimization_barrier((b2, second_first, part1[0]))
        t2 = step(early, b2)
        b3 = hop(t2, 2)
        part3 = local(half + few, half - few, t2)
        a2, _ = lax.optimization_barrier((a2, part3[0]))
        u2 = step(late, a2)
        a3 = hop(u2, 2)
        b3, second_rest, _ = lax.optimization_barrier((b3, second_rest, u2))
        second = second_first + second_rest
        got_b = b1 + b2 + b3
        kept_b, sent_b = shared(early, got_b)
        out = finish((0, half), (part0, part2), (kept_b, sent_b), second)
        a3, out = lax.optimization_barrier((a3, out))
        got_a = a1 + a2 + a3
    else:
        part0 = local_part(0, few, gain, queries, gates, lines, keys, values)
        local = lambda start, count: local_part(start, count, gain, queries, gates, lines, keys, values)
        got_a, got_b = arrived_a, arrived_b = a1, b1
        for i in range(1, chips - 1):
            arrived_a, arrived_b = hop(step(late, arrived_a), i), hop(step(early, arrived_b), i)
            got_a, got_b = got_a + arrived_a, got_b + arrived_b
        part1, part2, part3 = local(few, half - few), local(half, few), local(half + few, half - few)
        second = second_first
        kept_b, sent_b = shared(early, got_b)
        out = finish((0, half), (part0, part2), (kept_b, sent_b), second)
    kept_a, sent_a = shared(late, got_a)
    return finish((few, half + few), (part1, part3), (kept_a, sent_a), second, out)


def solution(mesh):
    rows = P(("group", "ctx", "rep"), "head")
    return jax.shard_map(
        per_device,
        mesh=mesh,
        in_specs=(rows, rows, rows, rows, P("head"), P("head"), P("head")),
        out_specs=rows,
        check_vma=False,
    )
```

time: 34.8 us -> 33.6 us (0.966)
  waiting for transfers between devices: 5.27 us -> 11.4 us
  Pallas kernels: 15.7 us -> 12 us
  starting transfers between devices: 12.3 us -> 8.67 us
    ppermute x6, waiting for transfers between devices: 4.01 us -> 8.76 us  [per_device(): hop = lambda x, i: lax.ppermute(x, 'ctx', [(i, i + 1)])]
    pallas_call x7, Pallas kernels: 15.7 us -> 12 us  [the longest x4 5.1 us: local_part(): pl.pallas_call(functools.partial(local_kernel, start), in_specs=[HERE] *...]
    ppermute x4 -> x5, starting transfers between devices: 6.99 us -> 3.4 us  [the longest x2 1.98 us: per_device(): onward = lambda x, pairs: lax.ppermute(x, ('ctx', 'rep'), pairs)]
    ppermute x4 -> x5, waiting for transfers between devices: 1.25 us -> 2.66 us  [the longest x3 2.66 us: per_device(): swap = lambda x: lax.ppermute(x, 'rep', [(0, 1), (1, 0)])]
    convert_element_type x6 -> x7, other arithmetic: 0.64 us -> 0.71 us  [mixed(): return total.astype(BF16)]
  transfers between devices with their start and end apart: 10 -> 11, of which waited for: 3 -> 5; matrix products, arithmetic and copies ran while one was open for 1% -> 2% of each run, Pallas kernels for 31% -> 20%
where the time goes in v4:
time: 33.6 us; the launch traced here: 33.3 us
  Pallas kernels  12 us (36%)
  waiting for transfers between devices  11.4 us (34%)
  starting transfers between devices  8.67 us (26%)
  other arithmetic  0.91 us (3%)
    ppermute x6, waiting for transfers between devices, per_device(): hop = lambda x, i: lax.ppermute(x, 'ctx', [(i, i + 1)])  8.76 us
    ppermute x6, starting transfers between devices, per_device(): hop = lambda x, i: lax.ppermute(x, 'ctx', [(i, i + 1)])  5.27 us
    pallas_call x4, Pallas kernels, local_part(): pl.pallas_call(functools.partial(local_kernel, start), in_specs=[HERE] *...  5.1 us
    pallas_call x1, Pallas kernels, block_states(): pl.pallas_call(states_kernel, in_specs=[ANY] * 4, out_specs=[HERE] * 7, o...  3.57 us
    pallas_call x2, Pallas kernels, finish(): pl.pallas_call(functools.partial(finish_kernel, starts), in_specs=[HERE]...  3.29 us
    ppermute x3, waiting for transfers between devices, per_device(): swap = lambda x: lax.ppermute(x, 'rep', [(0, 1), (1, 0)])  2.66 us
    ppermute x2, starting transfers between devices, per_device(): onward = lambda x, pairs: lax.ppermute(x, ('ctx', 'rep'), pairs)  1.98 us
    ppermute x3, starting transfers between devices, per_device(): swap = lambda x: lax.ppermute(x, 'rep', [(0, 1), (1, 0)])  1.42 us
  transfers between devices with their start and end apart: 11, of which 5 were waited for; matrix products, arithmetic and copies ran while one was open for 2% of the time, Pallas kernels for 20%

profile of v4, /device:TPU:25, one launch (start us, length us, event | category | flops | bytes accessed | tf_op | source)
XLA Modules:
  0.0 33.3 jit_solution(13727547582926425003)
XLA Ops:
  0.0 3.6 %block_states.1 = (bf16[10,128,128]{2,1,0:T(8,128)(2,1)S(1)}, bf16[10,128,128]{2,1,0:T(8,128)(2,1)S(1)}, bf16[20,128,128]{2,1,0:T(8,128)(2,1)S(1)}, bf16[384,256...) custom-call(f32[20]{0:T(128)} %rate_in.1, ...), custom_call_target="tpu_custom_call" | custom-call | tf_op jit(solution)/shard_map/block_states/pallas_call | solution.py:127
  3.6 0.7 %collective-permute-start = (bf16[10,128,128]{2,1,0:T(8,128)(2,1)S(1)}, bf16[10,128,128]{2,1,0:T(8,128)(2,1)S(1)}, u32[]{:S(2)}, u32[]{:S(2)}) collective-permute-start(bf16[10,128,128]{2,1,0:T(8,128)(2,1)S(1)} %get-tuple-element.44), channel_id=1, source_target_pairs={{0,1},{1,0},{2,3},{3,2},{4,5},{5,4},{6,7},{7,6},{8,9},{9,8},{10,11... | collective-permute-start | bytes 983048 | tf_op jit(solution)/shard_map/ppermute | solution.py:288
  4.3 0.7 %collective-permute-start.5 = (bf16[20,128,128]{2,1,0:T(8,128)(2,1)S(1)}, bf16[20,128,128]{2,1,0:T(8,128)(2,1)S(1)}, u32[]{:S(2)}, u32[]{:S(2)}) collective-permute-start(bf16[20,128,128]{2,1,0:T(8,128)(2,1)S(1)} %get-tuple-element.67), channel_id=1, source_target_pairs={{5,8},{7,10},{21,24},{23,26}} | collective-permute-start | bytes 1966088 | tf_op jit(solution)/shard_map/ppermute | solution.py:290
  5.1 0.5 %collective-permute-done = bf16[10,128,128]{2,1,0:T(8,128)(2,1)S(1)} collective-permute-done((bf16[10,128,128]{2,1,0:T(8,128)(2,1)S(1)}, bf16[10,128,128]{2,1,0:T(8,128)(2,1)S(1)}, u32[]{:S(2)}, u32[]{:S(2)}) %collective-permute-start) | collective-permute-done | bytes 327712 | tf_op jit(solution)/shard_map/ppermute | solution.py:288
  5.6 0.1 add_convert_fusion
  5.8 0.7 %collective-permute-start.2 = (bf16[5,128,128]{2,1,0:T(8,128)(2,1)S(1)}, bf16[5,128,128]{2,1,0:T(8,128)(2,1)S(1)}, u32[]{:S(2)}, u32[]{:S(2)}) collective-permute-start(bf16[5,128,128]{2,1,0:T(8,128)(2,1)S(1)} %get-tuple-element.83), channel_id=1, source_target_pairs={{0,4},{1,5},{2,6},{3,7},{16,20},{17,21},{18,22},{19,23}} | collective-permute-start | bytes 491528 | tf_op jit(solution)/shard_map/ppermute | solution.py:291
  6.4 0.7 %collective-permute-start.1 = (bf16[5,128,128]{2,1,0:T(8,128)(2,1)S(1)}, bf16[5,128,128]{2,1,0:T(8,128)(2,1)S(1)}, u32[]{:S(2)}, u32[]{:S(2)}) collective-permute-start(bf16[5,128,128]{2,1,0:T(8,128)(2,1)S(1)} %get-tuple-element.84), channel_id=1, source_target_pairs={{0,4},{1,5},{2,6},{3,7},{16,20},{17,21},{18,22},{19,23}} | collective-permute-start | bytes 491528 | tf_op jit(solution)/shard_map/ppermute | solution.py:291
  7.1 1.3 %collective-permute-start.8 = (bf16[20,128,128]{2,1,0:T(8,128)(2,1)S(1)}, bf16[20,128,128]{2,1,0:T(8,128)(2,1)S(1)}, u32[]{:S(2)}, u32[]{:S(2)}) collective-permute-start(bf16[20,128,128]{2,1,0:T(8,128)(2,1)S(1)} %get-tuple-element.67), channel_id=1, source_target_pairs={{0,1},{1,4},{4,5},{8,9},{9,12},{12,13},{2,3},{3,6},{6,7},{10,11},{... | collective-permute-start | bytes 1966088 | tf_op jit(solution)/shard_map/ppermute | solution.py:290
  8.5 1.3 %local_0.1 = (f32[384,640]{1,0:T(8,128)S(1)}, bf16[384,640]{1,0:T(8,128)(2,1)S(1)}, bf16[128,640]{1,0:T(8,128)(2,1)S(1)}, f32[384,640]{1,0:T(8,128)S(1)}) custom-call(f32[20,128]{1,0:T(8,128)S(1)} %bitcast.27, bf16[384,2560]{1,0:T(8,128)(2,1)S(1)} %copy-done, bf16[384,2560]{1,0:T(8,128)(2,1)S(1)} %copy-done.1, ...), custom_call_target="tpu_custom_call" | custom-call | flops 1 | bytes 1 | tf_op jit(solution)/shard_map/local_0/pallas_call | solution.py:194
  9.7 0.0 collective-permute-done.2
  9.8 0.1 fusion
  9.8 0.7 %collective-permute-start.4 = (bf16[5,128,128]{2,1,0:T(8,128)(2,1)S(1)}, bf16[5,128,128]{2,1,0:T(8,128)(2,1)S(1)}, u32[]{:S(2)}, u32[]{:S(2)}) collective-permute-start(bf16[5,128,128]{2,1,0:T(8,128)(2,1)S(1)} %fusion), channel_id=1, source_target_pairs={{4,8},{5,9},{6,10},{7,11},{20,24},{21,25},{22,26},{23,27}} | collective-permute-start | bytes 491528 | tf_op jit(solution)/shard_map/ppermute | solution.py:291
  10.5 1.3 %local_10.1 = (f32[384,640]{1,0:T(8,128)S(1)}, bf16[384,640]{1,0:T(8,128)(2,1)S(1)}, bf16[128,640]{1,0:T(8,128)(2,1)S(1)}, f32[384,640]{1,0:T(8,128)S(1)}) custom-call(f32[20,128]{1,0:T(8,128)S(1)} %bitcast.28, bf16[384,2560]{1,0:T(8,128)(2,1)S(1)} %copy-done, bf16[384,2560]{1,0:T(8,128)(2,1)S(1)} %copy-done.1, ...), custom_call_target="tpu_custom_call" | custom-call | flops 1 | bytes 1 | tf_op jit(solution)/shard_map/local_10/pallas_call | solution.py:194
  11.8 0.1 fusion.2
  11.9 0.7 %collective-permute-start.3 = (bf16[5,128,128]{2,1,0:T(8,128)(2,1)S(1)}, bf16[5,128,128]{2,1,0:T(8,128)(2,1)S(1)}, u32[]{:S(2)}, u32[]{:S(2)}) collective-permute-start(bf16[5,128,128]{2,1,0:T(8,128)(2,1)S(1)} %fusion.2), channel_id=1, source_target_pairs={{4,8},{5,9},{6,10},{7,11},{20,24},{21,25},{22,26},{23,27}} | collective-permute-start | bytes 491528 | tf_op jit(solution)/shard_map/ppermute | solution.py:291
  12.5 1.3 %local_5.1 = (f32[384,640]{1,0:T(8,128)S(1)}, bf16[384,640]{1,0:T(8,128)(2,1)S(1)}, bf16[128,640]{1,0:T(8,128)(2,1)S(1)}, f32[384,640]{1,0:T(8,128)S(1)}) custom-call(f32[20,128]{1,0:T(8,128)S(1)} %bitcast.29, bf16[384,2560]{1,0:T(8,128)(2,1)S(1)} %copy-done, bf16[384,2560]{1,0:T(8,128)(2,1)S(1)} %copy-done.1, ...), custom_call_target="tpu_custom_call" | custom-call | flops 1 | bytes 1 | tf_op jit(solution)/shard_map/local_5/pallas_call | solution.py:194
  13.8 0.1 fusion.1
  13.9 1.3 %collective-permute-start.7 = (bf16[5,128,128]{2,1,0:T(8,128)(2,1)S(1)}, bf16[5,128,128]{2,1,0:T(8,128)(2,1)S(1)}, u32[]{:S(2)}, u32[]{:S(2)}) collective-permute-start(bf16[5,128,128]{2,1,0:T(8,128)(2,1)S(1)} %fusion.1), channel_id=1, source_target_pairs={{8,12},{9,13},{10,14},{11,15},{24,28},{25,29},{26,30},{27,31}} | collective-permute-start | bytes 491528 | tf_op jit(solution)/shard_map/ppermute | solution.py:291
  15.2 1.3 %local_15.1 = (f32[384,640]{1,0:T(8,128)S(1)}, bf16[384,640]{1,0:T(8,128)(2,1)S(1)}, bf16[128,640]{1,0:T(8,128)(2,1)S(1)}, f32[384,640]{1,0:T(8,128)S(1)}) custom-call(f32[20,128]{1,0:T(8,128)S(1)} %bitcast.30, bf16[384,2560]{1,0:T(8,128)(2,1)S(1)} %copy-done, bf16[384,2560]{1,0:T(8,128)(2,1)S(1)} %copy-done.1, ...), custom_call_target="tpu_custom_call" | custom-call | flops 1 | bytes 1 | tf_op jit(solution)/shard_map/local_15/pallas_call | solution.py:194
  16.5 0.1 fusion.3
  16.6 1.3 %collective-permute-start.6 = (bf16[5,128,128]{2,1,0:T(8,128)(2,1)S(1)}, bf16[5,128,128]{2,1,0:T(8,128)(2,1)S(1)}, u32[]{:S(2)}, u32[]{:S(2)}) collective-permute-start(bf16[5,128,128]{2,1,0:T(8,128)(2,1)S(1)} %fusion.3), channel_id=1, source_target_pairs={{8,12},{9,13},{10,14},{11,15},{24,28},{25,29},{26,30},{27,31}} | collective-permute-start | bytes 491528 | tf_op jit(solution)/shard_map/ppermute | solution.py:291
  17.9 7.6 %collective-permute-done.7 = bf16[5,128,128]{2,1,0:T(8,128)(2,1)S(1)} collective-permute-done((bf16[5,128,128]{2,1,0:T(8,128)(2,1)S(1)}, bf16[5,128,128]{2,1,0:T(8,128)(2,1)S(1)}, u32[]{:S(2)}, u32[]{:S(2)}) %collective-permute-start.7) | collective-permute-done | bytes 163872 | tf_op jit(solution)/shard_map/ppermute | solution.py:291
  25.5 0.2 fusion.7
  25.6 0.1 collective-permute-start.9
  25.7 0.2 add.52.refs_10_
  25.9 1.2 %collective-permute-done.9.refs_9_ = bf16[5,128,128]{2,1,0:T(8,128)(2,1)S(1)} collective-permute-done((bf16[5,128,128]{2,1,0:T(8,128)(2,1)S(1)}, bf16[5,128,128]{2,1,0:T(8,128)(2,1)S(1)}, u32[]{:S(2)}, u32[]{:S(2)}) %collective-permute-start.9) | collective-permute-done | bytes 163872 | tf_op jit(solution)/shard_map/ppermute | solution.py:288
  27.1 1.6 %finish_0.1.refs_11_ = bf16[384,2560]{1,0:T(8,128)(2,1)} custom-call(f32[384,640]{1,0:T(8,128)S(1)} %get-tuple-element.49.refs_0_, bf16[384,640]{1,0:T(8,128)(2,1)S(1)} %get-tuple-element.64.refs_1_, bf16[128,640]{1,0:T(8,128)(2,1)S(1)} %get-tuple-element.65.refs_2_, f32[384,640]{1,0:T(8,128)S(1)} %get-tuple-element.66.refs_3_, ...), custom_call_target="tpu_custom_call" | custom-call | tf_op jit(solution)/shard_map/finish_0/pallas_call | solution.py:249
  28.7 1.1 %collective-permute-done.6 = bf16[5,128,128]{2,1,0:T(8,128)(2,1)S(1)} collective-permute-done((bf16[5,128,128]{2,1,0:T(8,128)(2,1)S(1)}, bf16[5,128,128]{2,1,0:T(8,128)(2,1)S(1)}, u32[]{:S(2)}, u32[]{:S(2)}) %collective-permute-start.6) | collective-permute-done | bytes 163872 | tf_op jit(solution)/shard_map/ppermute | solution.py:291
  29.9 0.2 fusion.11
  30.1 0.6 %collective-permute-start.10 = (bf16[5,128,128]{2,1,0:T(8,128)(2,1)S(1)}, bf16[5,128,128]{2,1,0:T(8,128)(2,1)S(1)}, u32[]{:S(2)}, u32[]{:S(2)}) collective-permute-start(bf16[5,128,128]{2,1,0:T(8,128)(2,1)S(1)} %get-tuple-element.79), channel_id=1, source_target_pairs={{0,1},{1,0},{2,3},{3,2},{4,5},{5,4},{6,7},{7,6},{8,9},{9,8},{10,11... | collective-permute-start | bytes 491528 | tf_op jit(solution)/shard_map/ppermute | solution.py:288
  30.7 1.0 %collective-permute-done.10.refs_9_ = bf16[5,128,128]{2,1,0:T(8,128)(2,1)S(1)} collective-permute-done((bf16[5,128,128]{2,1,0:T(8,128)(2,1)S(1)}, bf16[5,128,128]{2,1,0:T(8,128)(2,1)S(1)}, u32[]{:S(2)}, u32[]{:S(2)}) %collective-permute-start.10) | collective-permute-done | bytes 163872 | tf_op jit(solution)/shard_map/ppermute | solution.py:288
  31.7 1.6 %finish_5.1 = bf16[384,2560]{1,0:T(8,128)(2,1)} custom-call(f32[384,640]{1,0:T(8,128)S(1)} %get-tuple-element.55.refs_0_, bf16[384,640]{1,0:T(8,128)(2,1)S(1)} %get-tuple-element.56.refs_1_, bf16[128,640]{1,0:T(8,128)(2,1)S(1)} %get-tuple-element.57.refs_2_, f32[384,640]{1,0:T(8,128)S(1)} %get-tuple-element.58.refs_3_, ...), custom_call_target="tpu_custom_call", output_to_operand_aliasing={{}: (11, {})} | custom-call | tf_op jit(solution)/shard_map/finish_5/pallas_call | solution.py:249
  (21 shorter events, 0.1 us)
Async XLA Ops:
  0.0 8.4 %copy-start = (bf16[384,2560]{1,0:T(8,128)(2,1)S(1)}, bf16[384,2560]{1,0:T(8,128)(2,1)}, u32[]{:S(2)}) copy-start(bf16[384,2560]{1,0:T(8,128)(2,1)} %q_ref.3) | copy-start | bytes 5898244
  0.0 8.4 %copy-start.2 = (f32[2560]{0:T(1024)S(1)}, f32[2560]{0:T(1024)}, u32[]{:S(2)}) copy-start(f32[2560]{0:T(1024)} %param.11) | copy-start | bytes 30724
  0.0 8.4 %copy-start.1 = (bf16[384,2560]{1,0:T(8,128)(2,1)S(1)}, bf16[384,2560]{1,0:T(8,128)(2,1)}, u32[]{:S(2)}) copy-start(bf16[384,2560]{1,0:T(8,128)(2,1)} %g_ref.7) | copy-start | bytes 5898244
  3.6 2.0 %collective-permute-start = (bf16[10,128,128]{2,1,0:T(8,128)(2,1)S(1)}, bf16[10,128,128]{2,1,0:T(8,128)(2,1)S(1)}, u32[]{:S(2)}, u32[]{:S(2)}) collective-permute-start(bf16[10,128,128]{2,1,0:T(8,128)(2,1)S(1)} %get-tuple-element.44), channel_id=1, source_target_pairs={{0,1},{1,0},{2,3},{3,2},{4,5},{5,4},{6,7},{7,6},{8,9},{9,8},{10,11... | collective-permute-start | bytes 983048 | tf_op jit(solution)/shard_map/ppermute | solution.py:288
  4.3 9.5 %collective-permute-start.5 = (bf16[20,128,128]{2,1,0:T(8,128)(2,1)S(1)}, bf16[20,128,128]{2,1,0:T(8,128)(2,1)S(1)}, u32[]{:S(2)}, u32[]{:S(2)}) collective-permute-start(bf16[20,128,128]{2,1,0:T(8,128)(2,1)S(1)} %get-tuple-element.67), channel_id=1, source_target_pairs={{5,8},{7,10},{21,24},{23,26}} | collective-permute-start | bytes 1966088 | tf_op jit(solution)/shard_map/ppermute | solution.py:290
  5.8 4.0 %collective-permute-start.2 = (bf16[5,128,128]{2,1,0:T(8,128)(2,1)S(1)}, bf16[5,128,128]{2,1,0:T(8,128)(2,1)S(1)}, u32[]{:S(2)}, u32[]{:S(2)}) collective-permute-start(bf16[5,128,128]{2,1,0:T(8,128)(2,1)S(1)} %get-tuple-element.83), channel_id=1, source_target_pairs={{0,4},{1,5},{2,6},{3,7},{16,20},{17,21},{18,22},{19,23}} | collective-permute-start | bytes 491528 | tf_op jit(solution)/shard_map/ppermute | solution.py:291
  6.4 5.3 %collective-permute-start.1 = (bf16[5,128,128]{2,1,0:T(8,128)(2,1)S(1)}, bf16[5,128,128]{2,1,0:T(8,128)(2,1)S(1)}, u32[]{:S(2)}, u32[]{:S(2)}) collective-permute-start(bf16[5,128,128]{2,1,0:T(8,128)(2,1)S(1)} %get-tuple-element.84), channel_id=1, source_target_pairs={{0,4},{1,5},{2,6},{3,7},{16,20},{17,21},{18,22},{19,23}} | collective-permute-start | bytes 491528 | tf_op jit(solution)/shard_map/ppermute | solution.py:291
  7.1 18.3 %collective-permute-start.8 = (bf16[20,128,128]{2,1,0:T(8,128)(2,1)S(1)}, bf16[20,128,128]{2,1,0:T(8,128)(2,1)S(1)}, u32[]{:S(2)}, u32[]{:S(2)}) collective-permute-start(bf16[20,128,128]{2,1,0:T(8,128)(2,1)S(1)} %get-tuple-element.67), channel_id=1, source_target_pairs={{0,1},{1,4},{4,5},{8,9},{9,12},{12,13},{2,3},{3,6},{6,7},{10,11},{... | collective-permute-start | bytes 1966088 | tf_op jit(solution)/shard_map/ppermute | solution.py:290
  9.8 4.0 %collective-permute-start.4 = (bf16[5,128,128]{2,1,0:T(8,128)(2,1)S(1)}, bf16[5,128,128]{2,1,0:T(8,128)(2,1)S(1)}, u32[]{:S(2)}, u32[]{:S(2)}) collective-permute-start(bf16[5,128,128]{2,1,0:T(8,128)(2,1)S(1)} %fusion), channel_id=1, source_target_pairs={{4,8},{5,9},{6,10},{7,11},{20,24},{21,25},{22,26},{23,27}} | collective-permute-start | bytes 491528 | tf_op jit(solution)/shard_map/ppermute | solution.py:291
  11.9 4.6 %collective-permute-start.3 = (bf16[5,128,128]{2,1,0:T(8,128)(2,1)S(1)}, bf16[5,128,128]{2,1,0:T(8,128)(2,1)S(1)}, u32[]{:S(2)}, u32[]{:S(2)}) collective-permute-start(bf16[5,128,128]{2,1,0:T(8,128)(2,1)S(1)} %fusion.2), channel_id=1, source_target_pairs={{4,8},{5,9},{6,10},{7,11},{20,24},{21,25},{22,26},{23,27}} | collective-permute-start | bytes 491528 | tf_op jit(solution)/shard_map/ppermute | solution.py:291
  13.9 11.6 %collective-permute-start.7 = (bf16[5,128,128]{2,1,0:T(8,128)(2,1)S(1)}, bf16[5,128,128]{2,1,0:T(8,128)(2,1)S(1)}, u32[]{:S(2)}, u32[]{:S(2)}) collective-permute-start(bf16[5,128,128]{2,1,0:T(8,128)(2,1)S(1)} %fusion.1), channel_id=1, source_target_pairs={{8,12},{9,13},{10,14},{11,15},{24,28},{25,29},{26,30},{27,31}} | collective-permute-start | bytes 491528 | tf_op jit(solution)/shard_map/ppermute | solution.py:291
  16.6 13.3 %collective-permute-start.6 = (bf16[5,128,128]{2,1,0:T(8,128)(2,1)S(1)}, bf16[5,128,128]{2,1,0:T(8,128)(2,1)S(1)}, u32[]{:S(2)}, u32[]{:S(2)}) collective-permute-start(bf16[5,128,128]{2,1,0:T(8,128)(2,1)S(1)} %fusion.3), channel_id=1, source_target_pairs={{8,12},{9,13},{10,14},{11,15},{24,28},{25,29},{26,30},{27,31}} | collective-permute-start | bytes 491528 | tf_op jit(solution)/shard_map/ppermute | solution.py:291
  25.6 1.5 %collective-permute-start.9 = (bf16[5,128,128]{2,1,0:T(8,128)(2,1)S(1)}, bf16[5,128,128]{2,1,0:T(8,128)(2,1)S(1)}, u32[]{:S(2)}, u32[]{:S(2)}) collective-permute-start(bf16[5,128,128]{2,1,0:T(8,128)(2,1)S(1)} %get-tuple-element.81), channel_id=1, source_target_pairs={{0,1},{1,0},{2,3},{3,2},{4,5},{5,4},{6,7},{7,6},{8,9},{9,8},{10,11... | collective-permute-start | bytes 491528 | tf_op jit(solution)/shard_map/ppermute | solution.py:288
  30.1 1.6 %collective-permute-start.10 = (bf16[5,128,128]{2,1,0:T(8,128)(2,1)S(1)}, bf16[5,128,128]{2,1,0:T(8,128)(2,1)S(1)}, u32[]{:S(2)}, u32[]{:S(2)}) collective-permute-start(bf16[5,128,128]{2,1,0:T(8,128)(2,1)S(1)} %get-tuple-element.79), channel_id=1, source_target_pairs={{0,1},{1,0},{2,3},{3,2},{4,5},{5,4},{6,7},{7,6},{8,9},{9,8},{10,11... | collective-permute-start | bytes 491528 | tf_op jit(solution)/shard_map/ppermute | solution.py:288

commit v5 on v4

--- a/solution.py
+++ b/solution.py
@@ -206,7 +206,7 @@
 
 
 def finish_kernel(starts, *refs):
-    second_ref = refs[10]
+    second_ref = refs[5 * len(starts)]
     out_ref, retained, rows_ref, sems = refs[-4:]
     blocks = out_ref.shape[0] // BLOCK
     half = out_ref.shape[1] // BLOCK // 2
@@ -233,8 +233,8 @@
                 variance = jnp.mean(parted * parted, axis=-1, keepdims=True)
                 mixed_rows = silu_ref[rows, columns(g)] * (parted * lax.rsqrt(variance + EPSILON))
                 rows_ref[rows, here] = mixed_rows.astype(BF16)
-        target = out_ref.at[:, span(real_head(start, half), count)]
-        stores.append(fetch(rows_ref.at[:, columns(done, count)], target, sems.at[j]))
+            target = out_ref.at[:, span(real_head(start, half) + g, 1)]
+            stores.append(fetch(rows_ref.at[:, here], target, sems.at[done + g]))
         done += count
     for copy in stores:
         copy.wait()
@@ -242,21 +242,21 @@
 
 def finish(starts, parts, carries, second, into=None):
     length = parts[0][0].shape[0]
-    width = 2 * carries[0].shape[0] * BLOCK
+    width = sum(carry.shape[0] for carry in carries) * BLOCK
     features = second.shape[0] * BLOCK
     operands = [x for part, carry in zip(parts, carries) for x in (*part, carry)] + [second]
     operands += [] if into is None else [into]
     return pl.pallas_call(
         functools.partial(finish_kernel, starts),
-        in_specs=[HERE] * 11 + ([] if into is None else [ANY]),
+        in_specs=[HERE] * (len(operands) - (into is not None)) + ([] if into is None else [ANY]),
         out_specs=ANY,
         out_shape=jax.ShapeDtypeStruct((length, features), BF16),
         scratch_shapes=[
             pltpu.VMEM((length, width), F32),
             pltpu.VMEM((length, width), BF16),
-            pltpu.SemaphoreType.DMA((2,)),
+            pltpu.SemaphoreType.DMA((width // BLOCK,)),
         ],
-        input_output_aliases={} if into is None else {11: 0},
+        input_output_aliases={} if into is None else {len(operands) - 1: 0},
         compiler_params=pltpu.CompilerParams(vmem_limit_bytes=10 * MIB),
         name=f"finish_{starts[0]}",
     )(*operands)
@@ -342,7 +342,8 @@
         kept_b, sent_b = shared(early, got_b)
         out = finish((0, half), (part0, part2), (kept_b, sent_b), second)
     kept_a, sent_a = shared(late, got_a)
-    return finish((few, half + few), (part1, part3), (kept_a, sent_a), second, out)
+    out = finish((few,), (part1,), (kept_a,), second, out)
+    return finish((half + few,), (part3,), (sent_a,), second, out)
 
 
 def solution(mesh):

time: 33.6 us -> 33.4 us (level)
  waiting for transfers between devices: 11.4 us -> 10.4 us
  Pallas kernels: 12 us -> 12.8 us
    ppermute x3, waiting for transfers between devices: 2.66 us -> 1.63 us  [per_device(): swap = lambda x: lax.ppermute(x, 'rep', [(0, 1), (1, 0)])]
    pallas_call x2 -> x3, Pallas kernels: 3.29 us -> 4.08 us  [finish(): pl.pallas_call(functools.partial(finish_kernel, starts), in_specs=[HERE]...]
  transfers between devices with their start and end apart: 11 -> 11, of which waited for: 5 -> 4; matrix products, arithmetic and copies ran while one was open for 2% -> 2% of each run, Pallas kernels for 20% -> 24%
where the time goes in v5:
time: 33.4 us; the launch traced here: 33.2 us
  Pallas kernels  12.8 us (38%)
  waiting for transfers between devices  10.4 us (31%)
  starting transfers between devices  8.67 us (26%)
  other arithmetic  0.91 us (3%)
    ppermute x6, waiting for transfers between devices, per_device(): hop = lambda x, i: lax.ppermute(x, 'ctx', [(i, i + 1)])  8.78 us
    ppermute x6, starting transfers between devices, per_device(): hop = lambda x, i: lax.ppermute(x, 'ctx', [(i, i + 1)])  5.27 us
    pallas_call x4, Pallas kernels, local_part(): pl.pallas_call(functools.partial(local_kernel, start), in_specs=[HERE] *...  5.1 us
    pallas_call x3, Pallas kernels, finish(): pl.pallas_call(functools.partial(finish_kernel, starts), in_specs=[HERE]...  4.08 us
    pallas_call x1, Pallas kernels, block_states(): pl.pallas_call(states_kernel, in_specs=[ANY] * 4, out_specs=[HERE] * 7, o...  3.57 us
    ppermute x2, starting transfers between devices, per_device(): onward = lambda x, pairs: lax.ppermute(x, ('ctx', 'rep'), pairs)  1.98 us
    ppermute x3, waiting for transfers between devices, per_device(): swap = lambda x: lax.ppermute(x, 'rep', [(0, 1), (1, 0)])  1.63 us
    ppermute x3, starting transfers between devices, per_device(): swap = lambda x: lax.ppermute(x, 'rep', [(0, 1), (1, 0)])  1.42 us
  transfers between devices with their start and end apart: 11, of which 4 were waited for; matrix products, arithmetic and copies ran while one was open for 2% of the time, Pallas kernels for 24%

profile of v5, /device:TPU:25, one launch (start us, length us, event | category | flops | bytes accessed | tf_op | source)
XLA Modules:
  0.0 33.2 jit_solution(16360137670999056104)
XLA Ops:
  0.0 3.6 %block_states.1 = (bf16[10,128,128]{2,1,0:T(8,128)(2,1)S(1)}, bf16[10,128,128]{2,1,0:T(8,128)(2,1)S(1)}, bf16[20,128,128]{2,1,0:T(8,128)(2,1)S(1)}, bf16[384,256...) custom-call(f32[20]{0:T(128)} %rate_in.1, ...), custom_call_target="tpu_custom_call" | custom-call | tf_op jit(solution)/shard_map/block_states/pallas_call | solution.py:127
  3.6 0.7 %collective-permute-start = (bf16[10,128,128]{2,1,0:T(8,128)(2,1)S(1)}, bf16[10,128,128]{2,1,0:T(8,128)(2,1)S(1)}, u32[]{:S(2)}, u32[]{:S(2)}) collective-permute-start(bf16[10,128,128]{2,1,0:T(8,128)(2,1)S(1)} %get-tuple-element.44), channel_id=1, source_target_pairs={{0,1},{1,0},{2,3},{3,2},{4,5},{5,4},{6,7},{7,6},{8,9},{9,8},{10,11... | collective-permute-start | bytes 983048 | tf_op jit(solution)/shard_map/ppermute | solution.py:288
  4.3 0.7 %collective-permute-start.3 = (bf16[20,128,128]{2,1,0:T(8,128)(2,1)S(1)}, bf16[20,128,128]{2,1,0:T(8,128)(2,1)S(1)}, u32[]{:S(2)}, u32[]{:S(2)}) collective-permute-start(bf16[20,128,128]{2,1,0:T(8,128)(2,1)S(1)} %get-tuple-element.67), channel_id=1, source_target_pairs={{5,8},{7,10},{21,24},{23,26}} | collective-permute-start | bytes 1966088 | tf_op jit(solution)/shard_map/ppermute | solution.py:290
  5.1 0.5 %collective-permute-done = bf16[10,128,128]{2,1,0:T(8,128)(2,1)S(1)} collective-permute-done((bf16[10,128,128]{2,1,0:T(8,128)(2,1)S(1)}, bf16[10,128,128]{2,1,0:T(8,128)(2,1)S(1)}, u32[]{:S(2)}, u32[]{:S(2)}) %collective-permute-start) | collective-permute-done | bytes 327712 | tf_op jit(solution)/shard_map/ppermute | solution.py:288
  5.6 0.1 add_convert_fusion
  5.8 0.7 %collective-permute-start.1 = (bf16[5,128,128]{2,1,0:T(8,128)(2,1)S(1)}, bf16[5,128,128]{2,1,0:T(8,128)(2,1)S(1)}, u32[]{:S(2)}, u32[]{:S(2)}) collective-permute-start(bf16[5,128,128]{2,1,0:T(8,128)(2,1)S(1)} %get-tuple-element.84), channel_id=1, source_target_pairs={{0,4},{1,5},{2,6},{3,7},{16,20},{17,21},{18,22},{19,23}} | collective-permute-start | bytes 491528 | tf_op jit(solution)/shard_map/ppermute | solution.py:291
  6.4 0.7 %collective-permute-start.4 = (bf16[5,128,128]{2,1,0:T(8,128)(2,1)S(1)}, bf16[5,128,128]{2,1,0:T(8,128)(2,1)S(1)}, u32[]{:S(2)}, u32[]{:S(2)}) collective-permute-start(bf16[5,128,128]{2,1,0:T(8,128)(2,1)S(1)} %get-tuple-element.83), channel_id=1, source_target_pairs={{0,4},{1,5},{2,6},{3,7},{16,20},{17,21},{18,22},{19,23}} | collective-permute-start | bytes 491528 | tf_op jit(solution)/shard_map/ppermute | solution.py:291
  7.1 1.3 %collective-permute-start.8 = (bf16[20,128,128]{2,1,0:T(8,128)(2,1)S(1)}, bf16[20,128,128]{2,1,0:T(8,128)(2,1)S(1)}, u32[]{:S(2)}, u32[]{:S(2)}) collective-permute-start(bf16[20,128,128]{2,1,0:T(8,128)(2,1)S(1)} %get-tuple-element.67), channel_id=1, source_target_pairs={{0,1},{1,4},{4,5},{8,9},{9,12},{12,13},{2,3},{3,6},{6,7},{10,11},{... | collective-permute-start | bytes 1966088 | tf_op jit(solution)/shard_map/ppermute | solution.py:290
  8.5 1.3 %local_0.1 = (f32[384,640]{1,0:T(8,128)S(1)}, bf16[384,640]{1,0:T(8,128)(2,1)S(1)}, bf16[128,640]{1,0:T(8,128)(2,1)S(1)}, f32[384,640]{1,0:T(8,128)S(1)}) custom-call(f32[20,128]{1,0:T(8,128)S(1)} %bitcast.27, bf16[384,2560]{1,0:T(8,128)(2,1)S(1)} %copy-done, bf16[384,2560]{1,0:T(8,128)(2,1)S(1)} %copy-done.1, ...), custom_call_target="tpu_custom_call" | custom-call | flops 1 | bytes 1 | tf_op jit(solution)/shard_map/local_0/pallas_call | solution.py:194
  9.7 0.0 collective-permute-done.1
  9.8 0.1 fusion
  9.8 0.7 %collective-permute-start.2 = (bf16[5,128,128]{2,1,0:T(8,128)(2,1)S(1)}, bf16[5,128,128]{2,1,0:T(8,128)(2,1)S(1)}, u32[]{:S(2)}, u32[]{:S(2)}) collective-permute-start(bf16[5,128,128]{2,1,0:T(8,128)(2,1)S(1)} %fusion), channel_id=1, source_target_pairs={{4,8},{5,9},{6,10},{7,11},{20,24},{21,25},{22,26},{23,27}} | collective-permute-start | bytes 491528 | tf_op jit(solution)/shard_map/ppermute | solution.py:291
  10.5 1.3 %local_10.1 = (f32[384,640]{1,0:T(8,128)S(1)}, bf16[384,640]{1,0:T(8,128)(2,1)S(1)}, bf16[128,640]{1,0:T(8,128)(2,1)S(1)}, f32[384,640]{1,0:T(8,128)S(1)}) custom-call(f32[20,128]{1,0:T(8,128)S(1)} %bitcast.28, bf16[384,2560]{1,0:T(8,128)(2,1)S(1)} %copy-done, bf16[384,2560]{1,0:T(8,128)(2,1)S(1)} %copy-done.1, ...), custom_call_target="tpu_custom_call" | custom-call | flops 1 | bytes 1 | tf_op jit(solution)/shard_map/local_10/pallas_call | solution.py:194
  11.8 0.1 fusion.2
  11.9 0.7 %collective-permute-start.5 = (bf16[5,128,128]{2,1,0:T(8,128)(2,1)S(1)}, bf16[5,128,128]{2,1,0:T(8,128)(2,1)S(1)}, u32[]{:S(2)}, u32[]{:S(2)}) collective-permute-start(bf16[5,128,128]{2,1,0:T(8,128)(2,1)S(1)} %fusion.2), channel_id=1, source_target_pairs={{4,8},{5,9},{6,10},{7,11},{20,24},{21,25},{22,26},{23,27}} | collective-permute-start | bytes 491528 | tf_op jit(solution)/shard_map/ppermute | solution.py:291
  12.5 1.3 %local_5.1 = (f32[384,640]{1,0:T(8,128)S(1)}, bf16[384,640]{1,0:T(8,128)(2,1)S(1)}, bf16[128,640]{1,0:T(8,128)(2,1)S(1)}, f32[384,640]{1,0:T(8,128)S(1)}) custom-call(f32[20,128]{1,0:T(8,128)S(1)} %bitcast.29, bf16[384,2560]{1,0:T(8,128)(2,1)S(1)} %copy-done, bf16[384,2560]{1,0:T(8,128)(2,1)S(1)} %copy-done.1, ...), custom_call_target="tpu_custom_call" | custom-call | flops 1 | bytes 1 | tf_op jit(solution)/shard_map/local_5/pallas_call | solution.py:194
  13.8 0.1 fusion.1
  13.9 1.3 %collective-permute-start.7 = (bf16[5,128,128]{2,1,0:T(8,128)(2,1)S(1)}, bf16[5,128,128]{2,1,0:T(8,128)(2,1)S(1)}, u32[]{:S(2)}, u32[]{:S(2)}) collective-permute-start(bf16[5,128,128]{2,1,0:T(8,128)(2,1)S(1)} %fusion.1), channel_id=1, source_target_pairs={{8,12},{9,13},{10,14},{11,15},{24,28},{25,29},{26,30},{27,31}} | collective-permute-start | bytes 491528 | tf_op jit(solution)/shard_map/ppermute | solution.py:291
  15.2 1.3 %local_15.1 = (f32[384,640]{1,0:T(8,128)S(1)}, bf16[384,640]{1,0:T(8,128)(2,1)S(1)}, bf16[128,640]{1,0:T(8,128)(2,1)S(1)}, f32[384,640]{1,0:T(8,128)S(1)}) custom-call(f32[20,128]{1,0:T(8,128)S(1)} %bitcast.30, bf16[384,2560]{1,0:T(8,128)(2,1)S(1)} %copy-done, bf16[384,2560]{1,0:T(8,128)(2,1)S(1)} %copy-done.1, ...), custom_call_target="tpu_custom_call" | custom-call | flops 1 | bytes 1 | tf_op jit(solution)/shard_map/local_15/pallas_call | solution.py:194
  16.5 0.1 fusion.3
  16.6 1.3 %collective-permute-start.6 = (bf16[5,128,128]{2,1,0:T(8,128)(2,1)S(1)}, bf16[5,128,128]{2,1,0:T(8,128)(2,1)S(1)}, u32[]{:S(2)}, u32[]{:S(2)}) collective-permute-start(bf16[5,128,128]{2,1,0:T(8,128)(2,1)S(1)} %fusion.3), channel_id=1, source_target_pairs={{8,12},{9,13},{10,14},{11,15},{24,28},{25,29},{26,30},{27,31}} | collective-permute-start | bytes 491528 | tf_op jit(solution)/shard_map/ppermute | solution.py:291
  17.9 7.6 %collective-permute-done.7 = bf16[5,128,128]{2,1,0:T(8,128)(2,1)S(1)} collective-permute-done((bf16[5,128,128]{2,1,0:T(8,128)(2,1)S(1)}, bf16[5,128,128]{2,1,0:T(8,128)(2,1)S(1)}, u32[]{:S(2)}, u32[]{:S(2)}) %collective-permute-start.7) | collective-permute-done | bytes 163872 | tf_op jit(solution)/shard_map/ppermute | solution.py:291
  25.5 0.2 fusion.7
  25.6 0.1 collective-permute-start.9
  25.7 0.2 add.52.refs_10_.refs_5_
  25.9 1.2 %collective-permute-done.9.refs_9_ = bf16[5,128,128]{2,1,0:T(8,128)(2,1)S(1)} collective-permute-done((bf16[5,128,128]{2,1,0:T(8,128)(2,1)S(1)}, bf16[5,128,128]{2,1,0:T(8,128)(2,1)S(1)}, u32[]{:S(2)}, u32[]{:S(2)}) %collective-permute-start.9) | collective-permute-done | bytes 163872 | tf_op jit(solution)/shard_map/ppermute | solution.py:288
  27.1 1.6 %finish_0.1.refs_6_ = bf16[384,2560]{1,0:T(8,128)(2,1)} custom-call(f32[384,640]{1,0:T(8,128)S(1)} %get-tuple-element.49.refs_0_, bf16[384,640]{1,0:T(8,128)(2,1)S(1)} %get-tuple-element.64.refs_1_, bf16[128,640]{1,0:T(8,128)(2,1)S(1)} %get-tuple-element.65.refs_2_, f32[384,640]{1,0:T(8,128)S(1)} %get-tuple-element.66.refs_3_, ...), custom_call_target="tpu_custom_call" | custom-call | tf_op jit(solution)/shard_map/finish_0/pallas_call | solution.py:249
  28.7 1.2 %collective-permute-done.6 = bf16[5,128,128]{2,1,0:T(8,128)(2,1)S(1)} collective-permute-done((bf16[5,128,128]{2,1,0:T(8,128)(2,1)S(1)}, bf16[5,128,128]{2,1,0:T(8,128)(2,1)S(1)}, u32[]{:S(2)}, u32[]{:S(2)}) %collective-permute-start.6) | collective-permute-done | bytes 163872 | tf_op jit(solution)/shard_map/ppermute | solution.py:291
  29.9 0.2 fusion.11
  30.1 0.6 %collective-permute-start.10 = (bf16[5,128,128]{2,1,0:T(8,128)(2,1)S(1)}, bf16[5,128,128]{2,1,0:T(8,128)(2,1)S(1)}, u32[]{:S(2)}, u32[]{:S(2)}) collective-permute-start(bf16[5,128,128]{2,1,0:T(8,128)(2,1)S(1)} %get-tuple-element.80), channel_id=1, source_target_pairs={{0,1},{1,0},{2,3},{3,2},{4,5},{5,4},{6,7},{7,6},{8,9},{9,8},{10,11... | collective-permute-start | bytes 491528 | tf_op jit(solution)/shard_map/ppermute | solution.py:288
  30.7 1.2 %finish_5.1.refs_6_ = bf16[384,2560]{1,0:T(8,128)(2,1)} custom-call(f32[384,640]{1,0:T(8,128)S(1)} %get-tuple-element.56.refs_0_, bf16[384,640]{1,0:T(8,128)(2,1)S(1)} %get-tuple-element.75.refs_1_, bf16[128,640]{1,0:T(8,128)(2,1)S(1)} %get-tuple-element.76.refs_2_, f32[384,640]{1,0:T(8,128)S(1)} %get-tuple-element.77.refs_3_, ...), custom_call_target="tpu_custom_call", output_to_operand_aliasing={{}: (6, {})} | custom-call | tf_op jit(solution)/shard_map/finish_5/pallas_call | solution.py:249
  31.9 1.2 %finish_15.1 = bf16[384,2560]{1,0:T(8,128)(2,1)} custom-call(f32[384,640]{1,0:T(8,128)S(1)} %get-tuple-element.59.refs_0_, bf16[384,640]{1,0:T(8,128)(2,1)S(1)} %get-tuple-element.60.refs_1_, bf16[128,640]{1,0:T(8,128)(2,1)S(1)} %get-tuple-element.61.refs_2_, f32[384,640]{1,0:T(8,128)S(1)} %get-tuple-element.62.refs_3_, ...), custom_call_target="tpu_custom_call", output_to_operand_aliasing={{}: (6, {})} | custom-call | tf_op jit(solution)/shard_map/finish_15/pallas_call | solution.py:249
  (22 shorter events, 0.1 us)
Async XLA Ops:
  0.0 8.4 %copy-start = (bf16[384,2560]{1,0:T(8,128)(2,1)S(1)}, bf16[384,2560]{1,0:T(8,128)(2,1)}, u32[]{:S(2)}) copy-start(bf16[384,2560]{1,0:T(8,128)(2,1)} %q_ref.3) | copy-start | bytes 5898244
  0.0 8.4 %copy-start.2 = (f32[2560]{0:T(1024)S(1)}, f32[2560]{0:T(1024)}, u32[]{:S(2)}) copy-start(f32[2560]{0:T(1024)} %param.11) | copy-start | bytes 30724
  0.0 8.4 %copy-start.1 = (bf16[384,2560]{1,0:T(8,128)(2,1)S(1)}, bf16[384,2560]{1,0:T(8,128)(2,1)}, u32[]{:S(2)}) copy-start(bf16[384,2560]{1,0:T(8,128)(2,1)} %g_ref.7) | copy-start | bytes 5898244
  3.6 2.0 %collective-permute-start = (bf16[10,128,128]{2,1,0:T(8,128)(2,1)S(1)}, bf16[10,128,128]{2,1,0:T(8,128)(2,1)S(1)}, u32[]{:S(2)}, u32[]{:S(2)}) collective-permute-start(bf16[10,128,128]{2,1,0:T(8,128)(2,1)S(1)} %get-tuple-element.44), channel_id=1, source_target_pairs={{0,1},{1,0},{2,3},{3,2},{4,5},{5,4},{6,7},{7,6},{8,9},{9,8},{10,11... | collective-permute-start | bytes 983048 | tf_op jit(solution)/shard_map/ppermute | solution.py:288
  4.3 9.5 %collective-permute-start.3 = (bf16[20,128,128]{2,1,0:T(8,128)(2,1)S(1)}, bf16[20,128,128]{2,1,0:T(8,128)(2,1)S(1)}, u32[]{:S(2)}, u32[]{:S(2)}) collective-permute-start(bf16[20,128,128]{2,1,0:T(8,128)(2,1)S(1)} %get-tuple-element.67), channel_id=1, source_target_pairs={{5,8},{7,10},{21,24},{23,26}} | collective-permute-start | bytes 1966088 | tf_op jit(solution)/shard_map/ppermute | solution.py:290
  5.8 4.0 %collective-permute-start.1 = (bf16[5,128,128]{2,1,0:T(8,128)(2,1)S(1)}, bf16[5,128,128]{2,1,0:T(8,128)(2,1)S(1)}, u32[]{:S(2)}, u32[]{:S(2)}) collective-permute-start(bf16[5,128,128]{2,1,0:T(8,128)(2,1)S(1)} %get-tuple-element.84), channel_id=1, source_target_pairs={{0,4},{1,5},{2,6},{3,7},{16,20},{17,21},{18,22},{19,23}} | collective-permute-start | bytes 491528 | tf_op jit(solution)/shard_map/ppermute | solution.py:291
  6.4 5.3 %collective-permute-start.4 = (bf16[5,128,128]{2,1,0:T(8,128)(2,1)S(1)}, bf16[5,128,128]{2,1,0:T(8,128)(2,1)S(1)}, u32[]{:S(2)}, u32[]{:S(2)}) collective-permute-start(bf16[5,128,128]{2,1,0:T(8,128)(2,1)S(1)} %get-tuple-element.83), channel_id=1, source_target_pairs={{0,4},{1,5},{2,6},{3,7},{16,20},{17,21},{18,22},{19,23}} | collective-permute-start | bytes 491528 | tf_op jit(solution)/shard_map/ppermute | solution.py:291
  7.1 18.3 %collective-permute-start.8 = (bf16[20,128,128]{2,1,0:T(8,128)(2,1)S(1)}, bf16[20,128,128]{2,1,0:T(8,128)(2,1)S(1)}, u32[]{:S(2)}, u32[]{:S(2)}) collective-permute-start(bf16[20,128,128]{2,1,0:T(8,128)(2,1)S(1)} %get-tuple-element.67), channel_id=1, source_target_pairs={{0,1},{1,4},{4,5},{8,9},{9,12},{12,13},{2,3},{3,6},{6,7},{10,11},{... | collective-permute-start | bytes 1966088 | tf_op jit(solution)/shard_map/ppermute | solution.py:290
  9.8 4.0 %collective-permute-start.2 = (bf16[5,128,128]{2,1,0:T(8,128)(2,1)S(1)}, bf16[5,128,128]{2,1,0:T(8,128)(2,1)S(1)}, u32[]{:S(2)}, u32[]{:S(2)}) collective-permute-start(bf16[5,128,128]{2,1,0:T(8,128)(2,1)S(1)} %fusion), channel_id=1, source_target_pairs={{4,8},{5,9},{6,10},{7,11},{20,24},{21,25},{22,26},{23,27}} | collective-permute-start | bytes 491528 | tf_op jit(solution)/shard_map/ppermute | solution.py:291
  11.9 4.6 %collective-permute-start.5 = (bf16[5,128,128]{2,1,0:T(8,128)(2,1)S(1)}, bf16[5,128,128]{2,1,0:T(8,128)(2,1)S(1)}, u32[]{:S(2)}, u32[]{:S(2)}) collective-permute-start(bf16[5,128,128]{2,1,0:T(8,128)(2,1)S(1)} %fusion.2), channel_id=1, source_target_pairs={{4,8},{5,9},{6,10},{7,11},{20,24},{21,25},{22,26},{23,27}} | collective-permute-start | bytes 491528 | tf_op jit(solution)/shard_map/ppermute | solution.py:291
  13.9 11.6 %collective-permute-start.7 = (bf16[5,128,128]{2,1,0:T(8,128)(2,1)S(1)}, bf16[5,128,128]{2,1,0:T(8,128)(2,1)S(1)}, u32[]{:S(2)}, u32[]{:S(2)}) collective-permute-start(bf16[5,128,128]{2,1,0:T(8,128)(2,1)S(1)} %fusion.1), channel_id=1, source_target_pairs={{8,12},{9,13},{10,14},{11,15},{24,28},{25,29},{26,30},{27,31}} | collective-permute-start | bytes 491528 | tf_op jit(solution)/shard_map/ppermute | solution.py:291
  16.6 13.3 %collective-permute-start.6 = (bf16[5,128,128]{2,1,0:T(8,128)(2,1)S(1)}, bf16[5,128,128]{2,1,0:T(8,128)(2,1)S(1)}, u32[]{:S(2)}, u32[]{:S(2)}) collective-permute-start(bf16[5,128,128]{2,1,0:T(8,128)(2,1)S(1)} %fusion.3), channel_id=1, source_target_pairs={{8,12},{9,13},{10,14},{11,15},{24,28},{25,29},{26,30},{27,31}} | collective-permute-start | bytes 491528 | tf_op jit(solution)/shard_map/ppermute | solution.py:291
  25.6 1.5 %collective-permute-start.9 = (bf16[5,128,128]{2,1,0:T(8,128)(2,1)S(1)}, bf16[5,128,128]{2,1,0:T(8,128)(2,1)S(1)}, u32[]{:S(2)}, u32[]{:S(2)}) collective-permute-start(bf16[5,128,128]{2,1,0:T(8,128)(2,1)S(1)} %get-tuple-element.81), channel_id=1, source_target_pairs={{0,1},{1,0},{2,3},{3,2},{4,5},{5,4},{6,7},{7,6},{8,9},{9,8},{10,11... | collective-permute-start | bytes 491528 | tf_op jit(solution)/shard_map/ppermute | solution.py:288
  30.1 1.8 %collective-permute-start.10 = (bf16[5,128,128]{2,1,0:T(8,128)(2,1)S(1)}, bf16[5,128,128]{2,1,0:T(8,128)(2,1)S(1)}, u32[]{:S(2)}, u32[]{:S(2)}) collective-permute-start(bf16[5,128,128]{2,1,0:T(8,128)(2,1)S(1)} %get-tuple-element.80), channel_id=1, source_target_pairs={{0,1},{1,0},{2,3},{3,2},{4,5},{5,4},{6,7},{7,6},{8,9},{9,8},{10,11... | collective-permute-start | bytes 491528 | tf_op jit(solution)/shard_map/ppermute | solution.py:288

commit v6 on v5

--- a/solution.py
+++ b/solution.py
@@ -13,7 +13,7 @@
 F32 = jnp.float32
 BF16 = jnp.bfloat16
 MIB = 1024 * 1024
-CHUNK = 5
+CHUNK = 10
 TRANS = (((0,), (0,)), ((), ()))
 ROWS = (((1,), (1,)), ((), ()))
 ANY = pl.BlockSpec(memory_space=pl.ANY)

time: 33.4 us -> 33.2 us (level)
  no operation moved by 1% of the time
where the time goes in v6:
time: 33.2 us; the launch traced here: 33 us
  Pallas kernels  12.6 us (38%)
  waiting for transfers between devices  10.4 us (31%)
  starting transfers between devices  8.67 us (26%)
  other arithmetic  0.91 us (3%)
    ppermute x6, waiting for transfers between devices, per_device(): hop = lambda x, i: lax.ppermute(x, 'ctx', [(i, i + 1)])  8.78 us
    ppermute x6, starting transfers between devices, per_device(): hop = lambda x, i: lax.ppermute(x, 'ctx', [(i, i + 1)])  5.27 us
    pallas_call x4, Pallas kernels, local_part(): pl.pallas_call(functools.partial(local_kernel, start), in_specs=[HERE] *...  5.1 us
    pallas_call x3, Pallas kernels, finish(): pl.pallas_call(functools.partial(finish_kernel, starts), in_specs=[HERE]...  4.08 us
    pallas_call x1, Pallas kernels, block_states(): pl.pallas_call(states_kernel, in_specs=[ANY] * 4, out_specs=[HERE] * 7, o...  3.4 us
    ppermute x2, starting transfers between devices, per_device(): onward = lambda x, pairs: lax.ppermute(x, ('ctx', 'rep'), pairs)  1.98 us
    ppermute x3, waiting for transfers between devices, per_device(): swap = lambda x: lax.ppermute(x, 'rep', [(0, 1), (1, 0)])  1.63 us
    ppermute x3, starting transfers between devices, per_device(): swap = lambda x: lax.ppermute(x, 'rep', [(0, 1), (1, 0)])  1.42 us
  transfers between devices with their start and end apart: 11, of which 4 were waited for; matrix products, arithmetic and copies ran while one was open for 2% of the time, Pallas kernels for 24%

profile of v6, /device:TPU:25, one launch (start us, length us, event | category | flops | bytes accessed | tf_op | source)
XLA Modules:
  0.0 33.0 jit_solution(10356036016198510764)
XLA Ops:
  0.0 3.4 %block_states.1 = (bf16[10,128,128]{2,1,0:T(8,128)(2,1)S(1)}, bf16[10,128,128]{2,1,0:T(8,128)(2,1)S(1)}, bf16[20,128,128]{2,1,0:T(8,128)(2,1)S(1)}, bf16[384,256...) custom-call(f32[20]{0:T(128)} %rate_in.1, ...), custom_call_target="tpu_custom_call" | custom-call | tf_op jit(solution)/shard_map/block_states/pallas_call | solution.py:127
  3.4 0.7 %collective-permute-start = (bf16[10,128,128]{2,1,0:T(8,128)(2,1)S(1)}, bf16[10,128,128]{2,1,0:T(8,128)(2,1)S(1)}, u32[]{:S(2)}, u32[]{:S(2)}) collective-permute-start(bf16[10,128,128]{2,1,0:T(8,128)(2,1)S(1)} %get-tuple-element.44), channel_id=1, source_target_pairs={{0,1},{1,0},{2,3},{3,2},{4,5},{5,4},{6,7},{7,6},{8,9},{9,8},{10,11... | collective-permute-start | bytes 983048 | tf_op jit(solution)/shard_map/ppermute | solution.py:288
  4.2 0.7 %collective-permute-start.3 = (bf16[20,128,128]{2,1,0:T(8,128)(2,1)S(1)}, bf16[20,128,128]{2,1,0:T(8,128)(2,1)S(1)}, u32[]{:S(2)}, u32[]{:S(2)}) collective-permute-start(bf16[20,128,128]{2,1,0:T(8,128)(2,1)S(1)} %get-tuple-element.67), channel_id=1, source_target_pairs={{5,8},{7,10},{21,24},{23,26}} | collective-permute-start | bytes 1966088 | tf_op jit(solution)/shard_map/ppermute | solution.py:290
  4.9 0.5 %collective-permute-done = bf16[10,128,128]{2,1,0:T(8,128)(2,1)S(1)} collective-permute-done((bf16[10,128,128]{2,1,0:T(8,128)(2,1)S(1)}, bf16[10,128,128]{2,1,0:T(8,128)(2,1)S(1)}, u32[]{:S(2)}, u32[]{:S(2)}) %collective-permute-start) | collective-permute-done | bytes 327712 | tf_op jit(solution)/shard_map/ppermute | solution.py:288
  5.4 0.1 add_convert_fusion
  5.6 0.7 %collective-permute-start.1 = (bf16[5,128,128]{2,1,0:T(8,128)(2,1)S(1)}, bf16[5,128,128]{2,1,0:T(8,128)(2,1)S(1)}, u32[]{:S(2)}, u32[]{:S(2)}) collective-permute-start(bf16[5,128,128]{2,1,0:T(8,128)(2,1)S(1)} %get-tuple-element.84), channel_id=1, source_target_pairs={{0,4},{1,5},{2,6},{3,7},{16,20},{17,21},{18,22},{19,23}} | collective-permute-start | bytes 491528 | tf_op jit(solution)/shard_map/ppermute | solution.py:291
  6.3 0.7 %collective-permute-start.4 = (bf16[5,128,128]{2,1,0:T(8,128)(2,1)S(1)}, bf16[5,128,128]{2,1,0:T(8,128)(2,1)S(1)}, u32[]{:S(2)}, u32[]{:S(2)}) collective-permute-start(bf16[5,128,128]{2,1,0:T(8,128)(2,1)S(1)} %get-tuple-element.83), channel_id=1, source_target_pairs={{0,4},{1,5},{2,6},{3,7},{16,20},{17,21},{18,22},{19,23}} | collective-permute-start | bytes 491528 | tf_op jit(solution)/shard_map/ppermute | solution.py:291
  7.0 1.3 %collective-permute-start.8 = (bf16[20,128,128]{2,1,0:T(8,128)(2,1)S(1)}, bf16[20,128,128]{2,1,0:T(8,128)(2,1)S(1)}, u32[]{:S(2)}, u32[]{:S(2)}) collective-permute-start(bf16[20,128,128]{2,1,0:T(8,128)(2,1)S(1)} %get-tuple-element.67), channel_id=1, source_target_pairs={{0,1},{1,4},{4,5},{8,9},{9,12},{12,13},{2,3},{3,6},{6,7},{10,11},{... | collective-permute-start | bytes 1966088 | tf_op jit(solution)/shard_map/ppermute | solution.py:290
  8.3 1.3 %local_0.1 = (f32[384,640]{1,0:T(8,128)S(1)}, bf16[384,640]{1,0:T(8,128)(2,1)S(1)}, bf16[128,640]{1,0:T(8,128)(2,1)S(1)}, f32[384,640]{1,0:T(8,128)S(1)}) custom-call(f32[20,128]{1,0:T(8,128)S(1)} %bitcast.27, bf16[384,2560]{1,0:T(8,128)(2,1)S(1)} %copy-done, bf16[384,2560]{1,0:T(8,128)(2,1)S(1)} %copy-done.1, ...), custom_call_target="tpu_custom_call" | custom-call | flops 1 | bytes 1 | tf_op jit(solution)/shard_map/local_0/pallas_call | solution.py:194
  9.6 0.1 fusion
  9.7 0.7 %collective-permute-start.2 = (bf16[5,128,128]{2,1,0:T(8,128)(2,1)S(1)}, bf16[5,128,128]{2,1,0:T(8,128)(2,1)S(1)}, u32[]{:S(2)}, u32[]{:S(2)}) collective-permute-start(bf16[5,128,128]{2,1,0:T(8,128)(2,1)S(1)} %fusion), channel_id=1, source_target_pairs={{4,8},{5,9},{6,10},{7,11},{20,24},{21,25},{22,26},{23,27}} | collective-permute-start | bytes 491528 | tf_op jit(solution)/shard_map/ppermute | solution.py:291
  10.3 1.3 %local_10.1 = (f32[384,640]{1,0:T(8,128)S(1)}, bf16[384,640]{1,0:T(8,128)(2,1)S(1)}, bf16[128,640]{1,0:T(8,128)(2,1)S(1)}, f32[384,640]{1,0:T(8,128)S(1)}) custom-call(f32[20,128]{1,0:T(8,128)S(1)} %bitcast.28, bf16[384,2560]{1,0:T(8,128)(2,1)S(1)} %copy-done, bf16[384,2560]{1,0:T(8,128)(2,1)S(1)} %copy-done.1, ...), custom_call_target="tpu_custom_call" | custom-call | flops 1 | bytes 1 | tf_op jit(solution)/shard_map/local_10/pallas_call | solution.py:194
  11.6 0.1 fusion.2
  11.7 0.7 %collective-permute-start.5 = (bf16[5,128,128]{2,1,0:T(8,128)(2,1)S(1)}, bf16[5,128,128]{2,1,0:T(8,128)(2,1)S(1)}, u32[]{:S(2)}, u32[]{:S(2)}) collective-permute-start(bf16[5,128,128]{2,1,0:T(8,128)(2,1)S(1)} %fusion.2), channel_id=1, source_target_pairs={{4,8},{5,9},{6,10},{7,11},{20,24},{21,25},{22,26},{23,27}} | collective-permute-start | bytes 491528 | tf_op jit(solution)/shard_map/ppermute | solution.py:291
  12.4 1.3 %local_5.1 = (f32[384,640]{1,0:T(8,128)S(1)}, bf16[384,640]{1,0:T(8,128)(2,1)S(1)}, bf16[128,640]{1,0:T(8,128)(2,1)S(1)}, f32[384,640]{1,0:T(8,128)S(1)}) custom-call(f32[20,128]{1,0:T(8,128)S(1)} %bitcast.29, bf16[384,2560]{1,0:T(8,128)(2,1)S(1)} %copy-done, bf16[384,2560]{1,0:T(8,128)(2,1)S(1)} %copy-done.1, ...), custom_call_target="tpu_custom_call" | custom-call | flops 1 | bytes 1 | tf_op jit(solution)/shard_map/local_5/pallas_call | solution.py:194
  13.6 0.0 collective-permute-done.2
  13.7 0.1 fusion.1
  13.7 1.3 %collective-permute-start.7 = (bf16[5,128,128]{2,1,0:T(8,128)(2,1)S(1)}, bf16[5,128,128]{2,1,0:T(8,128)(2,1)S(1)}, u32[]{:S(2)}, u32[]{:S(2)}) collective-permute-start(bf16[5,128,128]{2,1,0:T(8,128)(2,1)S(1)} %fusion.1), channel_id=1, source_target_pairs={{8,12},{9,13},{10,14},{11,15},{24,28},{25,29},{26,30},{27,31}} | collective-permute-start | bytes 491528 | tf_op jit(solution)/shard_map/ppermute | solution.py:291
  15.0 1.3 %local_15.1 = (f32[384,640]{1,0:T(8,128)S(1)}, bf16[384,640]{1,0:T(8,128)(2,1)S(1)}, bf16[128,640]{1,0:T(8,128)(2,1)S(1)}, f32[384,640]{1,0:T(8,128)S(1)}) custom-call(f32[20,128]{1,0:T(8,128)S(1)} %bitcast.30, bf16[384,2560]{1,0:T(8,128)(2,1)S(1)} %copy-done, bf16[384,2560]{1,0:T(8,128)(2,1)S(1)} %copy-done.1, ...), custom_call_target="tpu_custom_call" | custom-call | flops 1 | bytes 1 | tf_op jit(solution)/shard_map/local_15/pallas_call | solution.py:194
  16.3 0.1 fusion.3
  16.4 1.3 %collective-permute-start.6 = (bf16[5,128,128]{2,1,0:T(8,128)(2,1)S(1)}, bf16[5,128,128]{2,1,0:T(8,128)(2,1)S(1)}, u32[]{:S(2)}, u32[]{:S(2)}) collective-permute-start(bf16[5,128,128]{2,1,0:T(8,128)(2,1)S(1)} %fusion.3), channel_id=1, source_target_pairs={{8,12},{9,13},{10,14},{11,15},{24,28},{25,29},{26,30},{27,31}} | collective-permute-start | bytes 491528 | tf_op jit(solution)/shard_map/ppermute | solution.py:291
  17.7 7.6 %collective-permute-done.7 = bf16[5,128,128]{2,1,0:T(8,128)(2,1)S(1)} collective-permute-done((bf16[5,128,128]{2,1,0:T(8,128)(2,1)S(1)}, bf16[5,128,128]{2,1,0:T(8,128)(2,1)S(1)}, u32[]{:S(2)}, u32[]{:S(2)}) %collective-permute-start.7) | collective-permute-done | bytes 163872 | tf_op jit(solution)/shard_map/ppermute | solution.py:291
  25.3 0.2 fusion.7
  25.5 0.1 collective-permute-start.9
  25.6 0.2 add.52.refs_10_.refs_5_
  25.8 1.2 %collective-permute-done.9.refs_9_ = bf16[5,128,128]{2,1,0:T(8,128)(2,1)S(1)} collective-permute-done((bf16[5,128,128]{2,1,0:T(8,128)(2,1)S(1)}, bf16[5,128,128]{2,1,0:T(8,128)(2,1)S(1)}, u32[]{:S(2)}, u32[]{:S(2)}) %collective-permute-start.9) | collective-permute-done | bytes 163872 | tf_op jit(solution)/shard_map/ppermute | solution.py:288
  26.9 1.6 %finish_0.1.refs_6_ = bf16[384,2560]{1,0:T(8,128)(2,1)} custom-call(f32[384,640]{1,0:T(8,128)S(1)} %get-tuple-element.49.refs_0_, bf16[384,640]{1,0:T(8,128)(2,1)S(1)} %get-tuple-element.64.refs_1_, bf16[128,640]{1,0:T(8,128)(2,1)S(1)} %get-tuple-element.65.refs_2_, f32[384,640]{1,0:T(8,128)S(1)} %get-tuple-element.66.refs_3_, ...), custom_call_target="tpu_custom_call" | custom-call | tf_op jit(solution)/shard_map/finish_0/pallas_call | solution.py:249
  28.6 1.2 %collective-permute-done.6 = bf16[5,128,128]{2,1,0:T(8,128)(2,1)S(1)} collective-permute-done((bf16[5,128,128]{2,1,0:T(8,128)(2,1)S(1)}, bf16[5,128,128]{2,1,0:T(8,128)(2,1)S(1)}, u32[]{:S(2)}, u32[]{:S(2)}) %collective-permute-start.6) | collective-permute-done | bytes 163872 | tf_op jit(solution)/shard_map/ppermute | solution.py:291
  29.7 0.2 fusion.11
  29.9 0.6 %collective-permute-start.10 = (bf16[5,128,128]{2,1,0:T(8,128)(2,1)S(1)}, bf16[5,128,128]{2,1,0:T(8,128)(2,1)S(1)}, u32[]{:S(2)}, u32[]{:S(2)}) collective-permute-start(bf16[5,128,128]{2,1,0:T(8,128)(2,1)S(1)} %get-tuple-element.80), channel_id=1, source_target_pairs={{0,1},{1,0},{2,3},{3,2},{4,5},{5,4},{6,7},{7,6},{8,9},{9,8},{10,11... | collective-permute-start | bytes 491528 | tf_op jit(solution)/shard_map/ppermute | solution.py:288
  30.5 1.2 %finish_5.1.refs_6_ = bf16[384,2560]{1,0:T(8,128)(2,1)} custom-call(f32[384,640]{1,0:T(8,128)S(1)} %get-tuple-element.56.refs_0_, bf16[384,640]{1,0:T(8,128)(2,1)S(1)} %get-tuple-element.75.refs_1_, bf16[128,640]{1,0:T(8,128)(2,1)S(1)} %get-tuple-element.76.refs_2_, f32[384,640]{1,0:T(8,128)S(1)} %get-tuple-element.77.refs_3_, ...), custom_call_target="tpu_custom_call", output_to_operand_aliasing={{}: (6, {})} | custom-call | tf_op jit(solution)/shard_map/finish_5/pallas_call | solution.py:249
  31.8 1.2 %finish_15.1 = bf16[384,2560]{1,0:T(8,128)(2,1)} custom-call(f32[384,640]{1,0:T(8,128)S(1)} %get-tuple-element.59.refs_0_, bf16[384,640]{1,0:T(8,128)(2,1)S(1)} %get-tuple-element.60.refs_1_, bf16[128,640]{1,0:T(8,128)(2,1)S(1)} %get-tuple-element.61.refs_2_, f32[384,640]{1,0:T(8,128)S(1)} %get-tuple-element.62.refs_3_, ...), custom_call_target="tpu_custom_call", output_to_operand_aliasing={{}: (6, {})} | custom-call | tf_op jit(solution)/shard_map/finish_15/pallas_call | solution.py:249
  (22 shorter events, 0.1 us)
Async XLA Ops:
  0.0 8.3 %copy-start = (bf16[384,2560]{1,0:T(8,128)(2,1)S(1)}, bf16[384,2560]{1,0:T(8,128)(2,1)}, u32[]{:S(2)}) copy-start(bf16[384,2560]{1,0:T(8,128)(2,1)} %q_ref.3) | copy-start | bytes 5898244
  0.0 8.3 %copy-start.2 = (f32[2560]{0:T(1024)S(1)}, f32[2560]{0:T(1024)}, u32[]{:S(2)}) copy-start(f32[2560]{0:T(1024)} %param.11) | copy-start | bytes 30724
  0.0 8.3 %copy-start.1 = (bf16[384,2560]{1,0:T(8,128)(2,1)S(1)}, bf16[384,2560]{1,0:T(8,128)(2,1)}, u32[]{:S(2)}) copy-start(bf16[384,2560]{1,0:T(8,128)(2,1)} %g_ref.7) | copy-start | bytes 5898244
  3.4 2.0 %collective-permute-start = (bf16[10,128,128]{2,1,0:T(8,128)(2,1)S(1)}, bf16[10,128,128]{2,1,0:T(8,128)(2,1)S(1)}, u32[]{:S(2)}, u32[]{:S(2)}) collective-permute-start(bf16[10,128,128]{2,1,0:T(8,128)(2,1)S(1)} %get-tuple-element.44), channel_id=1, source_target_pairs={{0,1},{1,0},{2,3},{3,2},{4,5},{5,4},{6,7},{7,6},{8,9},{9,8},{10,11... | collective-permute-start | bytes 983048 | tf_op jit(solution)/shard_map/ppermute | solution.py:288
  4.2 9.5 %collective-permute-start.3 = (bf16[20,128,128]{2,1,0:T(8,128)(2,1)S(1)}, bf16[20,128,128]{2,1,0:T(8,128)(2,1)S(1)}, u32[]{:S(2)}, u32[]{:S(2)}) collective-permute-start(bf16[20,128,128]{2,1,0:T(8,128)(2,1)S(1)} %get-tuple-element.67), channel_id=1, source_target_pairs={{5,8},{7,10},{21,24},{23,26}} | collective-permute-start | bytes 1966088 | tf_op jit(solution)/shard_map/ppermute | solution.py:290
  5.6 4.0 %collective-permute-start.1 = (bf16[5,128,128]{2,1,0:T(8,128)(2,1)S(1)}, bf16[5,128,128]{2,1,0:T(8,128)(2,1)S(1)}, u32[]{:S(2)}, u32[]{:S(2)}) collective-permute-start(bf16[5,128,128]{2,1,0:T(8,128)(2,1)S(1)} %get-tuple-element.84), channel_id=1, source_target_pairs={{0,4},{1,5},{2,6},{3,7},{16,20},{17,21},{18,22},{19,23}} | collective-permute-start | bytes 491528 | tf_op jit(solution)/shard_map/ppermute | solution.py:291
  6.3 5.3 %collective-permute-start.4 = (bf16[5,128,128]{2,1,0:T(8,128)(2,1)S(1)}, bf16[5,128,128]{2,1,0:T(8,128)(2,1)S(1)}, u32[]{:S(2)}, u32[]{:S(2)}) collective-permute-start(bf16[5,128,128]{2,1,0:T(8,128)(2,1)S(1)} %get-tuple-element.83), channel_id=1, source_target_pairs={{0,4},{1,5},{2,6},{3,7},{16,20},{17,21},{18,22},{19,23}} | collective-permute-start | bytes 491528 | tf_op jit(solution)/shard_map/ppermute | solution.py:291
  7.0 18.3 %collective-permute-start.8 = (bf16[20,128,128]{2,1,0:T(8,128)(2,1)S(1)}, bf16[20,128,128]{2,1,0:T(8,128)(2,1)S(1)}, u32[]{:S(2)}, u32[]{:S(2)}) collective-permute-start(bf16[20,128,128]{2,1,0:T(8,128)(2,1)S(1)} %get-tuple-element.67), channel_id=1, source_target_pairs={{0,1},{1,4},{4,5},{8,9},{9,12},{12,13},{2,3},{3,6},{6,7},{10,11},{... | collective-permute-start | bytes 1966088 | tf_op jit(solution)/shard_map/ppermute | solution.py:290
  9.7 4.0 %collective-permute-start.2 = (bf16[5,128,128]{2,1,0:T(8,128)(2,1)S(1)}, bf16[5,128,128]{2,1,0:T(8,128)(2,1)S(1)}, u32[]{:S(2)}, u32[]{:S(2)}) collective-permute-start(bf16[5,128,128]{2,1,0:T(8,128)(2,1)S(1)} %fusion), channel_id=1, source_target_pairs={{4,8},{5,9},{6,10},{7,11},{20,24},{21,25},{22,26},{23,27}} | collective-permute-start | bytes 491528 | tf_op jit(solution)/shard_map/ppermute | solution.py:291
  11.7 4.6 %collective-permute-start.5 = (bf16[5,128,128]{2,1,0:T(8,128)(2,1)S(1)}, bf16[5,128,128]{2,1,0:T(8,128)(2,1)S(1)}, u32[]{:S(2)}, u32[]{:S(2)}) collective-permute-start(bf16[5,128,128]{2,1,0:T(8,128)(2,1)S(1)} %fusion.2), channel_id=1, source_target_pairs={{4,8},{5,9},{6,10},{7,11},{20,24},{21,25},{22,26},{23,27}} | collective-permute-start | bytes 491528 | tf_op jit(solution)/shard_map/ppermute | solution.py:291
  13.7 11.6 %collective-permute-start.7 = (bf16[5,128,128]{2,1,0:T(8,128)(2,1)S(1)}, bf16[5,128,128]{2,1,0:T(8,128)(2,1)S(1)}, u32[]{:S(2)}, u32[]{:S(2)}) collective-permute-start(bf16[5,128,128]{2,1,0:T(8,128)(2,1)S(1)} %fusion.1), channel_id=1, source_target_pairs={{8,12},{9,13},{10,14},{11,15},{24,28},{25,29},{26,30},{27,31}} | collective-permute-start | bytes 491528 | tf_op jit(solution)/shard_map/ppermute | solution.py:291
  16.4 13.3 %collective-permute-start.6 = (bf16[5,128,128]{2,1,0:T(8,128)(2,1)S(1)}, bf16[5,128,128]{2,1,0:T(8,128)(2,1)S(1)}, u32[]{:S(2)}, u32[]{:S(2)}) collective-permute-start(bf16[5,128,128]{2,1,0:T(8,128)(2,1)S(1)} %fusion.3), channel_id=1, source_target_pairs={{8,12},{9,13},{10,14},{11,15},{24,28},{25,29},{26,30},{27,31}} | collective-permute-start | bytes 491528 | tf_op jit(solution)/shard_map/ppermute | solution.py:291
  25.5 1.5 %collective-permute-start.9 = (bf16[5,128,128]{2,1,0:T(8,128)(2,1)S(1)}, bf16[5,128,128]{2,1,0:T(8,128)(2,1)S(1)}, u32[]{:S(2)}, u32[]{:S(2)}) collective-permute-start(bf16[5,128,128]{2,1,0:T(8,128)(2,1)S(1)} %get-tuple-element.81), channel_id=1, source_target_pairs={{0,1},{1,0},{2,3},{3,2},{4,5},{5,4},{6,7},{7,6},{8,9},{9,8},{10,11... | collective-permute-start | bytes 491528 | tf_op jit(solution)/shard_map/ppermute | solution.py:288
  29.9 1.8 %collective-permute-start.10 = (bf16[5,128,128]{2,1,0:T(8,128)(2,1)S(1)}, bf16[5,128,128]{2,1,0:T(8,128)(2,1)S(1)}, u32[]{:S(2)}, u32[]{:S(2)}) collective-permute-start(bf16[5,128,128]{2,1,0:T(8,128)(2,1)S(1)} %get-tuple-element.80), channel_id=1, source_target_pairs={{0,1},{1,0},{2,3},{3,2},{4,5},{5,4},{6,7},{7,6},{8,9},{9,8},{10,11... | collective-permute-start | bytes 491528 | tf_op jit(solution)/shard_map/ppermute | solution.py:288

commit v7 on v6

--- a/solution.py
+++ b/solution.py
@@ -207,35 +207,30 @@
 
 def finish_kernel(starts, *refs):
     second_ref = refs[5 * len(starts)]
-    out_ref, retained, rows_ref, sems = refs[-4:]
+    out_ref, rows_ref, sems = refs[-3:]
     blocks = out_ref.shape[0] // BLOCK
     half = out_ref.shape[1] // BLOCK // 2
     done = 0
+    stores = []
     for j, start in enumerate(starts):
-        near_ref, faded_ref, factor_ref, _, carry_ref = refs[5 * j : 5 * j + 5]
+        near_ref, faded_ref, factor_ref, silu_ref, carry_ref = refs[5 * j : 5 * j + 5]
         for g in range(carry_ref.shape[0]):
             cols = columns(g)
-            here = columns(done + g)
+            here = columns(done)
             far = jnp.dot(faded_ref[:, cols], carry_ref[g], preferred_element_type=F32)
-            extra = jnp.dot(factor_ref[:, cols], second_ref[(start + half) % (2 * half) + g], preferred_element_type=F32)
-            retained[:BLOCK, here] = near_ref[:BLOCK, cols] + far[:BLOCK] + extra
-            retained[BLOCK:, here] = near_ref[BLOCK:, cols] + far[BLOCK:]
-        done += carry_ref.shape[0]
-    done = 0
-    stores = []
-    for j, start in enumerate(starts):
-        silu_ref, count = refs[5 * j + 3], refs[5 * j + 4].shape[0]
-        for g in range(count):
-            here = columns(done + g)
+            sent_as = (start + half) % (2 * half) + g
+            extra = jnp.dot(factor_ref[:, cols], second_ref[sent_as], preferred_element_type=F32)
             for t in range(blocks):
                 rows = slice(t * BLOCK, (t + 1) * BLOCK)
-                parted = retained[rows, here]
+                parted = near_ref[rows, cols] + far[rows]
+                if t == 0:
+                    parted = parted + extra
                 variance = jnp.mean(parted * parted, axis=-1, keepdims=True)
-                mixed_rows = silu_ref[rows, columns(g)] * (parted * lax.rsqrt(variance + EPSILON))
+                mixed_rows = silu_ref[rows, cols] * (parted * lax.rsqrt(variance + EPSILON))
                 rows_ref[rows, here] = mixed_rows.astype(BF16)
             target = out_ref.at[:, span(real_head(start, half) + g, 1)]
-            stores.append(fetch(rows_ref.at[:, here], target, sems.at[done + g]))
-        done += count
+            stores.append(fetch(rows_ref.at[:, here], target, sems.at[done]))
+            done += 1
     for copy in stores:
         copy.wait()
 
@@ -252,7 +247,6 @@
         out_specs=ANY,
         out_shape=jax.ShapeDtypeStruct((length, features), BF16),
         scratch_shapes=[
-            pltpu.VMEM((length, width), F32),
             pltpu.VMEM((length, width), BF16),
             pltpu.SemaphoreType.DMA((width // BLOCK,)),
         ],

time: 33.2 us -> 33.2 us (level)
  no operation moved by 1% of the time
where the time goes in v7:
time: 33.2 us; the launch traced here: 33 us
  Pallas kernels  12.6 us (38%)
  waiting for transfers between devices  10.4 us (31%)
  starting transfers between devices  8.67 us (26%)
  other arithmetic  0.91 us (3%)
    ppermute x6, waiting for transfers between devices, per_device(): hop = lambda x, i: lax.ppermute(x, 'ctx', [(i, i + 1)])  8.78 us
    ppermute x6, starting transfers between devices, per_device(): hop = lambda x, i: lax.ppermute(x, 'ctx', [(i, i + 1)])  5.27 us
    pallas_call x4, Pallas kernels, local_part(): pl.pallas_call(functools.partial(local_kernel, start), in_specs=[HERE] *...  5.1 us
    pallas_call x3, Pallas kernels, finish(): pl.pallas_call(functools.partial(finish_kernel, starts), in_specs=[HERE]...  4.08 us
    pallas_call x1, Pallas kernels, block_states(): pl.pallas_call(states_kernel, in_specs=[ANY] * 4, out_specs=[HERE] * 7, o...  3.4 us
    ppermute x2, starting transfers between devices, per_device(): onward = lambda x, pairs: lax.ppermute(x, ('ctx', 'rep'), pairs)  1.98 us
    ppermute x3, waiting for transfers between devices, per_device(): swap = lambda x: lax.ppermute(x, 'rep', [(0, 1), (1, 0)])  1.63 us
    ppermute x3, starting transfers between devices, per_device(): swap = lambda x: lax.ppermute(x, 'rep', [(0, 1), (1, 0)])  1.42 us
  transfers between devices with their start and end apart: 11, of which 4 were waited for; matrix products, arithmetic and copies ran while one was open for 2% of the time, Pallas kernels for 24%

profile of v7, /device:TPU:25, one launch (start us, length us, event | category | flops | bytes accessed | tf_op | source)
XLA Modules:
  0.0 33.0 jit_solution(10356036016198510764)
XLA Ops:
  0.0 3.4 %block_states.1 = (bf16[10,128,128]{2,1,0:T(8,128)(2,1)S(1)}, bf16[10,128,128]{2,1,0:T(8,128)(2,1)S(1)}, bf16[20,128,128]{2,1,0:T(8,128)(2,1)S(1)}, bf16[384,256...) custom-call(f32[20]{0:T(128)} %rate_in.1, ...), custom_call_target="tpu_custom_call" | custom-call | tf_op jit(solution)/shard_map/block_states/pallas_call | solution.py:127
  3.4 0.7 %collective-permute-start = (bf16[10,128,128]{2,1,0:T(8,128)(2,1)S(1)}, bf16[10,128,128]{2,1,0:T(8,128)(2,1)S(1)}, u32[]{:S(2)}, u32[]{:S(2)}) collective-permute-start(bf16[10,128,128]{2,1,0:T(8,128)(2,1)S(1)} %get-tuple-element.44), channel_id=1, source_target_pairs={{0,1},{1,0},{2,3},{3,2},{4,5},{5,4},{6,7},{7,6},{8,9},{9,8},{10,11... | collective-permute-start | bytes 983048 | tf_op jit(solution)/shard_map/ppermute | solution.py:282
  4.2 0.7 %collective-permute-start.3 = (bf16[20,128,128]{2,1,0:T(8,128)(2,1)S(1)}, bf16[20,128,128]{2,1,0:T(8,128)(2,1)S(1)}, u32[]{:S(2)}, u32[]{:S(2)}) collective-permute-start(bf16[20,128,128]{2,1,0:T(8,128)(2,1)S(1)} %get-tuple-element.67), channel_id=1, source_target_pairs={{5,8},{7,10},{21,24},{23,26}} | collective-permute-start | bytes 1966088 | tf_op jit(solution)/shard_map/ppermute | solution.py:284
  4.9 0.5 %collective-permute-done = bf16[10,128,128]{2,1,0:T(8,128)(2,1)S(1)} collective-permute-done((bf16[10,128,128]{2,1,0:T(8,128)(2,1)S(1)}, bf16[10,128,128]{2,1,0:T(8,128)(2,1)S(1)}, u32[]{:S(2)}, u32[]{:S(2)}) %collective-permute-start) | collective-permute-done | bytes 327712 | tf_op jit(solution)/shard_map/ppermute | solution.py:282
  5.4 0.1 add_convert_fusion
  5.6 0.7 %collective-permute-start.1 = (bf16[5,128,128]{2,1,0:T(8,128)(2,1)S(1)}, bf16[5,128,128]{2,1,0:T(8,128)(2,1)S(1)}, u32[]{:S(2)}, u32[]{:S(2)}) collective-permute-start(bf16[5,128,128]{2,1,0:T(8,128)(2,1)S(1)} %get-tuple-element.84), channel_id=1, source_target_pairs={{0,4},{1,5},{2,6},{3,7},{16,20},{17,21},{18,22},{19,23}} | collective-permute-start | bytes 491528 | tf_op jit(solution)/shard_map/ppermute | solution.py:285
  6.3 0.7 %collective-permute-start.4 = (bf16[5,128,128]{2,1,0:T(8,128)(2,1)S(1)}, bf16[5,128,128]{2,1,0:T(8,128)(2,1)S(1)}, u32[]{:S(2)}, u32[]{:S(2)}) collective-permute-start(bf16[5,128,128]{2,1,0:T(8,128)(2,1)S(1)} %get-tuple-element.83), channel_id=1, source_target_pairs={{0,4},{1,5},{2,6},{3,7},{16,20},{17,21},{18,22},{19,23}} | collective-permute-start | bytes 491528 | tf_op jit(solution)/shard_map/ppermute | solution.py:285
  7.0 1.3 %collective-permute-start.8 = (bf16[20,128,128]{2,1,0:T(8,128)(2,1)S(1)}, bf16[20,128,128]{2,1,0:T(8,128)(2,1)S(1)}, u32[]{:S(2)}, u32[]{:S(2)}) collective-permute-start(bf16[20,128,128]{2,1,0:T(8,128)(2,1)S(1)} %get-tuple-element.67), channel_id=1, source_target_pairs={{0,1},{1,4},{4,5},{8,9},{9,12},{12,13},{2,3},{3,6},{6,7},{10,11},{... | collective-permute-start | bytes 1966088 | tf_op jit(solution)/shard_map/ppermute | solution.py:284
  8.3 1.3 %local_0.1 = (f32[384,640]{1,0:T(8,128)S(1)}, bf16[384,640]{1,0:T(8,128)(2,1)S(1)}, bf16[128,640]{1,0:T(8,128)(2,1)S(1)}, f32[384,640]{1,0:T(8,128)S(1)}) custom-call(f32[20,128]{1,0:T(8,128)S(1)} %bitcast.27, bf16[384,2560]{1,0:T(8,128)(2,1)S(1)} %copy-done, bf16[384,2560]{1,0:T(8,128)(2,1)S(1)} %copy-done.1, ...), custom_call_target="tpu_custom_call" | custom-call | flops 1 | bytes 1 | tf_op jit(solution)/shard_map/local_0/pallas_call | solution.py:194
  9.6 0.1 fusion
  9.7 0.7 %collective-permute-start.2 = (bf16[5,128,128]{2,1,0:T(8,128)(2,1)S(1)}, bf16[5,128,128]{2,1,0:T(8,128)(2,1)S(1)}, u32[]{:S(2)}, u32[]{:S(2)}) collective-permute-start(bf16[5,128,128]{2,1,0:T(8,128)(2,1)S(1)} %fusion), channel_id=1, source_target_pairs={{4,8},{5,9},{6,10},{7,11},{20,24},{21,25},{22,26},{23,27}} | collective-permute-start | bytes 491528 | tf_op jit(solution)/shard_map/ppermute | solution.py:285
  10.3 1.3 %local_10.1 = (f32[384,640]{1,0:T(8,128)S(1)}, bf16[384,640]{1,0:T(8,128)(2,1)S(1)}, bf16[128,640]{1,0:T(8,128)(2,1)S(1)}, f32[384,640]{1,0:T(8,128)S(1)}) custom-call(f32[20,128]{1,0:T(8,128)S(1)} %bitcast.28, bf16[384,2560]{1,0:T(8,128)(2,1)S(1)} %copy-done, bf16[384,2560]{1,0:T(8,128)(2,1)S(1)} %copy-done.1, ...), custom_call_target="tpu_custom_call" | custom-call | flops 1 | bytes 1 | tf_op jit(solution)/shard_map/local_10/pallas_call | solution.py:194
  11.6 0.1 fusion.2
  11.7 0.7 %collective-permute-start.5 = (bf16[5,128,128]{2,1,0:T(8,128)(2,1)S(1)}, bf16[5,128,128]{2,1,0:T(8,128)(2,1)S(1)}, u32[]{:S(2)}, u32[]{:S(2)}) collective-permute-start(bf16[5,128,128]{2,1,0:T(8,128)(2,1)S(1)} %fusion.2), channel_id=1, source_target_pairs={{4,8},{5,9},{6,10},{7,11},{20,24},{21,25},{22,26},{23,27}} | collective-permute-start | bytes 491528 | tf_op jit(solution)/shard_map/ppermute | solution.py:285
  12.4 1.3 %local_5.1 = (f32[384,640]{1,0:T(8,128)S(1)}, bf16[384,640]{1,0:T(8,128)(2,1)S(1)}, bf16[128,640]{1,0:T(8,128)(2,1)S(1)}, f32[384,640]{1,0:T(8,128)S(1)}) custom-call(f32[20,128]{1,0:T(8,128)S(1)} %bitcast.29, bf16[384,2560]{1,0:T(8,128)(2,1)S(1)} %copy-done, bf16[384,2560]{1,0:T(8,128)(2,1)S(1)} %copy-done.1, ...), custom_call_target="tpu_custom_call" | custom-call | flops 1 | bytes 1 | tf_op jit(solution)/shard_map/local_5/pallas_call | solution.py:194
  13.6 0.0 collective-permute-done.2
  13.7 0.1 fusion.1
  13.7 1.3 %collective-permute-start.7 = (bf16[5,128,128]{2,1,0:T(8,128)(2,1)S(1)}, bf16[5,128,128]{2,1,0:T(8,128)(2,1)S(1)}, u32[]{:S(2)}, u32[]{:S(2)}) collective-permute-start(bf16[5,128,128]{2,1,0:T(8,128)(2,1)S(1)} %fusion.1), channel_id=1, source_target_pairs={{8,12},{9,13},{10,14},{11,15},{24,28},{25,29},{26,30},{27,31}} | collective-permute-start | bytes 491528 | tf_op jit(solution)/shard_map/ppermute | solution.py:285
  15.0 1.3 %local_15.1 = (f32[384,640]{1,0:T(8,128)S(1)}, bf16[384,640]{1,0:T(8,128)(2,1)S(1)}, bf16[128,640]{1,0:T(8,128)(2,1)S(1)}, f32[384,640]{1,0:T(8,128)S(1)}) custom-call(f32[20,128]{1,0:T(8,128)S(1)} %bitcast.30, bf16[384,2560]{1,0:T(8,128)(2,1)S(1)} %copy-done, bf16[384,2560]{1,0:T(8,128)(2,1)S(1)} %copy-done.1, ...), custom_call_target="tpu_custom_call" | custom-call | flops 1 | bytes 1 | tf_op jit(solution)/shard_map/local_15/pallas_call | solution.py:194
  16.3 0.1 fusion.3
  16.4 1.3 %collective-permute-start.6 = (bf16[5,128,128]{2,1,0:T(8,128)(2,1)S(1)}, bf16[5,128,128]{2,1,0:T(8,128)(2,1)S(1)}, u32[]{:S(2)}, u32[]{:S(2)}) collective-permute-start(bf16[5,128,128]{2,1,0:T(8,128)(2,1)S(1)} %fusion.3), channel_id=1, source_target_pairs={{8,12},{9,13},{10,14},{11,15},{24,28},{25,29},{26,30},{27,31}} | collective-permute-start | bytes 491528 | tf_op jit(solution)/shard_map/ppermute | solution.py:285
  17.7 7.6 %collective-permute-done.7 = bf16[5,128,128]{2,1,0:T(8,128)(2,1)S(1)} collective-permute-done((bf16[5,128,128]{2,1,0:T(8,128)(2,1)S(1)}, bf16[5,128,128]{2,1,0:T(8,128)(2,1)S(1)}, u32[]{:S(2)}, u32[]{:S(2)}) %collective-permute-start.7) | collective-permute-done | bytes 163872 | tf_op jit(solution)/shard_map/ppermute | solution.py:285
  25.3 0.2 fusion.7
  25.5 0.1 collective-permute-start.9
  25.6 0.2 add.52.refs_10_.refs_5_
  25.8 1.2 %collective-permute-done.9.refs_9_ = bf16[5,128,128]{2,1,0:T(8,128)(2,1)S(1)} collective-permute-done((bf16[5,128,128]{2,1,0:T(8,128)(2,1)S(1)}, bf16[5,128,128]{2,1,0:T(8,128)(2,1)S(1)}, u32[]{:S(2)}, u32[]{:S(2)}) %collective-permute-start.9) | collective-permute-done | bytes 163872 | tf_op jit(solution)/shard_map/ppermute | solution.py:282
  26.9 1.6 %finish_0.1.refs_6_ = bf16[384,2560]{1,0:T(8,128)(2,1)} custom-call(f32[384,640]{1,0:T(8,128)S(1)} %get-tuple-element.49.refs_0_, bf16[384,640]{1,0:T(8,128)(2,1)S(1)} %get-tuple-element.64.refs_1_, bf16[128,640]{1,0:T(8,128)(2,1)S(1)} %get-tuple-element.65.refs_2_, f32[384,640]{1,0:T(8,128)S(1)} %get-tuple-element.66.refs_3_, ...), custom_call_target="tpu_custom_call" | custom-call | tf_op jit(solution)/shard_map/finish_0/pallas_call | solution.py:244
  28.6 1.2 %collective-permute-done.6 = bf16[5,128,128]{2,1,0:T(8,128)(2,1)S(1)} collective-permute-done((bf16[5,128,128]{2,1,0:T(8,128)(2,1)S(1)}, bf16[5,128,128]{2,1,0:T(8,128)(2,1)S(1)}, u32[]{:S(2)}, u32[]{:S(2)}) %collective-permute-start.6) | collective-permute-done | bytes 163872 | tf_op jit(solution)/shard_map/ppermute | solution.py:285
  29.7 0.2 fusion.11
  29.9 0.6 %collective-permute-start.10 = (bf16[5,128,128]{2,1,0:T(8,128)(2,1)S(1)}, bf16[5,128,128]{2,1,0:T(8,128)(2,1)S(1)}, u32[]{:S(2)}, u32[]{:S(2)}) collective-permute-start(bf16[5,128,128]{2,1,0:T(8,128)(2,1)S(1)} %get-tuple-element.80), channel_id=1, source_target_pairs={{0,1},{1,0},{2,3},{3,2},{4,5},{5,4},{6,7},{7,6},{8,9},{9,8},{10,11... | collective-permute-start | bytes 491528 | tf_op jit(solution)/shard_map/ppermute | solution.py:282
  30.5 1.2 %finish_5.1.refs_6_ = bf16[384,2560]{1,0:T(8,128)(2,1)} custom-call(f32[384,640]{1,0:T(8,128)S(1)} %get-tuple-element.56.refs_0_, bf16[384,640]{1,0:T(8,128)(2,1)S(1)} %get-tuple-element.75.refs_1_, bf16[128,640]{1,0:T(8,128)(2,1)S(1)} %get-tuple-element.76.refs_2_, f32[384,640]{1,0:T(8,128)S(1)} %get-tuple-element.77.refs_3_, ...), custom_call_target="tpu_custom_call", output_to_operand_aliasing={{}: (6, {})} | custom-call | tf_op jit(solution)/shard_map/finish_5/pallas_call | solution.py:244
  31.8 1.2 %finish_15.1 = bf16[384,2560]{1,0:T(8,128)(2,1)} custom-call(f32[384,640]{1,0:T(8,128)S(1)} %get-tuple-element.59.refs_0_, bf16[384,640]{1,0:T(8,128)(2,1)S(1)} %get-tuple-element.60.refs_1_, bf16[128,640]{1,0:T(8,128)(2,1)S(1)} %get-tuple-element.61.refs_2_, f32[384,640]{1,0:T(8,128)S(1)} %get-tuple-element.62.refs_3_, ...), custom_call_target="tpu_custom_call", output_to_operand_aliasing={{}: (6, {})} | custom-call | tf_op jit(solution)/shard_map/finish_15/pallas_call | solution.py:244
  (22 shorter events, 0.1 us)
Async XLA Ops:
  0.0 8.3 %copy-start = (bf16[384,2560]{1,0:T(8,128)(2,1)S(1)}, bf16[384,2560]{1,0:T(8,128)(2,1)}, u32[]{:S(2)}) copy-start(bf16[384,2560]{1,0:T(8,128)(2,1)} %q_ref.3) | copy-start | bytes 5898244
  0.0 8.3 %copy-start.2 = (f32[2560]{0:T(1024)S(1)}, f32[2560]{0:T(1024)}, u32[]{:S(2)}) copy-start(f32[2560]{0:T(1024)} %param.11) | copy-start | bytes 30724
  0.0 8.3 %copy-start.1 = (bf16[384,2560]{1,0:T(8,128)(2,1)S(1)}, bf16[384,2560]{1,0:T(8,128)(2,1)}, u32[]{:S(2)}) copy-start(bf16[384,2560]{1,0:T(8,128)(2,1)} %g_ref.7) | copy-start | bytes 5898244
  3.4 2.0 %collective-permute-start = (bf16[10,128,128]{2,1,0:T(8,128)(2,1)S(1)}, bf16[10,128,128]{2,1,0:T(8,128)(2,1)S(1)}, u32[]{:S(2)}, u32[]{:S(2)}) collective-permute-start(bf16[10,128,128]{2,1,0:T(8,128)(2,1)S(1)} %get-tuple-element.44), channel_id=1, source_target_pairs={{0,1},{1,0},{2,3},{3,2},{4,5},{5,4},{6,7},{7,6},{8,9},{9,8},{10,11... | collective-permute-start | bytes 983048 | tf_op jit(solution)/shard_map/ppermute | solution.py:282
  4.2 9.5 %collective-permute-start.3 = (bf16[20,128,128]{2,1,0:T(8,128)(2,1)S(1)}, bf16[20,128,128]{2,1,0:T(8,128)(2,1)S(1)}, u32[]{:S(2)}, u32[]{:S(2)}) collective-permute-start(bf16[20,128,128]{2,1,0:T(8,128)(2,1)S(1)} %get-tuple-element.67), channel_id=1, source_target_pairs={{5,8},{7,10},{21,24},{23,26}} | collective-permute-start | bytes 1966088 | tf_op jit(solution)/shard_map/ppermute | solution.py:284
  5.6 4.0 %collective-permute-start.1 = (bf16[5,128,128]{2,1,0:T(8,128)(2,1)S(1)}, bf16[5,128,128]{2,1,0:T(8,128)(2,1)S(1)}, u32[]{:S(2)}, u32[]{:S(2)}) collective-permute-start(bf16[5,128,128]{2,1,0:T(8,128)(2,1)S(1)} %get-tuple-element.84), channel_id=1, source_target_pairs={{0,4},{1,5},{2,6},{3,7},{16,20},{17,21},{18,22},{19,23}} | collective-permute-start | bytes 491528 | tf_op jit(solution)/shard_map/ppermute | solution.py:285
  6.3 5.3 %collective-permute-start.4 = (bf16[5,128,128]{2,1,0:T(8,128)(2,1)S(1)}, bf16[5,128,128]{2,1,0:T(8,128)(2,1)S(1)}, u32[]{:S(2)}, u32[]{:S(2)}) collective-permute-start(bf16[5,128,128]{2,1,0:T(8,128)(2,1)S(1)} %get-tuple-element.83), channel_id=1, source_target_pairs={{0,4},{1,5},{2,6},{3,7},{16,20},{17,21},{18,22},{19,23}} | collective-permute-start | bytes 491528 | tf_op jit(solution)/shard_map/ppermute | solution.py:285
  7.0 18.3 %collective-permute-start.8 = (bf16[20,128,128]{2,1,0:T(8,128)(2,1)S(1)}, bf16[20,128,128]{2,1,0:T(8,128)(2,1)S(1)}, u32[]{:S(2)}, u32[]{:S(2)}) collective-permute-start(bf16[20,128,128]{2,1,0:T(8,128)(2,1)S(1)} %get-tuple-element.67), channel_id=1, source_target_pairs={{0,1},{1,4},{4,5},{8,9},{9,12},{12,13},{2,3},{3,6},{6,7},{10,11},{... | collective-permute-start | bytes 1966088 | tf_op jit(solution)/shard_map/ppermute | solution.py:284
  9.7 4.0 %collective-permute-start.2 = (bf16[5,128,128]{2,1,0:T(8,128)(2,1)S(1)}, bf16[5,128,128]{2,1,0:T(8,128)(2,1)S(1)}, u32[]{:S(2)}, u32[]{:S(2)}) collective-permute-start(bf16[5,128,128]{2,1,0:T(8,128)(2,1)S(1)} %fusion), channel_id=1, source_target_pairs={{4,8},{5,9},{6,10},{7,11},{20,24},{21,25},{22,26},{23,27}} | collective-permute-start | bytes 491528 | tf_op jit(solution)/shard_map/ppermute | solution.py:285
  11.7 4.6 %collective-permute-start.5 = (bf16[5,128,128]{2,1,0:T(8,128)(2,1)S(1)}, bf16[5,128,128]{2,1,0:T(8,128)(2,1)S(1)}, u32[]{:S(2)}, u32[]{:S(2)}) collective-permute-start(bf16[5,128,128]{2,1,0:T(8,128)(2,1)S(1)} %fusion.2), channel_id=1, source_target_pairs={{4,8},{5,9},{6,10},{7,11},{20,24},{21,25},{22,26},{23,27}} | collective-permute-start | bytes 491528 | tf_op jit(solution)/shard_map/ppermute | solution.py:285
  13.7 11.6 %collective-permute-start.7 = (bf16[5,128,128]{2,1,0:T(8,128)(2,1)S(1)}, bf16[5,128,128]{2,1,0:T(8,128)(2,1)S(1)}, u32[]{:S(2)}, u32[]{:S(2)}) collective-permute-start(bf16[5,128,128]{2,1,0:T(8,128)(2,1)S(1)} %fusion.1), channel_id=1, source_target_pairs={{8,12},{9,13},{10,14},{11,15},{24,28},{25,29},{26,30},{27,31}} | collective-permute-start | bytes 491528 | tf_op jit(solution)/shard_map/ppermute | solution.py:285
  16.4 13.3 %collective-permute-start.6 = (bf16[5,128,128]{2,1,0:T(8,128)(2,1)S(1)}, bf16[5,128,128]{2,1,0:T(8,128)(2,1)S(1)}, u32[]{:S(2)}, u32[]{:S(2)}) collective-permute-start(bf16[5,128,128]{2,1,0:T(8,128)(2,1)S(1)} %fusion.3), channel_id=1, source_target_pairs={{8,12},{9,13},{10,14},{11,15},{24,28},{25,29},{26,30},{27,31}} | collective-permute-start | bytes 491528 | tf_op jit(solution)/shard_map/ppermute | solution.py:285
  25.5 1.5 %collective-permute-start.9 = (bf16[5,128,128]{2,1,0:T(8,128)(2,1)S(1)}, bf16[5,128,128]{2,1,0:T(8,128)(2,1)S(1)}, u32[]{:S(2)}, u32[]{:S(2)}) collective-permute-start(bf16[5,128,128]{2,1,0:T(8,128)(2,1)S(1)} %get-tuple-element.81), channel_id=1, source_target_pairs={{0,1},{1,0},{2,3},{3,2},{4,5},{5,4},{6,7},{7,6},{8,9},{9,8},{10,11... | collective-permute-start | bytes 491528 | tf_op jit(solution)/shard_map/ppermute | solution.py:282
  29.9 1.8 %collective-permute-start.10 = (bf16[5,128,128]{2,1,0:T(8,128)(2,1)S(1)}, bf16[5,128,128]{2,1,0:T(8,128)(2,1)S(1)}, u32[]{:S(2)}, u32[]{:S(2)}) collective-permute-start(bf16[5,128,128]{2,1,0:T(8,128)(2,1)S(1)} %get-tuple-element.80), channel_id=1, source_target_pairs={{0,1},{1,0},{2,3},{3,2},{4,5},{5,4},{6,7},{7,6},{8,9},{9,8},{10,11... | collective-permute-start | bytes 491528 | tf_op jit(solution)/shard_map/ppermute | solution.py:282
